TPU v7x, 512 devices: a whole 4x8x8 slice. The times are simulated.
512 devices in a mesh: gx: 4 (over x), gy: 8 (over y_lo, core), gz: 16 (over y_hi, z).
Axes of the slice: x: 4, y: 8 (y_hi: 2, y_lo: 4; y = y_hi * 4 + y_lo), z: 8, core: 2. Of those that a mesh axis runs over, the one named last changes fastest.
Arguments:
- positions: float32 [3, 16, 8, 64, 64], P(None, 'gz', 'gx', 'gy'), may hold values from 0 to 1
- counts: int32 [16, 8, 64], P('gz', 'gx', 'gy'), may hold values from 16 to 64, as said below
Outputs:
- force: float32 [3, 16, 8, 64, 64], P(None, 'gz', 'gx', 'gy')
- energy: float32 [16, 8, 64, 64], P('gz', 'gx', 'gy')
Inputs may be any that keep to these rules, and one draw needn't show every extreme that they name: `counts`: every draw has some full cells.
All inputs are finite; a program needn't handle non-finite values.
Results may differ from a plain program's by a relative error of at most 0.0003.
Values sent between devices are 32-bit elements; how exact they have to be, the bound alone decides.
No kernel may reach another device: no remote copies, remote signals or barrier semaphores. Data moves between devices by JAX's collectives and lax.ppermute only.
A program may use at most 64 MiB of HBM per device.

v0:
```python
import jax
import jax.numpy as jnp
from jax import lax
from jax.sharding import PartitionSpec as P

SLOTS = 64


cutoff_sq = 4.95 * 4.95
cell_sides = (12.0, 12.0, 2.5)
density_width = 8.0
pair_width = 3.0
density_amp = 1.0
pair_amp = 2.0


def padded(x, sides, width):
    for axis, dim in sides:
        devices, length = (lax.axis_size(axis), x.shape[dim])
        up = [(i, (i + 1) % devices) for i in range(devices)]
        down = [(j, i) for i, j in up]
        last = lax.slice_in_dim(x, length - width, length, axis=dim)
        initial = lax.slice_in_dim(x, 0, width, axis=dim)
        before = lax.ppermute(last, axis, up)
        after = lax.ppermute(initial, axis, down)
        x = jnp.concatenate([before, x, after], axis=dim)
    return x


def passed_along(block, axis, distance):
    devices = range(lax.axis_size(axis))
    route = [((i - distance) % len(devices), i) for i in devices]
    return lax.ppermute(block, axis, route)


def kernels(squared):
    inside = jnp.where(squared < cutoff_sq, 1.0 - squared / cutoff_sq, 0.0)
    smooth = inside * inside
    smooth_slope = -2.0 * inside / cutoff_sq
    first = jnp.exp(-squared / density_width)
    second = jnp.exp(-squared / pair_width)
    return (
        density_amp * first * smooth,
        density_amp * first * (smooth_slope - smooth / density_width),
        pair_amp * second * smooth,
        pair_amp * second * (smooth_slope - smooth / pair_width),
    )


def neighbours(extended, centre_z, start_x, start_y, rows_x, rows_y, step_z, step_x):
    pieces = []
    for step_y in (-1, 0, 1):
        pieces.append(
            extended[
                :,
                centre_z + step_z,
                start_x + step_x : start_x + step_x + rows_x,
                start_y + step_y : start_y + step_y + rows_y,
            ]
        )
    return jnp.concatenate(pieces, axis=-1)


def pair_geometry(center, partner, step_z, step_x, slots):
    lateral = (jnp.arange(3 * slots) // slots - 1).astype(jnp.float32)
    moves = (float(step_x), lateral, float(step_z))
    squared = jnp.zeros((), jnp.float32)
    deltas = []
    for component in range(3):
        delta = (
            center[component][..., :, None] - partner[component][..., None, :] - moves[component]
        ) * cell_sides[component]
        deltas.append(delta)
        squared = squared + delta * delta
    weight = center[3][..., :, None] * partner[3][..., None, :]
    if step_z == 0 and step_x == 0:
        column = jnp.arange(3 * slots)[None, :]
        row_index = jnp.arange(slots)[:, None]
        weight = weight * (column != row_index + slots).astype(jnp.float32)
    return (deltas, squared, weight)


def densities(extended, centre_z, start_x, start_y, rows_x, rows_y, slots):
    center = extended[:, centre_z, start_x : start_x + rows_x, start_y : start_y + rows_y]
    summed = jnp.zeros(center.shape[1:], jnp.float32)
    for step_z in range(-2, 3):
        for step_x in range(-1, 2):
            partner = neighbours(
                extended, centre_z, start_x, start_y, rows_x, rows_y, step_z, step_x
            )
            deltas, squared, weight = pair_geometry(center, partner, step_z, step_x, slots)
            summed = summed + jnp.sum(weight * kernels(squared)[0], axis=-1)
    return summed


def forces(extended, centre_z, rows_x, rows_y, slots):
    center = extended[:, centre_z, 1 : 1 + rows_x, 1 : 1 + rows_y]
    pushes = [jnp.zeros(center.shape[1:], jnp.float32) for component in range(3)]
    pairs = jnp.zeros(center.shape[1:], jnp.float32)
    for step_z in range(-2, 3):
        for step_x in range(-1, 2):
            partner = neighbours(extended, centre_z, 1, 1, rows_x, rows_y, step_z, step_x)
            deltas, squared, weight = pair_geometry(center, partner, step_z, step_x, slots)
            values = kernels(squared)
            factor = weight * (
                (center[4][..., :, None] + partner[4][..., None, :]) * values[1] + values[3]
            )
            pushes = [
                pushes[component] - 2.0 * jnp.sum(factor * deltas[component], axis=-1)
                for component in range(3)
            ]
            pairs = pairs + jnp.sum(weight * values[2], axis=-1)
    return (jnp.stack(pushes), pairs)


def layers_of(field, depth, mover):
    below = [field]
    above = [field]
    for level in range(depth):
        below.append(mover(below[-1], 1))
        above.append(mover(above[-1], -1))
    ordered = below[:0:-1] + [field] + above[1:]
    return jnp.concatenate(ordered, axis=1)


def body(positions, counts):
    rows_x = positions.shape[2]
    rows_y = positions.shape[3]
    occupied = (jnp.arange(SLOTS)[None, None, None, :] < counts[..., None]).astype(jnp.float32)
    stacked = jnp.concatenate([positions, occupied[None]], axis=0)
    plane = padded(stacked, (("gx", 2), ("gy", 3)), 1)
    extended = layers_of(plane, 2, lambda values, distance: passed_along(values, "gz", distance))
    density = densities(extended, 2, 1, 1, rows_x, rows_y, SLOTS)
    own_root = jnp.sqrt(1.0 + density)
    slope = -0.5 / own_root
    slope_plane = padded(slope[None, None], (("gx", 2), ("gy", 3)), 1)
    slope_full = layers_of(
        slope_plane, 2, lambda values, distance: passed_along(values, "gz", distance)
    )
    full = jnp.concatenate([extended, slope_full], axis=0)
    pushes, pairs = forces(full, 2, rows_x, rows_y, SLOTS)
    force = pushes[:, None]
    energy = occupied * (-own_root[None] + 0.5 * pairs[None])
    return (force, energy)


def solution(mesh):
    return jax.shard_map(
        body,
        mesh=mesh,
        in_specs=(P(None, "gz", "gx", "gy", None), P("gz", "gx", "gy")),
        out_specs=(P(None, "gz", "gx", "gy", None), P("gz", "gx", "gy", None)),
        check_vma=False,
    )
```

profile of v0, /device:TPU:2, one launch (start us, length us, event | category | flops | bytes accessed | tf_op | source)
XLA Modules:
  0.0 169.6 jit_solution(7802113427435182823)
XLA Ops:
  0.6 0.7 copy-done.1
  1.4 0.7 fusion.111
  2.1 7.8 %collective-permute-start.1 = (f32[4,1,1,8,64]{4,3,2,0,1:T(8,128)S(1)}, f32[4,1,1,8,64]{4,3,2,0,1:T(8,128)S(1)}, u32[]{:S(2)}, u32[]{:S(2)}) collective-permute-start(f32[4,1,1,8,64]{4,3,2,0,1:T(8,128)S(1)} %get-tuple-element.337), channel_id=1, source_target_pairs={{128,0},{256,128},{384,256},{0,384},{129,1},{257,129},{385,257},{1... | collective-permute-start | bytes 24584 | tf_op jit(solution)/shard_map/ppermute | solution.py:25
  10.0 1.9 %collective-permute-start = (f32[4,1,1,8,64]{4,3,2,0,1:T(8,128)S(1)}, f32[4,1,1,8,64]{4,3,2,0,1:T(8,128)S(1)}, u32[]{:S(2)}, u32[]{:S(2)}) collective-permute-start(f32[4,1,1,8,64]{4,3,2,0,1:T(8,128)S(1)} %get-tuple-element.336), channel_id=1, source_target_pairs={{0,128},{128,256},{256,384},{384,0},{1,129},{129,257},{257,385},{3... | collective-permute-start | bytes 24584 | tf_op jit(solution)/shard_map/ppermute | solution.py:24
  12.1 3.5 %collective-permute-done = f32[4,1,1,8,64]{4,3,2,0,1:T(8,128)S(1)} collective-permute-done((f32[4,1,1,8,64]{4,3,2,0,1:T(8,128)S(1)}, f32[4,1,1,8,64]{4,3,2,0,1:T(8,128)S(1)}, u32[]{:S(2)}, u32[]{:S(2)}) %collective-permute-start) | collective-permute-done | bytes 8224 | tf_op jit(solution)/shard_map/ppermute | solution.py:24
  15.6 1.9 %collective-permute-start.3 = (f32[4,1,4,1,64]{4,3,2,0,1:T(1,128)S(1)}, f32[4,1,4,1,64]{4,3,2,0,1:T(1,128)S(1)}, u32[]{:S(2)}, u32[]{:S(2)}) collective-permute-start(f32[4,1,4,1,64]{4,3,2,0,1:T(1,128)S(1)} %get-tuple-element.332), channel_id=1, source_target_pairs={{16,0},{32,16},{48,32},{64,48},{80,64},{96,80},{112,96},{0,112},{1... | collective-permute-start | bytes 12296 | tf_op jit(solution)/shard_map/ppermute | solution.py:25
  17.6 2.4 %collective-permute-start.2 = (f32[4,1,4,1,64]{4,3,2,0,1:T(1,128)S(1)}, f32[4,1,4,1,64]{4,3,2,0,1:T(1,128)S(1)}, u32[]{:S(2)}, u32[]{:S(2)}) collective-permute-start(f32[4,1,4,1,64]{4,3,2,0,1:T(1,128)S(1)} %get-tuple-element.331), channel_id=1, source_target_pairs={{0,16},{16,32},{32,48},{48,64},{64,80},{80,96},{96,112},{112,0},{1... | collective-permute-start | bytes 12296 | tf_op jit(solution)/shard_map/ppermute | solution.py:24
  20.0 4.3 %collective-permute-done.2 = f32[4,1,4,1,64]{4,3,2,0,1:T(1,128)S(1)} collective-permute-done((f32[4,1,4,1,64]{4,3,2,0,1:T(1,128)S(1)}, f32[4,1,4,1,64]{4,3,2,0,1:T(1,128)S(1)}, u32[]{:S(2)}, u32[]{:S(2)}) %collective-permute-start.2) | collective-permute-done | bytes 4128 | tf_op jit(solution)/shard_map/ppermute | solution.py:24
  24.4 11.6 %collective-permute-start.6 = (f32[4,1,4,10,64]{4,3,2,0,1:T(8,128)S(1)}, f32[4,1,4,10,64]{4,3,2,0,1:T(8,128)S(1)}, u32[]{:S(2)}, u32[]{:S(2)}) collective-permute-start(f32[4,1,4,10,64]{4,3,2,0,1:T(8,128)S(1)} %pad_maximum_fusion.1), channel_id=1, source_target_pairs={{1,0},{2,1},{3,2},{4,3},{5,4},{6,5},{7,6},{8,7},{9,8},{10,9},{11,1... | collective-permute-start | bytes 122888 | tf_op jit(solution)/shard_map/ppermute | solution.py:33
  35.9 1.9 %collective-permute-start.4 = (f32[4,1,4,10,64]{4,3,2,0,1:T(8,128)S(1)}, f32[4,1,4,10,64]{4,3,2,0,1:T(8,128)S(1)}, u32[]{:S(2)}, u32[]{:S(2)}) collective-permute-start(f32[4,1,4,10,64]{4,3,2,0,1:T(8,128)S(1)} %pad_maximum_fusion.1), channel_id=1, source_target_pairs={{15,0},{0,1},{1,2},{2,3},{3,4},{4,5},{5,6},{6,7},{7,8},{8,9},{9,10... | collective-permute-start | bytes 122888 | tf_op jit(solution)/shard_map/ppermute | solution.py:33
  37.9 0.1 pad_maximum_fusion.26
  38.1 0.1 pad_maximum_fusion.28
  38.2 3.2 %multiply_reduce_fusion.54 = (f32[2,8,64]{2,1,0:T(8,128)S(1)}, f32[2,8,64]{2,1,0:T(8,128)S(1)}, f32[2,8,64]{2,1,0:T(8,128)S(1)}) fusion(f32[2,8,192]{2,1,0:T(8,128)S(1)} %get-tuple-element.304, f32[2,8,192]{2,1,0:T(8,128)S(1)} %get-tuple-element.305, f32[2,8,192]{2,1,0:T(8,128)S(1)} %get-tuple-element.306, f32[2,8,192]{2,1,0:T(8,128)S(1)} %get-tuple-element.303, ...), kind=kLoop, calls=%fused_computation.284 | loop fusion | flops 14152704 | bytes 226048 | tf_op jit(solution)/shard_map/reduce_sum | solution.py:92
  41.4 0.1 pad_maximum_fusion.29
  41.6 7.5 %collective-permute-done.4 = f32[4,1,4,10,64]{4,3,2,0,1:T(8,128)S(1)} collective-permute-done((f32[4,1,4,10,64]{4,3,2,0,1:T(8,128)S(1)}, f32[4,1,4,10,64]{4,3,2,0,1:T(8,128)S(1)}, u32[]{:S(2)}, u32[]{:S(2)}) %collective-permute-start.4) | collective-permute-done | bytes 40992 | tf_op jit(solution)/shard_map/ppermute | solution.py:33
  49.2 0.1 pad_maximum_fusion.23
  49.3 0.1 pad_maximum_fusion.25
  49.4 3.4 %multiply_reduce_fusion.51 = (f32[2,8,64]{2,1,0:T(8,128)S(1)}, f32[2,8,64]{2,1,0:T(8,128)S(1)}, f32[2,8,64]{2,1,0:T(8,128)S(1)}) fusion(f32[2,8,192]{2,1,0:T(8,128)S(1)} %get-tuple-element.316, f32[2,8,192]{2,1,0:T(8,128)S(1)} %get-tuple-element.317, f32[2,8,192]{2,1,0:T(8,128)S(1)} %get-tuple-element.318, f32[2,8,192]{2,1,0:T(8,128)S(1)} %get-tuple-element.315, ...), kind=kLoop, calls=%fused_computation.278 | loop fusion | flops 14545920 | bytes 176896 | tf_op jit(solution)/shard_map/reduce_sum | solution.py:92
  52.8 2.4 %collective-permute-start.7 = (f32[4,1,4,10,64]{4,3,2,0,1:T(8,128)S(1)}, f32[4,1,4,10,64]{4,3,2,0,1:T(8,128)S(1)}, u32[]{:S(2)}, u32[]{:S(2)}) collective-permute-start(f32[4,1,4,10,64]{4,3,2,0,1:T(8,128)S(1)} %collective-permute-done.6), channel_id=1, source_target_pairs={{1,0},{2,1},{3,2},{4,3},{5,4},{6,5},{7,6},{8,7},{9,8},{10,9},{11,1... | collective-permute-start | bytes 122888 | tf_op jit(solution)/shard_map/ppermute | solution.py:33
  55.3 3.4 %collective-permute-start.5 = (f32[4,1,4,10,64]{4,3,2,0,1:T(8,128)S(1)}, f32[4,1,4,10,64]{4,3,2,0,1:T(8,128)S(1)}, u32[]{:S(2)}, u32[]{:S(2)}) collective-permute-start(f32[4,1,4,10,64]{4,3,2,0,1:T(8,128)S(1)} %collective-permute-done.4), channel_id=1, source_target_pairs={{15,0},{0,1},{1,2},{2,3},{3,4},{4,5},{5,6},{6,7},{7,8},{8,9},{9,10... | collective-permute-start | bytes 122888 | tf_op jit(solution)/shard_map/ppermute | solution.py:33
  58.7 1.0 collective-permute-done.7
  59.7 0.1 pad_maximum_fusion.32
  59.9 8.3 %collective-permute-done.5 = f32[4,1,4,10,64]{4,3,2,0,1:T(8,128)S(1)} collective-permute-done((f32[4,1,4,10,64]{4,3,2,0,1:T(8,128)S(1)}, f32[4,1,4,10,64]{4,3,2,0,1:T(8,128)S(1)}, u32[]{:S(2)}, u32[]{:S(2)}) %collective-permute-start.5) | collective-permute-done | bytes 40992 | tf_op jit(solution)/shard_map/ppermute | solution.py:33
  68.3 0.1 pad_maximum_fusion.20
  68.4 0.1 pad_maximum_fusion.22
  68.6 3.4 %multiply_reduce_fusion.48 = (f32[2,8,64]{2,1,0:T(8,128)S(1)}, f32[2,8,64]{2,1,0:T(8,128)S(1)}, f32[2,8,64]{2,1,0:T(8,128)S(1)}) fusion(f32[2,8,192]{2,1,0:T(8,128)S(1)} %get-tuple-element.328, f32[2,8,192]{2,1,0:T(8,128)S(1)} %get-tuple-element.329, f32[2,8,192]{2,1,0:T(8,128)S(1)} %get-tuple-element.330, f32[2,8,192]{2,1,0:T(8,128)S(1)} %get-tuple-element.327, ...), kind=kLoop, calls=%fused_computation.272 | loop fusion | flops 14545920 | bytes 176896 | tf_op jit(solution)/shard_map/reduce_sum | solution.py:92
  71.9 3.4 %multiply_reduce_fusion.60 = (f32[2,8,64]{2,1,0:T(8,128)S(1)}, f32[2,8,64]{2,1,0:T(8,128)S(1)}, f32[2,8,64]{2,1,0:T(8,128)S(1)}) fusion(f32[2,8,192]{2,1,0:T(8,128)S(1)} %get-tuple-element.292, f32[2,8,64]{2,1,0:T(8,128)S(1)} %get-tuple-element.339, f32[192]{0:T(256)S(1)} %fusion.116, f32[2,8,192]{2,1,0:T(8,128)S(1)} %get-tuple-element.293, ...), kind=kLoop, calls=%fused_computation.296 | loop fusion | flops 14545920 | bytes 176896 | tf_op jit(solution)/shard_map/reduce_sum | solution.py:92
  75.3 3.4 %multiply_reduce_fusion.59 = (f32[2,8,64]{2,1,0:T(8,128)S(1)}, f32[2,8,64]{2,1,0:T(8,128)S(1)}, f32[2,8,64]{2,1,0:T(8,128)S(1)}) fusion(f32[2,8,192]{2,1,0:T(8,128)S(1)} %get-tuple-element.280, f32[2,8,192]{2,1,0:T(8,128)S(1)} %get-tuple-element.281, f32[2,8,192]{2,1,0:T(8,128)S(1)} %get-tuple-element.282, f32[2,8,192]{2,1,0:T(8,128)S(1)} %get-tuple-element.279, ...), kind=kLoop, calls=%fused_computation.294 | loop fusion | flops 14545920 | bytes 176896 | tf_op jit(solution)/shard_map/reduce_sum | solution.py:92
  78.8 5.0 %collective-permute-start.9 = (f32[1,1,1,8,64]{4,3,2,1,0:T(8,128)S(1)}, f32[1,1,1,8,64]{4,3,2,1,0:T(8,128)S(1)}, u32[]{:S(2)}, u32[]{:S(2)}) collective-permute-start(f32[1,1,1,8,64]{4,3,2,1,0:T(8,128)S(1)} %get-tuple-element.344), channel_id=1, source_target_pairs={{128,0},{256,128},{384,256},{0,384},{129,1},{257,129},{385,257},{1... | collective-permute-start | bytes 6152 | tf_op jit(solution)/shard_map/ppermute | solution.py:25
  83.8 1.9 %collective-permute-start.8 = (f32[1,1,1,8,64]{4,3,2,1,0:T(8,128)S(1)}, f32[1,1,1,8,64]{4,3,2,1,0:T(8,128)S(1)}, u32[]{:S(2)}, u32[]{:S(2)}) collective-permute-start(f32[1,1,1,8,64]{4,3,2,1,0:T(8,128)S(1)} %get-tuple-element.343), channel_id=1, source_target_pairs={{0,128},{128,256},{256,384},{384,0},{1,129},{129,257},{257,385},{3... | collective-permute-start | bytes 6152 | tf_op jit(solution)/shard_map/ppermute | solution.py:24
  85.8 3.5 %collective-permute-done.8 = f32[1,1,1,8,64]{4,3,2,1,0:T(8,128)S(1)} collective-permute-done((f32[1,1,1,8,64]{4,3,2,1,0:T(8,128)S(1)}, f32[1,1,1,8,64]{4,3,2,1,0:T(8,128)S(1)}, u32[]{:S(2)}, u32[]{:S(2)}) %collective-permute-start.8) | collective-permute-done | bytes 2080 | tf_op jit(solution)/shard_map/ppermute | solution.py:24
  89.3 1.9 %collective-permute-start.11 = (f32[1,1,4,1,64]{4,3,2,1,0:T(1,128)S(1)}, f32[1,1,4,1,64]{4,3,2,1,0:T(1,128)S(1)}, u32[]{:S(2)}, u32[]{:S(2)}) collective-permute-start(f32[1,1,4,1,64]{4,3,2,1,0:T(1,128)S(1)} %get-tuple-element.342), channel_id=1, source_target_pairs={{16,0},{32,16},{48,32},{64,48},{80,64},{96,80},{112,96},{0,112},{1... | collective-permute-start | bytes 3080 | tf_op jit(solution)/shard_map/ppermute | solution.py:25
  91.3 2.4 %collective-permute-start.10 = (f32[1,1,4,1,64]{4,3,2,1,0:T(1,128)S(1)}, f32[1,1,4,1,64]{4,3,2,1,0:T(1,128)S(1)}, u32[]{:S(2)}, u32[]{:S(2)}) collective-permute-start(f32[1,1,4,1,64]{4,3,2,1,0:T(1,128)S(1)} %get-tuple-element.341), channel_id=1, source_target_pairs={{0,16},{16,32},{32,48},{48,64},{64,80},{80,96},{96,112},{112,0},{1... | collective-permute-start | bytes 3080 | tf_op jit(solution)/shard_map/ppermute | solution.py:24
  93.7 4.2 %collective-permute-done.10 = f32[1,1,4,1,64]{4,3,2,1,0:T(1,128)S(1)} collective-permute-done((f32[1,1,4,1,64]{4,3,2,1,0:T(1,128)S(1)}, f32[1,1,4,1,64]{4,3,2,1,0:T(1,128)S(1)}, u32[]{:S(2)}, u32[]{:S(2)}) %collective-permute-start.10) | collective-permute-done | bytes 1056 | tf_op jit(solution)/shard_map/ppermute | solution.py:24
  98.0 1.9 %collective-permute-start.12 = (f32[1,1,4,10,64]{4,3,2,1,0:T(8,128)S(1)}, f32[1,1,4,10,64]{4,3,2,1,0:T(8,128)S(1)}, u32[]{:S(2)}, u32[]{:S(2)}) collective-permute-start(f32[1,1,4,10,64]{4,3,2,1,0:T(8,128)S(1)} %pad_maximum_fusion.36), channel_id=1, source_target_pairs={{15,0},{0,1},{1,2},{2,3},{3,4},{4,5},{5,6},{6,7},{7,8},{8,9},{9,10... | collective-permute-start | bytes 30728 | tf_op jit(solution)/shard_map/ppermute | solution.py:33
  99.9 9.9 %collective-permute-start.14 = (f32[1,1,4,10,64]{4,3,2,1,0:T(8,128)S(1)}, f32[1,1,4,10,64]{4,3,2,1,0:T(8,128)S(1)}, u32[]{:S(2)}, u32[]{:S(2)}) collective-permute-start(f32[1,1,4,10,64]{4,3,2,1,0:T(8,128)S(1)} %pad_maximum_fusion.36), channel_id=1, source_target_pairs={{1,0},{2,1},{3,2},{4,3},{5,4},{6,5},{7,6},{8,7},{9,8},{10,9},{11,1... | collective-permute-start | bytes 30728 | tf_op jit(solution)/shard_map/ppermute | solution.py:33
  109.9 1.9 %collective-permute-start.13 = (f32[1,1,4,10,64]{4,3,2,1,0:T(8,128)S(1)}, f32[1,1,4,10,64]{4,3,2,1,0:T(8,128)S(1)}, u32[]{:S(2)}, u32[]{:S(2)}) collective-permute-start(f32[1,1,4,10,64]{4,3,2,1,0:T(8,128)S(1)} %collective-permute-done.12), channel_id=1, source_target_pairs={{15,0},{0,1},{1,2},{2,3},{3,4},{4,5},{5,6},{6,7},{7,8},{8,9},{9,10... | collective-permute-start | bytes 30728 | tf_op jit(solution)/shard_map/ppermute | solution.py:33
  111.8 9.9 %collective-permute-start.15 = (f32[1,1,4,10,64]{4,3,2,1,0:T(8,128)S(1)}, f32[1,1,4,10,64]{4,3,2,1,0:T(8,128)S(1)}, u32[]{:S(2)}, u32[]{:S(2)}) collective-permute-start(f32[1,1,4,10,64]{4,3,2,1,0:T(8,128)S(1)} %collective-permute-done.14), channel_id=1, source_target_pairs={{1,0},{2,1},{3,2},{4,3},{5,4},{6,5},{7,6},{8,7},{9,8},{10,9},{11,1... | collective-permute-start | bytes 30728 | tf_op jit(solution)/shard_map/ppermute | solution.py:33
  121.9 1.5 collective-permute-done.15
  123.6 0.1 pad_maximum_fusion.18
  123.7 0.1 pad_maximum_fusion.4
  123.8 0.1 pad_maximum_fusion.17
  123.9 0.1 pad_maximum_fusion.5
  124.0 0.1 pad_maximum_fusion.16
  124.1 0.1 pad_maximum_fusion.6
  124.2 0.1 pad_maximum_fusion.15
  124.4 0.1 pad_maximum_fusion.7
  124.5 0.1 pad_maximum_fusion.14
  124.6 0.1 pad_maximum_fusion.8
  124.7 0.1 pad_maximum_fusion.13
  124.8 0.1 pad_maximum_fusion.9
  124.9 0.1 pad_maximum_fusion.12
  125.0 0.1 pad_maximum_fusion.10
  125.1 0.1 pad_maximum_fusion.11
  125.2 2.5 %multiply_reduce_fusion.38 = (f32[2,8,64]{2,1,0:T(8,128)S(1)}, f32[2,8,64]{2,1,0:T(8,128)S(1)}, f32[2,8,64]{2,1,0:T(8,128)S(1)}, f32[2,8,64]{2,1,0:T(8,128)S(1)}) fusion(f32[2,8,192]{2,1,0:T(8,128)S(1)} %get-tuple-element.193, f32[2,8,64]{2,1,0:T(8,128)S(1)} %get-tuple-element.338, f32[2,8,192]{2,1,0:T(8,128)S(1)} %get-tuple-element.191, ...), kind=kLoop, calls=%fused_computation.210 | loop fusion | flops 8450048 | bytes 148224 | tf_op jit(solution)/shard_map/reduce_sum | solution.py:109
  127.8 5.9 %multiply_reduce_fusion.31 = (f32[2,8,64]{2,1,0:T(8,128)S(1)}, f32[2,8,64]{2,1,0:T(8,128)S(1)}, f32[2,8,64]{2,1,0:T(8,128)S(1)}, f32[2,8,64]{2,1,0:T(8,128)S(1)}...) fusion(f32[2,8,192]{2,1,0:T(8,128)S(1)} %get-tuple-element.263, ...), kind=kLoop, calls=%fused_computation.161 | loop fusion | flops 17293312 | bytes 176896 | tf_op jit(solution)/shard_map/reduce_sum | solution.py:109
  133.7 5.6 %multiply_reduce_fusion.32 = (f32[2,8,64]{2,1,0:T(8,128)S(1)}, f32[2,8,64]{2,1,0:T(8,128)S(1)}, f32[2,8,64]{2,1,0:T(8,128)S(1)}, f32[2,8,64]{2,1,0:T(8,128)S(1)}...) fusion(f32[2,8,192]{2,1,0:T(8,128)S(1)} %get-tuple-element.253, ...), kind=kLoop, calls=%fused_computation.168 | loop fusion | flops 16900096 | bytes 176896 | tf_op jit(solution)/shard_map/reduce_sum | solution.py:109
  139.3 5.9 %multiply_reduce_fusion.33 = (f32[2,8,64]{2,1,0:T(8,128)S(1)}, f32[2,8,64]{2,1,0:T(8,128)S(1)}, f32[2,8,64]{2,1,0:T(8,128)S(1)}, f32[2,8,64]{2,1,0:T(8,128)S(1)}...) fusion(f32[2,8,192]{2,1,0:T(8,128)S(1)} %get-tuple-element.243, ...), kind=kLoop, calls=%fused_computation.175 | loop fusion | flops 17293312 | bytes 176896 | tf_op jit(solution)/shard_map/reduce_sum | solution.py:109
  145.2 5.9 %multiply_reduce_fusion.34 = (f32[2,8,64]{2,1,0:T(8,128)S(1)}, f32[2,8,64]{2,1,0:T(8,128)S(1)}, f32[2,8,64]{2,1,0:T(8,128)S(1)}, f32[2,8,64]{2,1,0:T(8,128)S(1)}...) fusion(f32[2,8,192]{2,1,0:T(8,128)S(1)} %get-tuple-element.233, ...), kind=kLoop, calls=%fused_computation.182 | loop fusion | flops 17293312 | bytes 176896 | tf_op jit(solution)/shard_map/reduce_sum | solution.py:109
  151.1 5.7 %multiply_reduce_fusion.35 = (f32[2,8,64]{2,1,0:T(8,128)S(1)}, f32[2,8,64]{2,1,0:T(8,128)S(1)}, f32[2,8,64]{2,1,0:T(8,128)S(1)}, f32[2,8,64]{2,1,0:T(8,128)S(1)}...) fusion(f32[2,8,192]{2,1,0:T(8,128)S(1)} %get-tuple-element.223, ...), kind=kLoop, calls=%fused_computation.189 | loop fusion | flops 16900096 | bytes 176896 | tf_op jit(solution)/shard_map/reduce_sum | solution.py:109
  156.7 5.9 %multiply_reduce_fusion.36 = (f32[2,8,64]{2,1,0:T(8,128)S(1)}, f32[2,8,64]{2,1,0:T(8,128)S(1)}, f32[2,8,64]{2,1,0:T(8,128)S(1)}, f32[2,8,64]{2,1,0:T(8,128)S(1)}...) fusion(f32[2,8,192]{2,1,0:T(8,128)S(1)} %get-tuple-element.213, ...), kind=kLoop, calls=%fused_computation.196 | loop fusion | flops 17293312 | bytes 176896 | tf_op jit(solution)/shard_map/reduce_sum | solution.py:109
  162.6 5.6 %multiply_reduce_fusion.37 = (f32[2,8,64]{2,1,0:T(8,128)S(1)}, f32[2,8,64]{2,1,0:T(8,128)S(1)}, f32[2,8,64]{2,1,0:T(8,128)S(1)}, f32[2,8,64]{2,1,0:T(8,128)S(1)}...) fusion(f32[2,8,192]{2,1,0:T(8,128)S(1)} %get-tuple-element.203, ...), kind=kLoop, calls=%fused_computation.203 | loop fusion | flops 16900096 | bytes 176896 | tf_op jit(solution)/shard_map/reduce_sum | solution.py:109
  168.3 0.6 maximum_bitcast_fusion.4
  168.9 0.7 fusion.112
  (84 shorter events, 1.3 us)
Async XLA Ops:
  0.6 0.7 copy-start.1
  2.1 9.8 %copy-start = (f32[3,1,2,8,64]{4,3,2,1,0:T(8,128)S(1)}, f32[3,1,2,8,64]{4,3,2,1,0:T(8,128)}, u32[]{:S(2)}) copy-start(f32[3,1,2,8,64]{4,3,2,1,0:T(8,128)} %param.2) | copy-start | bytes 36868
  2.1 9.9 %collective-permute-start.1 = (f32[4,1,1,8,64]{4,3,2,0,1:T(8,128)S(1)}, f32[4,1,1,8,64]{4,3,2,0,1:T(8,128)S(1)}, u32[]{:S(2)}, u32[]{:S(2)}) collective-permute-start(f32[4,1,1,8,64]{4,3,2,0,1:T(8,128)S(1)} %get-tuple-element.337), channel_id=1, source_target_pairs={{128,0},{256,128},{384,256},{0,384},{129,1},{257,129},{385,257},{1... | collective-permute-start | bytes 24584 | tf_op jit(solution)/shard_map/ppermute | solution.py:25
  10.0 5.6 %collective-permute-start = (f32[4,1,1,8,64]{4,3,2,0,1:T(8,128)S(1)}, f32[4,1,1,8,64]{4,3,2,0,1:T(8,128)S(1)}, u32[]{:S(2)}, u32[]{:S(2)}) collective-permute-start(f32[4,1,1,8,64]{4,3,2,0,1:T(8,128)S(1)} %get-tuple-element.336), channel_id=1, source_target_pairs={{0,128},{128,256},{256,384},{384,0},{1,129},{129,257},{257,385},{3... | collective-permute-start | bytes 24584 | tf_op jit(solution)/shard_map/ppermute | solution.py:24
  15.6 4.4 %collective-permute-start.3 = (f32[4,1,4,1,64]{4,3,2,0,1:T(1,128)S(1)}, f32[4,1,4,1,64]{4,3,2,0,1:T(1,128)S(1)}, u32[]{:S(2)}, u32[]{:S(2)}) collective-permute-start(f32[4,1,4,1,64]{4,3,2,0,1:T(1,128)S(1)} %get-tuple-element.332), channel_id=1, source_target_pairs={{16,0},{32,16},{48,32},{64,48},{80,64},{96,80},{112,96},{0,112},{1... | collective-permute-start | bytes 12296 | tf_op jit(solution)/shard_map/ppermute | solution.py:25
  17.6 6.8 %collective-permute-start.2 = (f32[4,1,4,1,64]{4,3,2,0,1:T(1,128)S(1)}, f32[4,1,4,1,64]{4,3,2,0,1:T(1,128)S(1)}, u32[]{:S(2)}, u32[]{:S(2)}) collective-permute-start(f32[4,1,4,1,64]{4,3,2,0,1:T(1,128)S(1)} %get-tuple-element.331), channel_id=1, source_target_pairs={{0,16},{16,32},{32,48},{48,64},{64,80},{80,96},{96,112},{112,0},{1... | collective-permute-start | bytes 12296 | tf_op jit(solution)/shard_map/ppermute | solution.py:24
  24.4 17.0 %collective-permute-start.6 = (f32[4,1,4,10,64]{4,3,2,0,1:T(8,128)S(1)}, f32[4,1,4,10,64]{4,3,2,0,1:T(8,128)S(1)}, u32[]{:S(2)}, u32[]{:S(2)}) collective-permute-start(f32[4,1,4,10,64]{4,3,2,0,1:T(8,128)S(1)} %pad_maximum_fusion.1), channel_id=1, source_target_pairs={{1,0},{2,1},{3,2},{4,3},{5,4},{6,5},{7,6},{8,7},{9,8},{10,9},{11,1... | collective-permute-start | bytes 122888 | tf_op jit(solution)/shard_map/ppermute | solution.py:33
  35.9 13.2 %collective-permute-start.4 = (f32[4,1,4,10,64]{4,3,2,0,1:T(8,128)S(1)}, f32[4,1,4,10,64]{4,3,2,0,1:T(8,128)S(1)}, u32[]{:S(2)}, u32[]{:S(2)}) collective-permute-start(f32[4,1,4,10,64]{4,3,2,0,1:T(8,128)S(1)} %pad_maximum_fusion.1), channel_id=1, source_target_pairs={{15,0},{0,1},{1,2},{2,3},{3,4},{4,5},{5,6},{6,7},{7,8},{8,9},{9,10... | collective-permute-start | bytes 122888 | tf_op jit(solution)/shard_map/ppermute | solution.py:33
  52.8 6.9 %collective-permute-start.7 = (f32[4,1,4,10,64]{4,3,2,0,1:T(8,128)S(1)}, f32[4,1,4,10,64]{4,3,2,0,1:T(8,128)S(1)}, u32[]{:S(2)}, u32[]{:S(2)}) collective-permute-start(f32[4,1,4,10,64]{4,3,2,0,1:T(8,128)S(1)} %collective-permute-done.6), channel_id=1, source_target_pairs={{1,0},{2,1},{3,2},{4,3},{5,4},{6,5},{7,6},{8,7},{9,8},{10,9},{11,1... | collective-permute-start | bytes 122888 | tf_op jit(solution)/shard_map/ppermute | solution.py:33
  55.3 13.0 %collective-permute-start.5 = (f32[4,1,4,10,64]{4,3,2,0,1:T(8,128)S(1)}, f32[4,1,4,10,64]{4,3,2,0,1:T(8,128)S(1)}, u32[]{:S(2)}, u32[]{:S(2)}) collective-permute-start(f32[4,1,4,10,64]{4,3,2,0,1:T(8,128)S(1)} %collective-permute-done.4), channel_id=1, source_target_pairs={{15,0},{0,1},{1,2},{2,3},{3,4},{4,5},{5,6},{6,7},{7,8},{8,9},{9,10... | collective-permute-start | bytes 122888 | tf_op jit(solution)/shard_map/ppermute | solution.py:33
  78.8 7.0 %collective-permute-start.9 = (f32[1,1,1,8,64]{4,3,2,1,0:T(8,128)S(1)}, f32[1,1,1,8,64]{4,3,2,1,0:T(8,128)S(1)}, u32[]{:S(2)}, u32[]{:S(2)}) collective-permute-start(f32[1,1,1,8,64]{4,3,2,1,0:T(8,128)S(1)} %get-tuple-element.344), channel_id=1, source_target_pairs={{128,0},{256,128},{384,256},{0,384},{129,1},{257,129},{385,257},{1... | collective-permute-start | bytes 6152 | tf_op jit(solution)/shard_map/ppermute | solution.py:25
  83.8 5.5 %collective-permute-start.8 = (f32[1,1,1,8,64]{4,3,2,1,0:T(8,128)S(1)}, f32[1,1,1,8,64]{4,3,2,1,0:T(8,128)S(1)}, u32[]{:S(2)}, u32[]{:S(2)}) collective-permute-start(f32[1,1,1,8,64]{4,3,2,1,0:T(8,128)S(1)} %get-tuple-element.343), channel_id=1, source_target_pairs={{0,128},{128,256},{256,384},{384,0},{1,129},{129,257},{257,385},{3... | collective-permute-start | bytes 6152 | tf_op jit(solution)/shard_map/ppermute | solution.py:24
  89.3 4.4 %collective-permute-start.11 = (f32[1,1,4,1,64]{4,3,2,1,0:T(1,128)S(1)}, f32[1,1,4,1,64]{4,3,2,1,0:T(1,128)S(1)}, u32[]{:S(2)}, u32[]{:S(2)}) collective-permute-start(f32[1,1,4,1,64]{4,3,2,1,0:T(1,128)S(1)} %get-tuple-element.342), channel_id=1, source_target_pairs={{16,0},{32,16},{48,32},{64,48},{80,64},{96,80},{112,96},{0,112},{1... | collective-permute-start | bytes 3080 | tf_op jit(solution)/shard_map/ppermute | solution.py:25
  91.3 6.7 %collective-permute-start.10 = (f32[1,1,4,1,64]{4,3,2,1,0:T(1,128)S(1)}, f32[1,1,4,1,64]{4,3,2,1,0:T(1,128)S(1)}, u32[]{:S(2)}, u32[]{:S(2)}) collective-permute-start(f32[1,1,4,1,64]{4,3,2,1,0:T(1,128)S(1)} %get-tuple-element.341), channel_id=1, source_target_pairs={{0,16},{16,32},{32,48},{48,64},{64,80},{80,96},{96,112},{112,0},{1... | collective-permute-start | bytes 3080 | tf_op jit(solution)/shard_map/ppermute | solution.py:24
  98.0 11.9 %collective-permute-start.12 = (f32[1,1,4,10,64]{4,3,2,1,0:T(8,128)S(1)}, f32[1,1,4,10,64]{4,3,2,1,0:T(8,128)S(1)}, u32[]{:S(2)}, u32[]{:S(2)}) collective-permute-start(f32[1,1,4,10,64]{4,3,2,1,0:T(8,128)S(1)} %pad_maximum_fusion.36), channel_id=1, source_target_pairs={{15,0},{0,1},{1,2},{2,3},{3,4},{4,5},{5,6},{6,7},{7,8},{8,9},{9,10... | collective-permute-start | bytes 30728 | tf_op jit(solution)/shard_map/ppermute | solution.py:33
  99.9 11.9 %collective-permute-start.14 = (f32[1,1,4,10,64]{4,3,2,1,0:T(8,128)S(1)}, f32[1,1,4,10,64]{4,3,2,1,0:T(8,128)S(1)}, u32[]{:S(2)}, u32[]{:S(2)}) collective-permute-start(f32[1,1,4,10,64]{4,3,2,1,0:T(8,128)S(1)} %pad_maximum_fusion.36), channel_id=1, source_target_pairs={{1,0},{2,1},{3,2},{4,3},{5,4},{6,5},{7,6},{8,7},{9,8},{10,9},{11,1... | collective-permute-start | bytes 30728 | tf_op jit(solution)/shard_map/ppermute | solution.py:33
  109.9 11.9 %collective-permute-start.13 = (f32[1,1,4,10,64]{4,3,2,1,0:T(8,128)S(1)}, f32[1,1,4,10,64]{4,3,2,1,0:T(8,128)S(1)}, u32[]{:S(2)}, u32[]{:S(2)}) collective-permute-start(f32[1,1,4,10,64]{4,3,2,1,0:T(8,128)S(1)} %collective-permute-done.12), channel_id=1, source_target_pairs={{15,0},{0,1},{1,2},{2,3},{3,4},{4,5},{5,6},{6,7},{7,8},{8,9},{9,10... | collective-permute-start | bytes 30728 | tf_op jit(solution)/shard_map/ppermute | solution.py:33
  111.8 11.5 %collective-permute-start.15 = (f32[1,1,4,10,64]{4,3,2,1,0:T(8,128)S(1)}, f32[1,1,4,10,64]{4,3,2,1,0:T(8,128)S(1)}, u32[]{:S(2)}, u32[]{:S(2)}) collective-permute-start(f32[1,1,4,10,64]{4,3,2,1,0:T(8,128)S(1)} %collective-permute-done.14), channel_id=1, source_target_pairs={{1,0},{2,1},{3,2},{4,3},{5,4},{6,5},{7,6},{8,7},{9,8},{10,9},{11,1... | collective-permute-start | bytes 30728 | tf_op jit(solution)/shard_map/ppermute | solution.py:33
where the time goes:
time: 170 us
  starting transfers between devices  68.4 us (40%)
  other arithmetic  64.5 us (38%)
  waiting for transfers between devices  34 us (20%)
    ppermute x8, starting transfers between devices, passed_along(): return lax.ppermute(block, axis, route)  43.1 us
    reduce_sum x8, other arithmetic, forces(): jnp.sum(factor * deltas[component], axis=-1)  42.9 us
    ppermute x8, waiting for transfers between devices, passed_along(): return lax.ppermute(block, axis, route)  18.4 us
    reduce_sum x5, other arithmetic, densities(): summed = summed + jnp.sum(weight * kernels(squared)[0], axis=-1)  16.7 us
    ppermute x4, starting transfers between devices, padded(): after = lax.ppermute(initial, axis, down)  16.7 us
    ppermute x4, waiting for transfers between devices, padded(): before = lax.ppermute(last, axis, up)  15.6 us
    ppermute x4, starting transfers between devices, padded(): before = lax.ppermute(last, axis, up)  8.65 us
  transfers between devices with their start and end apart: 16, of which 8 were waited for; matrix products, arithmetic and copies ran while one was open for 2% of the time, Pallas kernels for 0%

commit v1 on v0

v1 whole, which is shorter than its diff:
```python
import math

import jax
import jax.numpy as jnp
import ml_dtypes
import numpy as np
from jax import lax
from jax.experimental import pallas as pl
from jax.experimental.pallas import tpu as pltpu
from jax.sharding import PartitionSpec as P

SLOTS = 64
FAR = 100.0

cutoff_sq = 4.95 * 4.95
side_xy, side_z = 12.0, 2.5
KAPPA = math.log2(math.e) / 8.0
UNIT = math.sqrt(KAPPA)
TOP = KAPPA * cutoff_sq
RATIO = 8.0 / 3.0
DENSITY = 2.0 ** (-TOP) / TOP**2
PAIR = 2.0 ** (-TOP * RATIO)
SLOPE = 2.0 * 2.0 ** (-TOP) / TOP
G1, G2 = 2.0 / cutoff_sq, 1.0 / (8.0 * TOP)
H1, H2 = 4.0 * PAIR / TOP * 2.0 / cutoff_sq, 4.0 * PAIR / (3.0 * TOP * TOP)
PHI = 2.0 * PAIR / TOP**2

ROWS = 32
NY = 10
TERMS = 32
f32, bf16 = jnp.float32, jnp.bfloat16


def constants():
    lane = np.arange(256)
    off = np.zeros((ROWS, 256), np.float32)
    scale = np.zeros((ROWS, 256), np.float32)
    step = np.zeros((ROWS, 256), np.float32)
    off[0:10] = lane // SLOTS - 2
    off[10:20] = np.arange(10)[:, None] - 5
    off[20:30] = -0.5
    scale[0:20] = side_xy * UNIT
    scale[20:30] = side_z * UNIT
    step[20:30] = side_z * UNIT
    sel_b = np.zeros((NY, TERMS, 160), np.float32)
    sel_a = np.zeros((NY, TERMS, 160), np.float32)
    tops = []
    rest = np.float32(TOP)
    for _ in range(3):
        piece = rest.astype(ml_dtypes.bfloat16).astype(np.float32)
        tops.append(piece)
        rest = np.float32(rest - piece)
    for j in range(NY):
        row = 0
        for c in range(3):
            for pa, pb in ((0, 0), (0, 1), (0, 2), (1, 0), (1, 1), (2, 0)):
                sel_a[j, row, 32 * pa + 10 * c + j] = 2.0
                sel_b[j, row, 32 * pb + 10 * c + j] = 1.0
                row += 1
        for p in range(3):
            sel_a[j, row, 144] = -1.0
            sel_b[j, row, 96 + 16 * p + j] = 1.0
            row += 1
            sel_a[j, row, 96 + 16 * p + j] = -1.0
            sel_b[j, row, 144] = 1.0
            row += 1
            sel_a[j, row, 144] = tops[p]
            sel_b[j, row, 144] = 1.0
            row += 1
    outside = np.zeros((TERMS, 256), np.float32)
    outside[18] = 2.0**14
    return (
        off,
        scale,
        step,
        sel_b.reshape(NY * TERMS, 160).astype(ml_dtypes.bfloat16),
        sel_a.reshape(NY * TERMS, 160).astype(ml_dtypes.bfloat16),
        np.eye(256, dtype=np.float32).astype(ml_dtypes.bfloat16),
        outside.astype(ml_dtypes.bfloat16),
    )


def split3(x):
    a = x.astype(bf16)
    r = x - a.astype(f32)
    b = r.astype(bf16)
    c = (r - b.astype(f32)).astype(bf16)
    return a, b, c


def lanes_summed(rows):
    ones = jnp.ones((8, rows.shape[1]), f32)
    return lax.dot_general(
        ones,
        rows,
        (((1,), (1,)), ((), ())),
        precision=lax.Precision.HIGHEST,
        preferred_element_type=f32,
    )


def kernel(lo, mid, hi, off, scale, step, sel_b, sel_a, eye, outside, force, energy, R, B, A, ACC, COL, SUM, V):
    for l in range(9):
        raw = (lo, mid, hi)[l % 3][l // 3]
        v = (raw + off[...]) * scale[...] + float(l - 4) * step[...]
        sq = v * v
        n = sq + pltpu.roll(sq, ROWS - 10, 0) + pltpu.roll(sq, ROWS - 20, 0)
        pieces = jnp.concatenate(
            split3(v) + split3(n[:16]) + (jnp.ones((16, 256), bf16),), axis=0
        )
        partner = jnp.dot(sel_b[...], pieces, preferred_element_type=f32).astype(bf16)
        B[l, 0] = outside[...]
        B[l, NY + 1] = outside[...]
        for j in range(NY):
            B[l, j + 1] = partner[TERMS * j : TERMS * (j + 1)]
        if 2 <= l <= 6:
            V[...] = v
            centre = jnp.dot(sel_a[...], pieces, preferred_element_type=f32).astype(bf16)
            for j in range(NY):
                for c in range(3):
                    R[l - 2, j, c : c + 1, :] = V[10 * c + j : 10 * c + j + 1, :]
                A[l - 2, j] = lax.dot_general(
                    eye[...],
                    centre[TERMS * j : TERMS * (j + 1)],
                    (((1,), (1,)), ((), ())),
                    preferred_element_type=f32,
                ).astype(bf16)

    def density(l, j):
        for h in range(2):
            lhs = A[l, j, 64 * h : 64 * h + 192, :]
            total = jnp.zeros((192, 128), f32)
            for a in range(5):
                for c in range(3):
                    rhs = B[l + a, j + c, :, 128 * h : 128 * h + 128]
                    tau = jnp.maximum(jnp.dot(lhs, rhs, preferred_element_type=f32), 0.0)
                    total = total + tau * tau * jnp.exp2(tau)
            if h == 0:
                ACC[0:192] = total
                ACC[192:256] = jnp.zeros((64, 128), f32)
            else:
                ACC[64:256] += total
        summed = lanes_summed(ACC[...])[0:1]
        root = jnp.sqrt(jnp.maximum(summed * DENSITY, 0.5))
        R[l, j, 3:4, :] = (-0.5 * SLOPE) / root
        R[l, j, 4:5, :] = root

    @pl.loop(0, 5)
    def _(l):
        @pl.loop(0, NY)
        def _(j):
            density(l, j)

    @pl.loop(0, 8)
    def _(j):
        own = pltpu.roll(R[2, j + 1], 256 - 64, 1)[:, 0:128]
        COL[:, 0:8] = own.T

        @pl.loop(0, 8)
        def _(g):
            rows = pl.ds(pl.multiple_of(g * 16, 16), 16)
            cols = COL[rows, :]
            xp, yp, zp, sp = (jnp.broadcast_to(cols[:, i : i + 1], (16, 128)) for i in range(4))
            fx = fy = fz = ph = jnp.zeros((16, 128), f32)
            for a in range(5):
                for c in range(3):
                    for h in range(2):
                        ln = slice(128 * h, 128 * h + 128)
                        dx = xp - R[a, j + c, 0:1, ln]
                        dy = yp - R[a, j + c, 1:2, ln]
                        dz = zp - R[a, j + c, 2:3, ln]
                        slopes = sp + R[a, j + c, 3:4, ln]
                        tau = jnp.maximum(TOP - (dx * dx + dy * dy + dz * dz), 0.0)
                        u = jnp.exp2(tau) * tau
                        w = jnp.exp2(tau * RATIO) * tau
                        ph = ph + w * tau
                        push = slopes * (u * (G1 + G2 * tau)) + w * (H1 + H2 * tau)
                        fx = fx + push * dx
                        fy = fy + push * dy
                        fz = fz + push * dz
            for i, part in enumerate((fx, fy, fz, ph)):
                SUM[i, rows, :] = part

        occupied = own[0:1] < 0.5 * FAR * side_xy * UNIT
        for i in range(3):
            total = lanes_summed(SUM[i])[0:1] * (1.0 / UNIT)
            force[i, pl.ds(j, 1), :] = jnp.where(occupied, total, 0.0)
        pairs = lanes_summed(SUM[3])[0:1] * PHI - 2.0
        energy[pl.ds(j, 1), :] = jnp.where(occupied, 0.5 * pairs - own[4:5], 0.0)


def shifted(x, axis, distance):
    n = lax.axis_size(axis)
    return lax.ppermute(x, axis, [((i - distance) % n, i) for i in range(n)])


def local_step(lo, mid, hi, interpret=False):
    consts = [jnp.asarray(c) for c in constants()]
    vmem = pl.BlockSpec(memory_space=pltpu.VMEM)
    return pl.pallas_call(
        kernel,
        out_shape=(
            jax.ShapeDtypeStruct((3, 8, 128), f32),
            jax.ShapeDtypeStruct((8, 128), f32),
        ),
        in_specs=[vmem] * 10,
        out_specs=(vmem, vmem),
        scratch_shapes=[
            pltpu.VMEM((5, NY, 8, 256), f32),
            pltpu.VMEM((9, NY + 2, TERMS, 256), bf16),
            pltpu.VMEM((5, NY, 256, TERMS), bf16),
            pltpu.VMEM((256, 128), f32),
            pltpu.VMEM((128, 128), f32),
            pltpu.VMEM((4, 128, 128), f32),
            pltpu.VMEM((ROWS, 256), f32),
        ],
        compiler_params=pltpu.CompilerParams(vmem_limit_bytes=48 * 2**20),
        interpret=interpret,
    )(lo, mid, hi, *consts)


def body(positions, counts):
    empty = jnp.arange(SLOTS) >= counts[0][..., None]
    x = jnp.where(empty, FAR, positions[0, 0])
    own = jnp.stack([x, positions[1, 0], positions[2, 0]])
    own = jnp.swapaxes(own, 1, 2).reshape(3, 8, 128)
    before = shifted(own[:, 7:8], "gy", 1)
    after = shifted(own[:, 0:1], "gy", -1)
    own = jnp.concatenate([before, own, after], axis=1)
    before = shifted(own[:, :, 64:], "gx", 1)
    after = shifted(own[:, :, :64], "gx", -1)
    own = jnp.concatenate([before, own, after], axis=2).reshape(30, 256)
    own = jnp.pad(own, ((0, 2), (0, 0)))
    mid = jnp.stack([shifted(own, "gz", 3), own, shifted(own, "gz", -3)])
    lo = shifted(mid, "gz", 1)
    hi = shifted(mid, "gz", -1)
    force, energy = local_step(lo, mid, hi)
    force = jnp.swapaxes(force.reshape(3, 8, 2, 64), 1, 2)[:, None]
    energy = jnp.swapaxes(energy.reshape(8, 2, 64), 0, 1)[None]
    return force, energy


def solution(mesh):
    return jax.shard_map(
        body,
        mesh=mesh,
        in_specs=(P(None, "gz", "gx", "gy", None), P("gz", "gx", "gy")),
        out_specs=(P(None, "gz", "gx", "gy", None), P("gz", "gx", "gy", None)),
        check_vma=False,
    )
```

time: 170 us -> 140 us (0.82)
  Pallas kernels: 0 us -> 71.7 us
  other arithmetic: 64.5 us -> 0.88 us
  starting transfers between devices: 68.4 us -> 39 us
  waiting for transfers between devices: 34 us -> 23.8 us
  local copies, waits for them, and re-layouts: 1.1 us -> 3.03 us
    pallas_call x0 -> x1, Pallas kernels: none -> 71.7 us  [local_step(): pl.pallas_call(kernel, out_shape=(jax.ShapeDtypeStruct((3, 8, 128), f32),...]
    reduce_sum x13 -> x0, other arithmetic: 59.6 us -> none  [the longest x8 42.9 us: forces(): jnp.sum(factor * deltas[component], axis=-1)]
    ppermute x16 -> x8, starting transfers between devices: 68.4 us -> 39 us  [shifted(): return lax.ppermute(x, axis, [((i - distance) % n, i) for i in range(n)])]
    ppermute x16 -> x8, waiting for transfers between devices: 34 us -> 23.8 us  [shifted(): return lax.ppermute(x, axis, [((i - distance) % n, i) for i in range(n)])]
    concatenate x30 -> x2, other arithmetic: 3.03 us -> 0.1 us  [the longest x1 0.09 us: body(): own = jnp.concatenate([before, own, after], axis=2).reshape(30, 256)]
  transfers between devices with their start and end apart: 16 -> 8, of which waited for: 8 -> 5; matrix products, arithmetic and copies ran while one was open for 2% -> 0% of each run, Pallas kernels for 0% -> 0%
where the time goes in v1:
time: 140 us; the launch traced here: 139 us
  Pallas kernels  71.7 us (51%)
  starting transfers between devices  39 us (28%)
  waiting for transfers between devices  23.8 us (17%)
  local copies, waits for them, and re-layouts  3.03 us (2%)
    pallas_call x1, Pallas kernels, local_step(): pl.pallas_call(kernel, out_shape=(jax.ShapeDtypeStruct((3, 8, 128), f32),...  71.7 us
    ppermute x8, starting transfers between devices, shifted(): return lax.ppermute(x, axis, [((i - distance) % n, i) for i in range(n)])  39 us
    ppermute x8, waiting for transfers between devices, shifted(): return lax.ppermute(x, axis, [((i - distance) % n, i) for i in range(n)])  23.8 us
  transfers between devices with their start and end apart: 8, of which 5 were waited for; matrix products, arithmetic and copies ran while one was open for 0% of the time, Pallas kernels for 0%

profile of v1, /device:TPU:2, one launch (start us, length us, event | category | flops | bytes accessed | tf_op | source)
XLA Modules:
  0.0 139.2 jit_solution(16980648078761425001)
XLA Ops:
  0.6 0.7 slice_bitcast_fusion.1
  1.3 0.0 copy-start.7
  1.4 0.7 copy-done.7
  2.0 0.8 bitcast_select_fusion
  2.8 0.1 reshape.33
  2.9 1.9 %collective-permute-start = (f32[3,1,128]{2,1,0:T(1,128)S(1)}, f32[3,1,128]{2,1,0:T(1,128)S(1)}, u32[]{:S(2)}, u32[]{:S(2)}) collective-permute-start(f32[3,1,128]{2,1,0:T(1,128)S(1)} %get-tuple-element.12), channel_id=1, source_target_pairs={{112,0},{0,16},{16,32},{32,48},{48,64},{64,80},{80,96},{96,112},{1... | collective-permute-start | bytes 4616 | tf_op jit(solution)/shard_map/ppermute | solution.py:194
  4.8 5.4 %collective-permute-start.1 = (f32[3,1,128]{2,1,0:T(1,128)S(1)}, f32[3,1,128]{2,1,0:T(1,128)S(1)}, u32[]{:S(2)}, u32[]{:S(2)}) collective-permute-start(f32[3,1,128]{2,1,0:T(1,128)S(1)} %get-tuple-element.13), channel_id=1, source_target_pairs={{16,0},{32,16},{48,32},{64,48},{80,64},{96,80},{112,96},{0,112},{1... | collective-permute-start | bytes 4616 | tf_op jit(solution)/shard_map/ppermute | solution.py:194
  10.3 0.0 collective-permute-done
  10.3 1.3 collective-permute-done.1
  11.6 0.0 copy-start.4
  11.6 0.0 copy-start.5
  11.6 0.0 copy-start.6
  11.6 0.1 fusion
  11.7 3.4 %collective-permute-start.2 = (f32[3,10,64]{2,1,0:T(8,128)S(1)}, f32[3,10,64]{2,1,0:T(8,128)S(1)}, u32[]{:S(2)}, u32[]{:S(2)}) collective-permute-start(f32[3,10,64]{2,1,0:T(8,128)S(1)} %get-tuple-element.8), channel_id=1, source_target_pairs={{384,0},{0,128},{128,256},{256,384},{385,1},{1,129},{129,257},{257... | collective-permute-start | bytes 23048 | tf_op jit(solution)/shard_map/ppermute | solution.py:194
  15.1 6.3 %collective-permute-start.3 = (f32[3,10,64]{2,1,0:T(8,128)S(1)}, f32[3,10,64]{2,1,0:T(8,128)S(1)}, u32[]{:S(2)}, u32[]{:S(2)}) collective-permute-start(f32[3,10,64]{2,1,0:T(8,128)S(1)} %get-tuple-element.9), channel_id=1, source_target_pairs={{128,0},{256,128},{384,256},{0,384},{129,1},{257,129},{385,257},{1... | collective-permute-start | bytes 23048 | tf_op jit(solution)/shard_map/ppermute | solution.py:194
  21.4 0.0 collective-permute-done.2
  21.4 1.5 %collective-permute-done.3 = f32[3,10,64]{2,1,0:T(8,128)S(1)} collective-permute-done((f32[3,10,64]{2,1,0:T(8,128)S(1)}, f32[3,10,64]{2,1,0:T(8,128)S(1)}, u32[]{:S(2)}, u32[]{:S(2)}) %collective-permute-start.3) | collective-permute-done | bytes 7712 | tf_op jit(solution)/shard_map/ppermute | solution.py:194
  22.9 0.0 copy-start.2
  22.9 0.1 pad_maximum_fusion.1
  23.0 0.0 copy-start.1
  23.1 0.0 copy-start
  23.1 14.2 %collective-permute-start.5 = (f32[32,256]{1,0:T(8,128)S(1)}, f32[32,256]{1,0:T(8,128)S(1)}, u32[]{:S(2)}, u32[]{:S(2)}) collective-permute-start(f32[32,256]{1,0:T(8,128)S(1)} %get-tuple-element.7), channel_id=1, source_target_pairs={{3,0},{4,1},{5,2},{6,3},{7,4},{8,5},{9,6},{10,7},{11,8},{12,9},{13... | collective-permute-start | bytes 98312 | tf_op jit(solution)/shard_map/ppermute | solution.py:194
  37.3 1.9 %collective-permute-start.4 = (f32[32,256]{1,0:T(8,128)S(1)}, f32[32,256]{1,0:T(8,128)S(1)}, u32[]{:S(2)}, u32[]{:S(2)}) collective-permute-start(f32[32,256]{1,0:T(8,128)S(1)} %get-tuple-element.7), channel_id=1, source_target_pairs={{13,0},{14,1},{15,2},{0,3},{1,4},{2,5},{3,6},{4,7},{5,8},{6,9},{7,... | collective-permute-start | bytes 98312 | tf_op jit(solution)/shard_map/ppermute | solution.py:194
  39.2 0.0 collective-permute-done.5
  39.2 12.4 %collective-permute-done.4 = f32[32,256]{1,0:T(8,128)S(1)} collective-permute-done((f32[32,256]{1,0:T(8,128)S(1)}, f32[32,256]{1,0:T(8,128)S(1)}, u32[]{:S(2)}, u32[]{:S(2)}) %collective-permute-start.4) | collective-permute-done | bytes 32800 | tf_op jit(solution)/shard_map/ppermute | solution.py:194
  51.6 0.0 copy-start.3
  51.6 1.9 %collective-permute-start.7 = (f32[3,32,256]{2,1,0:T(8,128)S(1)}, f32[3,32,256]{2,1,0:T(8,128)S(1)}, u32[]{:S(2)}, u32[]{:S(2)}) collective-permute-start(f32[3,32,256]{2,1,0:T(8,128)S(1)} %pad_maximum_fusion.mid), channel_id=1, source_target_pairs={{1,0},{2,1},{3,2},{4,3},{5,4},{6,5},{7,6},{8,7},{9,8},{10,9},{11,1... | collective-permute-start | bytes 294920 | tf_op jit(solution)/shard_map/ppermute | solution.py:194
  53.6 3.9 %collective-permute-start.6 = (f32[3,32,256]{2,1,0:T(8,128)S(1)}, f32[3,32,256]{2,1,0:T(8,128)S(1)}, u32[]{:S(2)}, u32[]{:S(2)}) collective-permute-start(f32[3,32,256]{2,1,0:T(8,128)S(1)} %pad_maximum_fusion.mid), channel_id=1, source_target_pairs={{15,0},{0,1},{1,2},{2,3},{3,4},{4,5},{5,6},{6,7},{7,8},{8,9},{9,10... | collective-permute-start | bytes 294920 | tf_op jit(solution)/shard_map/ppermute | solution.py:194
  57.5 0.7 collective-permute-done.7.hi
  58.1 7.9 %collective-permute-done.6.lo = f32[3,32,256]{2,1,0:T(8,128)S(1)} collective-permute-done((f32[3,32,256]{2,1,0:T(8,128)S(1)}, f32[3,32,256]{2,1,0:T(8,128)S(1)}, u32[]{:S(2)}, u32[]{:S(2)}) %collective-permute-start.6) | collective-permute-done | bytes 98336 | tf_op jit(solution)/shard_map/ppermute | solution.py:194
  66.1 0.0 copy-done.4
  66.1 0.0 copy-done.5
  66.1 0.0 copy-done.6
  66.1 0.0 copy-done.2
  66.1 0.0 copy-done.1
  66.1 0.0 copy-done
  66.1 0.0 copy-done.3
  66.1 71.7 %shard_map.104 = (f32[3,8,128]{2,1,0:T(8,128)S(1)}, f32[8,128]{1,0:T(8,128)S(1)}) custom-call(f32[3,32,256]{2,1,0:T(8,128)S(1)} %collective-permute-done.6.lo, f32[3,32,256]{2,1,0:T(8,128)S(1)} %pad_maximum_fusion.mid, f32[3,32,256]{2,1,0:T(8,128)S(1)} %collective-permute-done.7.hi, f32[32,256]{1,0:T(8,128)S(1)} %copy-done.5, f32[32,256]{1,0:T(8,128)S(1)} %copy-done.4, ...), custom_call_target="tpu_custom_call" | custom-call | tf_op jit(solution)/shard_map/pallas_call | solution.py:200
  137.8 0.1 reshape.36
  137.9 0.6 copy.19
  138.5 0.1 reshape.35
  138.6 0.6 copy.18
  (7 shorter events, 0.1 us)
Async XLA Ops:
  1.3 0.7 copy-start.7
  2.9 7.4 %collective-permute-start = (f32[3,1,128]{2,1,0:T(1,128)S(1)}, f32[3,1,128]{2,1,0:T(1,128)S(1)}, u32[]{:S(2)}, u32[]{:S(2)}) collective-permute-start(f32[3,1,128]{2,1,0:T(1,128)S(1)} %get-tuple-element.12), channel_id=1, source_target_pairs={{112,0},{0,16},{16,32},{32,48},{48,64},{64,80},{80,96},{96,112},{1... | collective-permute-start | bytes 4616 | tf_op jit(solution)/shard_map/ppermute | solution.py:194
  4.8 6.7 %collective-permute-start.1 = (f32[3,1,128]{2,1,0:T(1,128)S(1)}, f32[3,1,128]{2,1,0:T(1,128)S(1)}, u32[]{:S(2)}, u32[]{:S(2)}) collective-permute-start(f32[3,1,128]{2,1,0:T(1,128)S(1)} %get-tuple-element.13), channel_id=1, source_target_pairs={{16,0},{32,16},{48,32},{64,48},{80,64},{96,80},{112,96},{0,112},{1... | collective-permute-start | bytes 4616 | tf_op jit(solution)/shard_map/ppermute | solution.py:194
  11.6 54.5 %copy-start.4 = (f32[32,256]{1,0:T(8,128)S(1)}, f32[32,256]{1,0:T(8,128)}, u32[]{:S(2)}) copy-start(f32[32,256]{1,0:T(8,128)} %constant.20.clone.scale) | copy-start | bytes 98308
  11.6 54.5 %copy-start.5 = (f32[32,256]{1,0:T(8,128)S(1)}, f32[32,256]{1,0:T(8,128)}, u32[]{:S(2)}) copy-start(f32[32,256]{1,0:T(8,128)} %constant.19.clone.off) | copy-start | bytes 98308
  11.6 54.5 %copy-start.6 = (bf16[32,256]{1,0:T(8,128)(2,1)S(1)}, bf16[32,256]{1,0:T(8,128)(2,1)}, u32[]{:S(2)}) copy-start(bf16[32,256]{1,0:T(8,128)(2,1)} %constant.25.clone.outside) | copy-start | bytes 49156
  11.7 9.7 %collective-permute-start.2 = (f32[3,10,64]{2,1,0:T(8,128)S(1)}, f32[3,10,64]{2,1,0:T(8,128)S(1)}, u32[]{:S(2)}, u32[]{:S(2)}) collective-permute-start(f32[3,10,64]{2,1,0:T(8,128)S(1)} %get-tuple-element.8), channel_id=1, source_target_pairs={{384,0},{0,128},{128,256},{256,384},{385,1},{1,129},{129,257},{257... | collective-permute-start | bytes 23048 | tf_op jit(solution)/shard_map/ppermute | solution.py:194
  15.1 7.8 %collective-permute-start.3 = (f32[3,10,64]{2,1,0:T(8,128)S(1)}, f32[3,10,64]{2,1,0:T(8,128)S(1)}, u32[]{:S(2)}, u32[]{:S(2)}) collective-permute-start(f32[3,10,64]{2,1,0:T(8,128)S(1)} %get-tuple-element.9), channel_id=1, source_target_pairs={{128,0},{256,128},{384,256},{0,384},{129,1},{257,129},{385,257},{1... | collective-permute-start | bytes 23048 | tf_op jit(solution)/shard_map/ppermute | solution.py:194
  22.9 43.2 %copy-start.2 = (bf16[256,256]{1,0:T(8,128)(2,1)S(1)}, bf16[256,256]{1,0:T(8,128)(2,1)}, u32[]{:S(2)}) copy-start(bf16[256,256]{1,0:T(8,128)(2,1)} %constant.24.clone.eye) | copy-start | bytes 393220
  23.0 43.1 %copy-start.1 = (bf16[320,160]{1,0:T(8,128)(2,1)S(1)}, bf16[320,160]{1,0:T(8,128)(2,1)}, u32[]{:S(2)}) copy-start(bf16[320,160]{1,0:T(8,128)(2,1)} %constant.22.clone.sel_b) | copy-start | bytes 307204
  23.1 43.1 %copy-start = (bf16[320,160]{1,0:T(8,128)(2,1)S(1)}, bf16[320,160]{1,0:T(8,128)(2,1)}, u32[]{:S(2)}) copy-start(bf16[320,160]{1,0:T(8,128)(2,1)} %constant.23.clone.sel_a) | copy-start | bytes 307204
  23.1 16.1 %collective-permute-start.5 = (f32[32,256]{1,0:T(8,128)S(1)}, f32[32,256]{1,0:T(8,128)S(1)}, u32[]{:S(2)}, u32[]{:S(2)}) collective-permute-start(f32[32,256]{1,0:T(8,128)S(1)} %get-tuple-element.7), channel_id=1, source_target_pairs={{3,0},{4,1},{5,2},{6,3},{7,4},{8,5},{9,6},{10,7},{11,8},{12,9},{13... | collective-permute-start | bytes 98312 | tf_op jit(solution)/shard_map/ppermute | solution.py:194
  37.3 14.3 %collective-permute-start.4 = (f32[32,256]{1,0:T(8,128)S(1)}, f32[32,256]{1,0:T(8,128)S(1)}, u32[]{:S(2)}, u32[]{:S(2)}) collective-permute-start(f32[32,256]{1,0:T(8,128)S(1)} %get-tuple-element.7), channel_id=1, source_target_pairs={{13,0},{14,1},{15,2},{0,3},{1,4},{2,5},{3,6},{4,7},{5,8},{6,9},{7,... | collective-permute-start | bytes 98312 | tf_op jit(solution)/shard_map/ppermute | solution.py:194
  51.6 14.5 %copy-start.3 = (f32[32,256]{1,0:T(8,128)S(1)}, f32[32,256]{1,0:T(8,128)}, u32[]{:S(2)}) copy-start(f32[32,256]{1,0:T(8,128)} %constant.21.clone.step) | copy-start | bytes 98308
  51.6 6.5 %collective-permute-start.7 = (f32[3,32,256]{2,1,0:T(8,128)S(1)}, f32[3,32,256]{2,1,0:T(8,128)S(1)}, u32[]{:S(2)}, u32[]{:S(2)}) collective-permute-start(f32[3,32,256]{2,1,0:T(8,128)S(1)} %pad_maximum_fusion.mid), channel_id=1, source_target_pairs={{1,0},{2,1},{3,2},{4,3},{5,4},{6,5},{7,6},{8,7},{9,8},{10,9},{11,1... | collective-permute-start | bytes 294920 | tf_op jit(solution)/shard_map/ppermute | solution.py:194
  53.6 12.5 %collective-permute-start.6 = (f32[3,32,256]{2,1,0:T(8,128)S(1)}, f32[3,32,256]{2,1,0:T(8,128)S(1)}, u32[]{:S(2)}, u32[]{:S(2)}) collective-permute-start(f32[3,32,256]{2,1,0:T(8,128)S(1)} %pad_maximum_fusion.mid), channel_id=1, source_target_pairs={{15,0},{0,1},{1,2},{2,3},{3,4},{4,5},{5,6},{6,7},{7,8},{8,9},{9,10... | collective-permute-start | bytes 294920 | tf_op jit(solution)/shard_map/ppermute | solution.py:194

commit v2 on v1

v2 whole, which is shorter than its diff:
```python
import math

import jax
import jax.numpy as jnp
import ml_dtypes
import numpy as np
from jax import lax
from jax.experimental import pallas as pl
from jax.experimental.pallas import tpu as pltpu
from jax.sharding import PartitionSpec as P

SLOTS = 64
FAR = 100.0

cutoff_sq = 4.95 * 4.95
side_xy, side_z = 12.0, 2.5
KAPPA = math.log2(math.e) / 8.0
UNIT = math.sqrt(KAPPA)
TOP = KAPPA * cutoff_sq
RATIO = 8.0 / 3.0
DENSITY = 2.0 ** (-TOP) / TOP**2
PAIR = 2.0 ** (-TOP * RATIO)
SLOPE = 2.0 * 2.0 ** (-TOP) / TOP
G1, G2 = 2.0 / cutoff_sq, 1.0 / (8.0 * TOP)
H1, H2 = 4.0 * PAIR / TOP * 2.0 / cutoff_sq, 4.0 * PAIR / (3.0 * TOP * TOP)
PHI = 2.0 * PAIR / TOP**2

NY = 10
TILE = 16
LAYERS, MIDDLE = 9, 5
TERMS = 32
DEPTH = 13 * TILE
WINDOW, CHUNK, EXTRA = 768, 768, 128
UNROLL = 5
CAPACITY = LAYERS * 256 + WINDOW + EXTRA
EMPTY = FAR * side_xy * UNIT
BOX = (side_xy * UNIT, 4 * side_xy * UNIT, 0.5 * side_z * UNIT)
NEAR = TOP * 1.001
f32, bf16 = jnp.float32, jnp.bfloat16


def constants():
    sel_b = np.zeros((NY, TERMS, DEPTH), np.float32)
    sel_a = np.zeros((NY, TERMS, DEPTH), np.float32)
    tops = []
    rest = np.float32(TOP)
    for _ in range(3):
        piece = rest.astype(ml_dtypes.bfloat16).astype(np.float32)
        tops.append(piece)
        rest = np.float32(rest - piece)
    one = 12 * TILE
    for j in range(NY):
        row = 0
        for c in range(3):
            for pa, pb in ((0, 0), (0, 1), (0, 2), (1, 0), (1, 1), (2, 0)):
                sel_a[j, row, TILE * (3 * c + pa) + j] = 2.0
                sel_b[j, row, TILE * (3 * c + pb) + j] = 1.0
                row += 1
        for p in range(3):
            sel_a[j, row, one] = -1.0
            sel_b[j, row, TILE * (9 + p) + j] = 1.0
            row += 1
            sel_a[j, row, TILE * (9 + p) + j] = -1.0
            sel_b[j, row, one] = 1.0
            row += 1
            sel_a[j, row, one] = tops[p]
            sel_b[j, row, one] = 1.0
            row += 1
    across = np.zeros((DEPTH, NY, 128), np.float32)
    across[:, :, :TERMS] = sel_b.transpose(2, 0, 1)
    outside = np.zeros((WINDOW + EXTRA, TERMS), np.float32)
    outside[:, 18] = 2.0**14
    lane = np.arange(256)
    cast = lambda x: x.astype(ml_dtypes.bfloat16)
    return (
        cast(across.reshape(DEPTH, NY * 128)),
        cast(sel_a.reshape(NY * TERMS, DEPTH)),
        cast(np.eye(256, dtype=np.float32)),
        cast((lane[:, None] <= lane[None, :]).astype(np.float32)),
        cast(outside),
    )


def split3(x):
    a = x.astype(bf16)
    r = x - a.astype(f32)
    b = r.astype(bf16)
    c = (r - b.astype(f32)).astype(bf16)
    return (a, b, c)


def pieces(x, y, z):
    parts = split3(x) + split3(y) + split3(z) + split3(x * x + y * y + z * z)
    return jnp.concatenate(parts + (jnp.ones((TILE, x.shape[1]), bf16),), axis=0)


def lanes_summed(rows):
    ones = jnp.ones((8, rows.shape[1]), bf16)
    total = jnp.zeros((8, rows.shape[0]), f32)
    for part in split3(rows):
        total = total + lax.dot_general(
            ones, part, (((1,), (1,)), ((), ())), preferred_element_type=f32
        )
    return total


def across(x, index):
    return jnp.take_along_axis(x, index, axis=1)


def taken(x, index):
    low = across(x[:, :128], index & 127)
    high = across(x[:, 128:], index & 127)
    return jnp.where(index >= 128, high, low)


def packed(count, fields, group):
    place = lax.broadcasted_iota(jnp.int32, (TILE, 128), 1) + 128 * group
    want = place.astype(f32)
    low, high = count[:, :128], count[:, 128:]
    beyond = want >= low[:, 127:128]
    at = jnp.zeros((TILE, 128), jnp.int32)
    for step in (64, 32, 16, 8, 4, 2, 1):
        probe = at + (step - 1)
        seen = across(high, probe)
        if group == 0:
            seen = jnp.where(beyond, seen, across(low, probe))
        at = jnp.where(seen <= want, at + step, at)
    there = want < high[:, 127:128]
    found = []
    for field, blank in zip(fields, (EMPTY, 0.0, 0.0)):
        value = across(field[:, 128:], at)
        if group == 0:
            value = jnp.where(beyond, value, across(field[:, :128], at))
        found.append(jnp.where(there, value, blank))
    return found


def push_parts(centre, partner, sums):
    (xp, yp, zp, sp), (xq, yq, zq, sq), (fx, fy, fz, ph) = centre, partner, sums
    dx, dy, dz = xp - xq, yp - yq, zp - zq
    tau = jnp.maximum(TOP - (dx * dx + dy * dy + dz * dz), 0.0)
    u = jnp.exp2(tau) * tau
    w = jnp.exp2(tau * RATIO) * tau
    push = (sp + sq) * (u * (G1 + G2 * tau)) + w * (H1 + H2 * tau)
    return fx + push * dx, fy + push * dy, fz + push * dz, ph + w * tau


def kernel(
    at_z, recv, place_b, sel_a, eye, upto, outside, force, energy,
    COUNT, MASK, CUM, NUMS, OFF, XYZ, TURNED, P, C, D, SLOPE_D, ROOT_D, OWN, COL, SUM, RES, sem,
):
    SLOPE_D[...] = jnp.ones(SLOPE_D.shape, f32)
    row = lax.broadcasted_iota(jnp.int32, (TILE, 256), 0)
    cell = lax.broadcasted_iota(jnp.int32, (TILE, 256), 1) // SLOTS
    real = row < NY
    ring = recv.shape[0]

    for l in range(LAYERS):
        source = lax.rem(at_z[0] + (l + ring - 4), ring)
        raw = recv[source, 1 if l == LAYERS - 1 else 0]
        x = (raw[0:TILE] + (cell - 2).astype(f32)) * (side_xy * UNIT)
        y = (pltpu.roll(raw, 32 - NY, 0)[0:TILE] + (row - 5).astype(f32)) * (side_xy * UNIT)
        z = (pltpu.roll(raw, 32 - 2 * NY, 0)[0:TILE] + (l - 4.5)) * (side_z * UNIT)
        for c, value in enumerate((x, y, z)):
            XYZ[l, c] = value
        apart = [jnp.maximum(jnp.abs(v) - side, 0.0) for v, side in zip((x, y, z), BOX)]
        far = apart[0] * apart[0] + apart[1] * apart[1] + apart[2] * apart[2]
        mark = lambda test: jnp.where(real & test, 1.0, 0.0).astype(bf16)
        MASK[TILE * l : TILE * (l + 1)] = mark(far < 4.0 * NEAR)
        if 2 <= l <= 6:
            MASK[TILE * (l + 7) : TILE * (l + 8)] = mark(far < NEAR)
        if l == 4:
            inside = (cell >= 1) & (cell <= 2) & (row >= 1) & (row <= 8) & (x < 0.5 * EMPTY)
            MASK[TILE * 14 : TILE * 15] = mark(inside)
            MASK[TILE * 15 : TILE * 16] = jnp.zeros((TILE, 256), bf16)
    CUM[...] = jnp.dot(MASK[...], upto[...], preferred_element_type=f32)
    COUNT[...] = lax.dot_general(
        jnp.ones((8, 256), bf16), MASK[...], (((1,), (1,)), ((), ())), preferred_element_type=f32
    ).astype(jnp.int32)
    copy = pltpu.make_async_copy(COUNT, NUMS, sem)
    copy.start()

    for l in range(MIDDLE):
        count = CUM[TILE * (l + 9) : TILE * (l + 10)]
        fields = [XYZ[l + 2, c] for c in range(3)]
        groups = [packed(count, fields, w) for w in range(2)]
        for w in range(2):
            for c in range(3):
                D[l, c, w] = groups[w][c]
            terms = jnp.dot(sel_a[...], pieces(*groups[w]), preferred_element_type=f32).astype(bf16)
            for j in range(NY):
                C[l, j, w] = terms[TERMS * j : TERMS * (j + 1)]
    copy.wait()

    for j in range(NY + 2):
        start = jnp.int32(0)
        for l in range(LAYERS):
            OFF[l, j] = start
            if 1 <= j <= NY:
                start = start + ((NUMS[0, TILE * l + j - 1] + 15) >> 4 << 4)
        OFF[LAYERS, j] = start
    for l in range(LAYERS):
        count = CUM[TILE * l : TILE * (l + 1)]
        fields = [XYZ[l, c] for c in range(3)]
        both = [pieces(*packed(count, fields, w)) for w in range(2)]
        TURNED[256 * l : 256 * (l + 1)] = lax.dot_general(
            eye[...],
            jnp.concatenate(both, axis=1),
            (((1,), (1,)), ((), ())),
            preferred_element_type=f32,
        ).astype(bf16)
    for j in range(NY):
        place = place_b[:, 128 * j : 128 * (j + 1)]
        rows = jnp.dot(TURNED[...], place, preferred_element_type=f32)[:, :TERMS].astype(bf16)
        for l in range(LAYERS):
            start = pl.multiple_of(OFF[l, j + 1], 16)
            P[j + 1, pl.ds(start, 256), :] = rows[256 * l : 256 * (l + 1)]
    for j in range(NY + 2):
        P[j, pl.ds(pl.multiple_of(OFF[LAYERS, j], 16), WINDOW + EXTRA), :] = outside[...]

    def density(rows, lanes):
        tau = jnp.maximum(jnp.dot(rows, lanes, preferred_element_type=f32), 0.0)
        value = tau * tau * jnp.exp2(tau)
        return jnp.sum(value.reshape(-1, 8, 128), axis=0)

    def summed(l, j, w):
        total = jnp.zeros((8, 128), f32)
        for side in range(3):
            start = pl.multiple_of(OFF[l, j + side], 16)
            for part in range(0, WINDOW, CHUNK):
                at = pl.multiple_of(start + part, 16)
                total = total + density(P[j + side, pl.ds(at, CHUNK), :], C[l, j, w])
        SLOPE_D[l, w, pl.ds(j, 1), :] = jnp.sum(total, axis=0, keepdims=True)

    def rest(l, j, w):
        total = jnp.zeros((8, 128), f32)
        for side in range(3):
            start = OFF[l, j + side] + WINDOW
            more = jnp.maximum(OFF[l + MIDDLE, j + side] - start + EXTRA - 1, 0) // EXTRA

            def further(i, total):
                at = pl.multiple_of(start + i * EXTRA, 16)
                return total + density(P[j + side, pl.ds(at, EXTRA), :], C[l, j, w])

            total = lax.fori_loop(0, more, further, total)
        SLOPE_D[l, w, pl.ds(j, 1), :] += jnp.sum(total, axis=0, keepdims=True)

    @pl.loop(0, MIDDLE)
    def _(l):
        @pl.loop(0, NY, step=UNROLL)
        def _(first):
            for u in range(UNROLL):
                summed(l, first + u, 0)
            for u in range(UNROLL):
                j = first + u
                many = NUMS[0, TILE * (l + 9) + j] > 128
                longest = jnp.int32(0)
                for side in range(3):
                    longest = jnp.maximum(longest, OFF[l + MIDDLE, j + side] - OFF[l, j + side])

                @pl.when(many)
                def _(j=j):
                    summed(l, j, 1)

                @pl.when(longest > WINDOW)
                def _(j=j, many=many):
                    @pl.loop(0, jnp.where(many, 2, 1))
                    def _(w):
                        rest(l, j, w)

    root = jnp.sqrt(jnp.maximum(SLOPE_D[...] * DENSITY, 0.5))
    ROOT_D[...] = root
    SLOPE_D[...] = (-0.5 * SLOPE) / root

    count = CUM[TILE * 11 : TILE * 12]
    before = count[:, SLOTS - 1 : SLOTS].astype(jnp.int32)
    index = lax.broadcasted_iota(jnp.int32, (TILE, 128), 1) + before
    for c, pair in enumerate(
        [[D[2, c, w] for w in range(2)] for c in range(3)]
        + [[A[2, w] for w in range(2)] for A in (SLOPE_D, ROOT_D)]
    ):
        OWN[c] = taken(jnp.concatenate(pair, axis=1), index)

    def partner(l, j, w):
        one = pl.ds(j, 1)
        return (D[l, 0, w, one, :], D[l, 1, w, one, :], D[l, 2, w, one, :], SLOPE_D[l, w, one, :])

    def centre(j, rows):
        cols = COL[j, rows, :]
        return tuple(jnp.broadcast_to(cols[:, i : i + 1], (16, 128)) for i in range(4))

    @pl.loop(0, 8)
    def _(j):
        stack = jnp.concatenate([OWN[c, pl.ds(j + 1, 1), :] for c in range(4)] * 2, axis=0)
        COL[j, :, 0:8] = stack.T

        @pl.loop(0, (NUMS[0, TILE * 14 + j + 1] + 15) >> 4)
        def _(g):
            rows = pl.ds(pl.multiple_of(g * 16, 16), 16)
            mine = centre(j, rows)
            sums = (jnp.zeros((16, 128), f32),) * 4
            for l in range(MIDDLE):
                for side in range(3):
                    sums = push_parts(mine, partner(l, j + side, 0), sums)
            for i in range(4):
                SUM[j, i, rows, :] = sums[i]

    @pl.loop(0, MIDDLE)
    def _(l):
        @pl.loop(0, NY)
        def _(k):
            @pl.when(NUMS[0, TILE * (l + 9) + k] > 128)
            def _():
                @pl.loop(jnp.maximum(k - 2, 0), jnp.minimum(k + 1, 8))
                def _(j):
                    @pl.loop(0, (NUMS[0, TILE * 14 + j + 1] + 15) >> 4)
                    def _(g):
                        rows = pl.ds(pl.multiple_of(g * 16, 16), 16)
                        sums = tuple(SUM[j, i, rows, :] for i in range(4))
                        sums = push_parts(centre(j, rows), partner(l, k, 1), sums)
                        for i in range(4):
                            SUM[j, i, rows, :] = sums[i]

    for j in range(8):
        for i in range(4):
            RES[i, j : j + 1, :] = lanes_summed(SUM[j, i])[0:1]

    back = pltpu.roll(count, 256 - SLOTS, 1)[:, :128].astype(jnp.int32) - 1 - before
    back = jnp.concatenate([pltpu.roll(back, TILE - 1, 0)[0:8]], axis=0)
    occupied = pltpu.roll(XYZ[4, 0], 256 - SLOTS, 1)[:, :128]
    occupied = pltpu.roll(occupied, TILE - 1, 0)[0:8] < 0.5 * EMPTY
    back = jnp.where(occupied, back, 0)
    for i in range(3):
        force[i] = jnp.where(occupied, across(RES[i], back) * (1.0 / UNIT), 0.0)
    root = pltpu.roll(OWN[4], TILE - 1, 0)[0:8]
    energy[...] = jnp.where(occupied, across(RES[3] * (0.5 * PHI) - 1.0 - root, back), 0.0)


def local_step(at_z, recv, interpret=False):
    consts = [jnp.asarray(c) for c in constants()]
    vmem = pl.BlockSpec(memory_space=pltpu.VMEM)
    return pl.pallas_call(
        kernel,
        out_shape=(
            jax.ShapeDtypeStruct((3, 8, 128), f32),
            jax.ShapeDtypeStruct((8, 128), f32),
        ),
        in_specs=[pl.BlockSpec(memory_space=pltpu.SMEM)] + [vmem] * 6,
        out_specs=(vmem, vmem),
        scratch_shapes=[
            pltpu.VMEM((8, 256), jnp.int32),
            pltpu.VMEM((256, 256), bf16),
            pltpu.VMEM((256, 256), f32),
            pltpu.SMEM((8, 256), jnp.int32),
            pltpu.SMEM((LAYERS + 1, TILE), jnp.int32),
            pltpu.VMEM((LAYERS, 3, TILE, 256), f32),
            pltpu.VMEM((LAYERS * 256, DEPTH), bf16),
            pltpu.VMEM((NY + 2, CAPACITY, TERMS), bf16),
            pltpu.VMEM((MIDDLE, NY, 2, TERMS, 128), bf16),
            pltpu.VMEM((MIDDLE, 3, 2, TILE, 128), f32),
            pltpu.VMEM((MIDDLE, 2, TILE, 128), f32),
            pltpu.VMEM((MIDDLE, 2, TILE, 128), f32),
            pltpu.VMEM((5, TILE, 128), f32),
            pltpu.VMEM((8, 128, 128), f32),
            pltpu.VMEM((8, 4, 128, 128), f32),
            pltpu.VMEM((4, 8, 128), f32),
            pltpu.SemaphoreType.DMA,
        ],
        compiler_params=pltpu.CompilerParams(vmem_limit_bytes=48 * 2**20),
        interpret=interpret,
    )(at_z, recv, *consts)


def along(axis, ring, distance):
    n = lax.axis_size(axis)
    return [(i, i - i % ring + (i + distance) % ring) for i in range(n)]


def around_y(distance):
    nz, ny = lax.axis_size("gz"), lax.axis_size("gy")
    pairs = []
    for k in range(nz):
        for j in range(ny):
            there = j + distance
            layer = k if 0 <= there < ny else (k + nz // 2) % nz
            pairs.append((j * nz + k, (there % ny) * nz + layer))
    return pairs


def turned(pair, swap):
    return jnp.where(swap, pair[::-1], pair)


def gathered(positions, counts):
    nz = lax.axis_size("gz")
    half = nz // 2
    at_y, at_z = lax.axis_index("gy"), lax.axis_index("gz") % half
    last_y = lax.axis_size("gy") - 1
    empty = jnp.arange(SLOTS) >= counts[0][..., None]
    x = jnp.where(empty, FAR, positions[0, 0])
    own = jnp.stack([x, positions[1, 0], positions[2, 0]])
    own = jnp.swapaxes(own, 1, 2).reshape(3, 8, 128)
    other = lax.ppermute(own, "gz", along("gz", nz, half))
    both = jnp.stack([own, other])
    up = turned(both[:, :, 7:8], at_y == last_y)
    down = turned(both[:, :, 0:1], at_y == 0)
    before = lax.ppermute(up, ("gy", "gz"), around_y(1))
    after = lax.ppermute(down, ("gy", "gz"), around_y(-1))
    both = jnp.concatenate([before, both, after], axis=2)
    nx = lax.axis_size("gx")
    before = lax.ppermute(both[..., 64:], "gx", along("gx", nx, 1))
    after = lax.ppermute(both[..., :64], "gx", along("gx", nx, -1))
    both = jnp.concatenate([before, both, after], axis=3).reshape(2, 30, 256)
    both = jnp.pad(both, ((0, 0), (0, 2), (0, 0)))
    chunks = []
    for there in range(half):
        ahead = at_z - there
        first = (jnp.abs(ahead) < half // 2) | (ahead == -(half // 2))
        chunks.append(turned(both, ~first))
    groups = [list(range(half)), list(range(half, nz))]
    recv = lax.all_to_all(jnp.stack(chunks), "gz", 0, 0, axis_index_groups=groups)
    return at_z.astype(jnp.int32).reshape(1), recv


def body(positions, counts):
    force, energy = local_step(*gathered(positions, counts))
    force = jnp.swapaxes(force.reshape(3, 8, 2, 64), 1, 2)[:, None]
    energy = jnp.swapaxes(energy.reshape(8, 2, 64), 0, 1)[None]
    return force, energy


def solution(mesh):
    return jax.shard_map(
        body,
        mesh=mesh,
        in_specs=(P(None, "gz", "gx", "gy", None), P("gz", "gx", "gy")),
        out_specs=(P(None, "gz", "gx", "gy", None), P("gz", "gx", "gy", None)),
        check_vma=False,
    )
```

time: 140 us -> 94.9 us (0.68)
  the two profiles are of different devices: /device:TPU:2 before, /device:TPU:122 now
where the time goes in v2:
time: 94.9 us; the launch traced here: 94.6 us
  Pallas kernels  41.4 us (44%)
  blocking collectives  26 us (27%)
  starting transfers between devices  12.3 us (13%)
  waiting for transfers between devices  9.78 us (10%)
  local copies, waits for them, and re-layouts  3.13 us (3%)
  other arithmetic  1.01 us (1%)
    pallas_call x1, Pallas kernels, local_step(): pl.pallas_call(kernel, out_shape=(jax.ShapeDtypeStruct((3, 8, 128), f32),...  41.4 us
    all_to_all x1, blocking collectives, gathered(): lax.all_to_all(jnp.stack(chunks), 'gz', 0, 0, axis_index_groups=groups)  26 us
    ppermute x1, starting transfers between devices, gathered(): other = lax.ppermute(own, 'gz', along('gz', nz, half))  4.7 us
    ppermute x1, waiting for transfers between devices, gathered(): other = lax.ppermute(own, 'gz', along('gz', nz, half))  4.69 us
    ppermute x1, starting transfers between devices, gathered(): before = lax.ppermute(both[..., 64:], 'gx', along('gx', nx, 1))  3.39 us
    ppermute x1, waiting for transfers between devices, gathered(): after = lax.ppermute(both[..., :64], 'gx', along('gx', nx, -1))  3.29 us
    ppermute x1, starting transfers between devices, gathered(): after = lax.ppermute(both[..., :64], 'gx', along('gx', nx, -1))  2.44 us
  transfers between devices with their start and end apart: 5, of which 4 were waited for; matrix products, arithmetic and copies ran while one was open for 0% of the time, Pallas kernels for 0%

profile of v2, /device:TPU:122, one launch (start us, length us, event | category | flops | bytes accessed | tf_op | source)
XLA Modules:
  0.0 94.6 jit_solution(18069783051463114800)
XLA Ops:
  0.6 0.7 slice_bitcast_fusion.1
  1.3 0.0 copy-start.5
  1.4 0.7 copy-done.5
  2.0 0.8 bitcast_select_fusion
  2.8 0.1 reshape.37
  2.9 4.7 %collective-permute-start = (f32[3,8,128]{2,1,0:T(8,128)S(1)}, f32[3,8,128]{2,1,0:T(8,128)S(1)}, u32[]{:S(2)}, u32[]{:S(2)}) collective-permute-start(f32[3,8,128]{2,1,0:T(8,128)S(1)} %reshape.37), channel_id=1, source_target_pairs={{0,8},{1,9},{2,10},{3,11},{4,12},{5,13},{6,14},{7,15},{8,0},{9,1},... | collective-permute-start | bytes 36872 | tf_op jit(solution)/shard_map/ppermute | solution.py:404
  7.6 0.1 stack_reshape.3
  7.7 4.7 %collective-permute-done = f32[3,8,128]{2,1,0:T(8,128)S(1)} collective-permute-done((f32[3,8,128]{2,1,0:T(8,128)S(1)}, f32[3,8,128]{2,1,0:T(8,128)S(1)}, u32[]{:S(2)}, u32[]{:S(2)}) %collective-permute-start) | collective-permute-done | bytes 12320 | tf_op jit(solution)/shard_map/ppermute | solution.py:404
  12.4 0.0 collective-permute-start.1
  12.5 1.7 %collective-permute-start.2 = (f32[2,3,1,128]{3,2,1,0:T(1,128)S(1)}, f32[2,3,1,128]{3,2,1,0:T(1,128)S(1)}, u32[]{:S(2)}, u32[]{:S(2)}) collective-permute-start(f32[2,3,1,128]{3,2,1,0:T(1,128)S(1)} %broadcast_select_fusion), channel_id=1, source_target_pairs={{0,120},{16,0},{32,16},{48,32},{64,48},{80,64},{96,80},{112,96},{1... | collective-permute-start | bytes 9224 | tf_op jit(solution)/shard_map/ppermute | solution.py:409
  14.2 1.3 %collective-permute-done.1 = f32[2,3,1,128]{3,2,1,0:T(1,128)S(1)} collective-permute-done((f32[2,3,1,128]{3,2,1,0:T(1,128)S(1)}, f32[2,3,1,128]{3,2,1,0:T(1,128)S(1)}, u32[]{:S(2)}, u32[]{:S(2)}) %collective-permute-start.1) | collective-permute-done | bytes 3104 | tf_op jit(solution)/shard_map/ppermute | solution.py:408
  15.4 0.0 collective-permute-done.2
  15.5 0.1 fusion.16
  15.6 3.4 %collective-permute-start.3 = (f32[2,3,10,64]{3,2,1,0:T(8,128)S(1)}, f32[2,3,10,64]{3,2,1,0:T(8,128)S(1)}, u32[]{:S(2)}, u32[]{:S(2)}) collective-permute-start(f32[2,3,10,64]{3,2,1,0:T(8,128)S(1)} %get-tuple-element.6), channel_id=1, source_target_pairs={{0,128},{128,256},{256,384},{384,0},{1,129},{129,257},{257,385},{3... | collective-permute-start | bytes 46088 | tf_op jit(solution)/shard_map/ppermute | solution.py:412
  19.0 2.4 %collective-permute-start.4 = (f32[2,3,10,64]{3,2,1,0:T(8,128)S(1)}, f32[2,3,10,64]{3,2,1,0:T(8,128)S(1)}, u32[]{:S(2)}, u32[]{:S(2)}) collective-permute-start(f32[2,3,10,64]{3,2,1,0:T(8,128)S(1)} %get-tuple-element.7), channel_id=1, source_target_pairs={{0,384},{128,0},{256,128},{384,256},{1,385},{129,1},{257,129},{385... | collective-permute-start | bytes 46088 | tf_op jit(solution)/shard_map/ppermute | solution.py:413
  21.5 0.5 collective-permute-done.3
  22.0 3.3 %collective-permute-done.4 = f32[2,3,10,64]{3,2,1,0:T(8,128)S(1)} collective-permute-done((f32[2,3,10,64]{3,2,1,0:T(8,128)S(1)}, f32[2,3,10,64]{3,2,1,0:T(8,128)S(1)}, u32[]{:S(2)}, u32[]{:S(2)}) %collective-permute-start.4) | collective-permute-done | bytes 15392 | tf_op jit(solution)/shard_map/ppermute | solution.py:413
  25.3 0.1 pad_maximum_fusion
  25.4 0.1 copy.13
  25.6 0.0 copy-start.4
  25.7 0.0 copy-start.3
  25.7 0.0 copy-start
  25.7 0.0 copy-start.1
  25.7 0.0 copy-start.2
  25.7 26.0 %all_to_all.5.recv = f32[8,2,32,256]{3,2,1,0:T(8,128)S(1)} all-to-all(f32[8,2,32,256]{3,2,1,0:T(8,128)S(1)} %fusion.15), channel_id=1, replica_groups={{0,1,2,3,4,5,6,7},{8,9,10,11,12,13,14,15},{16,17,18,19,20,21,22,23},{24..., dimensions={0} | all-to-all | bytes 1048576 | tf_op jit(solution)/shard_map/all_to_all | solution.py:422
  51.7 0.0 copy-done.4
  51.7 0.0 copy-done.3
  51.7 0.0 copy-done
  51.7 0.0 copy-done.1
  51.8 0.0 copy-done.2
  51.8 41.4 %shard_map.86 = (f32[3,8,128]{2,1,0:T(8,128)S(1)}, f32[8,128]{1,0:T(8,128)S(1)}) custom-call(s32[1]{0:T(128)} %bitcast.at_z, f32[8,2,32,256]{3,2,1,0:T(8,128)S(1)} %all_to_all.5.recv, bf16[208,1280]{1,0:T(8,128)(2,1)S(1)} %copy-done, bf16[320,208]{1,0:T(8,128)(2,1)S(1)} %copy-done.2, bf16[256,256]{1,0:T(8,128)(2,1)S(1)} %copy-done.3, ...), custom_call_target="tpu_custom_call" | custom-call | tf_op jit(solution)/shard_map/pallas_call | solution.py:343
  93.2 0.1 reshape.39
  93.3 0.6 copy.19
  93.9 0.1 reshape.40
  94.0 0.6 copy.20
  (16 shorter events, 0.1 us)
Async XLA Ops:
  1.3 0.7 copy-start.5
  2.9 9.5 %collective-permute-start = (f32[3,8,128]{2,1,0:T(8,128)S(1)}, f32[3,8,128]{2,1,0:T(8,128)S(1)}, u32[]{:S(2)}, u32[]{:S(2)}) collective-permute-start(f32[3,8,128]{2,1,0:T(8,128)S(1)} %reshape.37), channel_id=1, source_target_pairs={{0,8},{1,9},{2,10},{3,11},{4,12},{5,13},{6,14},{7,15},{8,0},{9,1},... | collective-permute-start | bytes 36872 | tf_op jit(solution)/shard_map/ppermute | solution.py:404
  12.4 3.0 %collective-permute-start.1 = (f32[2,3,1,128]{3,2,1,0:T(1,128)S(1)}, f32[2,3,1,128]{3,2,1,0:T(1,128)S(1)}, u32[]{:S(2)}, u32[]{:S(2)}) collective-permute-start(f32[2,3,1,128]{3,2,1,0:T(1,128)S(1)} %broadcast_select_fusion.1), channel_id=1, source_target_pairs={{0,16},{16,32},{32,48},{48,64},{64,80},{80,96},{96,112},{112,8},{1... | collective-permute-start | bytes 9224 | tf_op jit(solution)/shard_map/ppermute | solution.py:408
  12.5 3.0 %collective-permute-start.2 = (f32[2,3,1,128]{3,2,1,0:T(1,128)S(1)}, f32[2,3,1,128]{3,2,1,0:T(1,128)S(1)}, u32[]{:S(2)}, u32[]{:S(2)}) collective-permute-start(f32[2,3,1,128]{3,2,1,0:T(1,128)S(1)} %broadcast_select_fusion), channel_id=1, source_target_pairs={{0,120},{16,0},{32,16},{48,32},{64,48},{80,64},{96,80},{112,96},{1... | collective-permute-start | bytes 9224 | tf_op jit(solution)/shard_map/ppermute | solution.py:409
  15.6 6.4 %collective-permute-start.3 = (f32[2,3,10,64]{3,2,1,0:T(8,128)S(1)}, f32[2,3,10,64]{3,2,1,0:T(8,128)S(1)}, u32[]{:S(2)}, u32[]{:S(2)}) collective-permute-start(f32[2,3,10,64]{3,2,1,0:T(8,128)S(1)} %get-tuple-element.6), channel_id=1, source_target_pairs={{0,128},{128,256},{256,384},{384,0},{1,129},{129,257},{257,385},{3... | collective-permute-start | bytes 46088 | tf_op jit(solution)/shard_map/ppermute | solution.py:412
  19.0 6.3 %collective-permute-start.4 = (f32[2,3,10,64]{3,2,1,0:T(8,128)S(1)}, f32[2,3,10,64]{3,2,1,0:T(8,128)S(1)}, u32[]{:S(2)}, u32[]{:S(2)}) collective-permute-start(f32[2,3,10,64]{3,2,1,0:T(8,128)S(1)} %get-tuple-element.7), channel_id=1, source_target_pairs={{0,384},{128,0},{256,128},{384,256},{1,385},{129,1},{257,129},{385... | collective-permute-start | bytes 46088 | tf_op jit(solution)/shard_map/ppermute | solution.py:413
  25.6 26.1 %copy-start.4 = (bf16[256,256]{1,0:T(8,128)(2,1)S(1)}, bf16[256,256]{1,0:T(8,128)(2,1)}, u32[]{:S(2)}) copy-start(bf16[256,256]{1,0:T(8,128)(2,1)} %constant.63.clone.upto) | copy-start | bytes 393220
  25.7 26.1 %copy-start.3 = (bf16[256,256]{1,0:T(8,128)(2,1)S(1)}, bf16[256,256]{1,0:T(8,128)(2,1)}, u32[]{:S(2)}) copy-start(bf16[256,256]{1,0:T(8,128)(2,1)} %constant.62.clone.eye) | copy-start | bytes 393220
  25.7 26.1 %copy-start = (bf16[208,1280]{1,0:T(8,128)(2,1)S(1)}, bf16[208,1280]{1,0:T(8,128)(2,1)}, u32[]{:S(2)}) copy-start(bf16[208,1280]{1,0:T(8,128)(2,1)} %constant.60.clone.place_b) | copy-start | bytes 1597444
  25.7 26.0 %copy-start.1 = (bf16[896,32]{1,0:T(8,128)(2,1)S(1)}, bf16[896,32]{1,0:T(8,128)(2,1)}, u32[]{:S(2)}) copy-start(bf16[896,32]{1,0:T(8,128)(2,1)} %constant.64.clone.outside) | copy-start | bytes 172036
  25.7 26.0 %copy-start.2 = (bf16[320,208]{1,0:T(8,128)(2,1)S(1)}, bf16[320,208]{1,0:T(8,128)(2,1)}, u32[]{:S(2)}) copy-start(bf16[320,208]{1,0:T(8,128)(2,1)} %constant.61.clone.sel_a) | copy-start | bytes 399364

commit v3 on v2

--- a/solution.py
+++ b/solution.py
@@ -1,3 +1,4 @@
+import functools
 import math
 
 import jax
@@ -30,8 +31,8 @@
 LAYERS, MIDDLE = 9, 5
 TERMS = 32
 DEPTH = 13 * TILE
-WINDOW, CHUNK, EXTRA = 768, 768, 128
-UNROLL = 5
+WINDOW, EDGE, EXTRA = 768, 512, 128
+STEP = 16
 CAPACITY = LAYERS * 256 + WINDOW + EXTRA
 EMPTY = FAR * side_xy * UNIT
 BOX = (side_xy * UNIT, 4 * side_xy * UNIT, 0.5 * side_z * UNIT)
@@ -148,7 +149,7 @@
 
 def kernel(
     at_z, recv, place_b, sel_a, eye, upto, outside, force, energy,
-    COUNT, MASK, CUM, NUMS, OFF, XYZ, TURNED, P, C, D, SLOPE_D, ROOT_D, OWN, COL, SUM, RES, sem,
+    COUNT, MASK, CUM, NUMS, OFF, XYZ, TURNED, P, C, D, SLOPE_D, ROOT_D, OWN, LATE, COL, SUM, RES, sem,
 ):
     SLOPE_D[...] = jnp.ones(SLOPE_D.shape, f32)
     row = lax.broadcasted_iota(jnp.int32, (TILE, 256), 0)
@@ -157,8 +158,7 @@
     ring = recv.shape[0]
 
     for l in range(LAYERS):
-        source = lax.rem(at_z[0] + (l + ring - 4), ring)
-        raw = recv[source, 1 if l == LAYERS - 1 else 0]
+        raw = recv[lax.rem(at_z[0] + (l + ring - 4), ring)]
         x = (raw[0:TILE] + (cell - 2).astype(f32)) * (side_xy * UNIT)
         y = (pltpu.roll(raw, 32 - NY, 0)[0:TILE] + (row - 5).astype(f32)) * (side_xy * UNIT)
         z = (pltpu.roll(raw, 32 - 2 * NY, 0)[0:TILE] + (l - 4.5)) * (side_z * UNIT)
@@ -226,48 +226,47 @@
 
     def summed(l, j, w):
         total = jnp.zeros((8, 128), f32)
-        for side in range(3):
-            start = pl.multiple_of(OFF[l, j + side], 16)
-            for part in range(0, WINDOW, CHUNK):
-                at = pl.multiple_of(start + part, 16)
-                total = total + density(P[j + side, pl.ds(at, CHUNK), :], C[l, j, w])
-        SLOPE_D[l, w, pl.ds(j, 1), :] = jnp.sum(total, axis=0, keepdims=True)
+        for k in range(max(j - 1, 0), min(j + 2, NY)):
+            window = EDGE if k in (0, NY - 1) else WINDOW
+            start = pl.multiple_of(OFF[l, k + 1], 16)
+            total = total + density(P[k + 1, pl.ds(start, window), :], C[l, j, w])
+        SLOPE_D[l, w, j : j + 1, :] = jnp.sum(total, axis=0, keepdims=True)
 
     def rest(l, j, w):
         total = jnp.zeros((8, 128), f32)
-        for side in range(3):
-            start = OFF[l, j + side] + WINDOW
-            more = jnp.maximum(OFF[l + MIDDLE, j + side] - start + EXTRA - 1, 0) // EXTRA
+        for k in range(max(j - 1, 0), min(j + 2, NY)):
+            start = OFF[l, k + 1] + (EDGE if k in (0, NY - 1) else WINDOW)
+            more = jnp.maximum(OFF[l + MIDDLE, k + 1] - start + EXTRA - 1, 0) // EXTRA
 
             def further(i, total):
                 at = pl.multiple_of(start + i * EXTRA, 16)
-                return total + density(P[j + side, pl.ds(at, EXTRA), :], C[l, j, w])
+                return total + density(P[k + 1, pl.ds(at, EXTRA), :], C[l, j, w])
 
             total = lax.fori_loop(0, more, further, total)
-        SLOPE_D[l, w, pl.ds(j, 1), :] += jnp.sum(total, axis=0, keepdims=True)
+        SLOPE_D[l, w, j : j + 1, :] += jnp.sum(total, axis=0, keepdims=True)
 
     @pl.loop(0, MIDDLE)
     def _(l):
-        @pl.loop(0, NY, step=UNROLL)
-        def _(first):
-            for u in range(UNROLL):
-                summed(l, first + u, 0)
-            for u in range(UNROLL):
-                j = first + u
-                many = NUMS[0, TILE * (l + 9) + j] > 128
-                longest = jnp.int32(0)
-                for side in range(3):
-                    longest = jnp.maximum(longest, OFF[l + MIDDLE, j + side] - OFF[l, j + side])
-
-                @pl.when(many)
-                def _(j=j):
-                    summed(l, j, 1)
-
-                @pl.when(longest > WINDOW)
-                def _(j=j, many=many):
-                    @pl.loop(0, jnp.where(many, 2, 1))
-                    def _(w):
-                        rest(l, j, w)
+        for j in range(NY):
+            summed(l, j, 0)
+        excess = []
+        for k in range(NY):
+            length = OFF[l + MIDDLE, k + 1] - OFF[l, k + 1]
+            excess.append(length - (EDGE if k in (0, NY - 1) else WINDOW))
+        for j in range(NY):
+            many = NUMS[0, TILE * (l + 9) + j] > 128
+
+            @pl.when(many)
+            def _():
+                summed(l, j, 1)
+
+            most = functools.reduce(jnp.maximum, excess[max(j - 1, 0) : min(j + 2, NY)])
+
+            @pl.when(most > 0)
+            def _():
+                @pl.loop(0, jnp.where(many, 2, 1))
+                def _(w):
+                    rest(l, j, w)
 
     root = jnp.sqrt(jnp.maximum(SLOPE_D[...] * DENSITY, 0.5))
     ROOT_D[...] = root
@@ -282,41 +281,70 @@
     ):
         OWN[c] = taken(jnp.concatenate(pair, axis=1), index)
 
+    start = jnp.zeros((TILE, 1), f32)
+    place = lax.broadcasted_iota(jnp.int32, (TILE, 128), 1)
+    for c in range(4):
+        LATE[c] = jnp.full((TILE, 128), EMPTY if c == 0 else 0.0, f32)
+    for l in range(MIDDLE):
+        held = jnp.maximum(CUM[TILE * (l + 9) : TILE * (l + 10), 255:256] - 128.0, 0.0)
+        held = jnp.broadcast_to(held, (TILE, 128))
+        for side in range(3):
+            n = pltpu.roll(held, (TILE + 1 - side) % TILE, 0)
+            first = jnp.broadcast_to(start, (TILE, 128))
+            ours = (place.astype(f32) >= first) & (place.astype(f32) < first + n)
+            index = (place - first.astype(jnp.int32)) & 127
+            for c, field in enumerate([D[l, c, 1] for c in range(3)] + [SLOPE_D[l, 1]]):
+                field = pltpu.roll(field, (TILE + 1 - side) % TILE, 0)
+                LATE[c] = jnp.where(ours, across(field, index), LATE[c])
+            start = start + n[:, 0:1]
+    inner = lax.broadcasted_iota(jnp.int32, (TILE, 1), 0)
+    inner = (inner >= 1) & (inner <= 8)
+    crowded = jnp.max(jnp.where(inner, start, 0.0)) > 128.0
+
+    @pl.when(crowded)
+    def _():
+        LATE[0] = jnp.full((TILE, 128), EMPTY, f32)
+
     def partner(l, j, w):
         one = pl.ds(j, 1)
         return (D[l, 0, w, one, :], D[l, 1, w, one, :], D[l, 2, w, one, :], SLOPE_D[l, w, one, :])
 
     def centre(j, rows):
         cols = COL[j, rows, :]
-        return tuple(jnp.broadcast_to(cols[:, i : i + 1], (16, 128)) for i in range(4))
+        return tuple(jnp.broadcast_to(cols[:, i : i + 1], (STEP, 128)) for i in range(4))
+
+    def steps(j):
+        return (NUMS[0, TILE * 14 + j + 1] + STEP - 1) // STEP
 
     @pl.loop(0, 8)
     def _(j):
         stack = jnp.concatenate([OWN[c, pl.ds(j + 1, 1), :] for c in range(4)] * 2, axis=0)
         COL[j, :, 0:8] = stack.T
 
-        @pl.loop(0, (NUMS[0, TILE * 14 + j + 1] + 15) >> 4)
+        @pl.loop(0, steps(j))
         def _(g):
-            rows = pl.ds(pl.multiple_of(g * 16, 16), 16)
+            rows = pl.ds(pl.multiple_of(g * STEP, STEP), STEP)
             mine = centre(j, rows)
-            sums = (jnp.zeros((16, 128), f32),) * 4
+            sums = (jnp.zeros((STEP, 128), f32),) * 4
             for l in range(MIDDLE):
                 for side in range(3):
                     sums = push_parts(mine, partner(l, j + side, 0), sums)
+            late = tuple(LATE[c, pl.ds(j + 1, 1), :] for c in range(4))
+            sums = push_parts(mine, late, sums)
             for i in range(4):
                 SUM[j, i, rows, :] = sums[i]
 
-    @pl.loop(0, MIDDLE)
-    def _(l):
-        @pl.loop(0, NY)
-        def _(k):
-            @pl.when(NUMS[0, TILE * (l + 9) + k] > 128)
-            def _():
+    @pl.when(crowded)
+    def _():
+        @pl.loop(0, MIDDLE)
+        def _(l):
+            @pl.loop(0, NY)
+            def _(k):
                 @pl.loop(jnp.maximum(k - 2, 0), jnp.minimum(k + 1, 8))
                 def _(j):
-                    @pl.loop(0, (NUMS[0, TILE * 14 + j + 1] + 15) >> 4)
+                    @pl.loop(0, steps(j))
                     def _(g):
-                        rows = pl.ds(pl.multiple_of(g * 16, 16), 16)
+                        rows = pl.ds(pl.multiple_of(g * STEP, STEP), STEP)
                         sums = tuple(SUM[j, i, rows, :] for i in range(4))
                         sums = push_parts(centre(j, rows), partner(l, k, 1), sums)
                         for i in range(4):
@@ -331,10 +359,15 @@
     occupied = pltpu.roll(XYZ[4, 0], 256 - SLOTS, 1)[:, :128]
     occupied = pltpu.roll(occupied, TILE - 1, 0)[0:8] < 0.5 * EMPTY
     back = jnp.where(occupied, back, 0)
-    for i in range(3):
-        force[i] = jnp.where(occupied, across(RES[i], back) * (1.0 / UNIT), 0.0)
     root = pltpu.roll(OWN[4], TILE - 1, 0)[0:8]
-    energy[...] = jnp.where(occupied, across(RES[3] * (0.5 * PHI) - 1.0 - root, back), 0.0)
+    values = [RES[i] * (1.0 / UNIT) for i in range(3)] + [RES[3] * (0.5 * PHI) - 1.0 - root]
+    for i, value in enumerate(values):
+        value = jnp.where(occupied, across(value, back), 0.0)
+        for half, part in enumerate((value, pltpu.roll(value, SLOTS, 1))):
+            if i < 3:
+                force[i, half] = part[:, :SLOTS]
+            else:
+                energy[half] = part[:, :SLOTS]
 
 
 def local_step(at_z, recv, interpret=False):
@@ -343,8 +376,8 @@
     return pl.pallas_call(
         kernel,
         out_shape=(
-            jax.ShapeDtypeStruct((3, 8, 128), f32),
-            jax.ShapeDtypeStruct((8, 128), f32),
+            jax.ShapeDtypeStruct((3, 2, 8, SLOTS), f32),
+            jax.ShapeDtypeStruct((2, 8, SLOTS), f32),
         ),
         in_specs=[pl.BlockSpec(memory_space=pltpu.SMEM)] + [vmem] * 6,
         out_specs=(vmem, vmem),
@@ -362,6 +395,7 @@
             pltpu.VMEM((MIDDLE, 2, TILE, 128), f32),
             pltpu.VMEM((MIDDLE, 2, TILE, 128), f32),
             pltpu.VMEM((5, TILE, 128), f32),
+            pltpu.VMEM((4, TILE, 128), f32),
             pltpu.VMEM((8, 128, 128), f32),
             pltpu.VMEM((8, 4, 128, 128), f32),
             pltpu.VMEM((4, 8, 128), f32),
@@ -372,62 +406,31 @@
     )(at_z, recv, *consts)
 
 
-def along(axis, ring, distance):
+def along(axis, distance):
     n = lax.axis_size(axis)
-    return [(i, i - i % ring + (i + distance) % ring) for i in range(n)]
-
-
-def around_y(distance):
-    nz, ny = lax.axis_size("gz"), lax.axis_size("gy")
-    pairs = []
-    for k in range(nz):
-        for j in range(ny):
-            there = j + distance
-            layer = k if 0 <= there < ny else (k + nz // 2) % nz
-            pairs.append((j * nz + k, (there % ny) * nz + layer))
-    return pairs
-
-
-def turned(pair, swap):
-    return jnp.where(swap, pair[::-1], pair)
+    return [(i, (i + distance) % n) for i in range(n)]
 
 
 def gathered(positions, counts):
     nz = lax.axis_size("gz")
-    half = nz // 2
-    at_y, at_z = lax.axis_index("gy"), lax.axis_index("gz") % half
-    last_y = lax.axis_size("gy") - 1
     empty = jnp.arange(SLOTS) >= counts[0][..., None]
     x = jnp.where(empty, FAR, positions[0, 0])
     own = jnp.stack([x, positions[1, 0], positions[2, 0]])
     own = jnp.swapaxes(own, 1, 2).reshape(3, 8, 128)
-    other = lax.ppermute(own, "gz", along("gz", nz, half))
-    both = jnp.stack([own, other])
-    up = turned(both[:, :, 7:8], at_y == last_y)
-    down = turned(both[:, :, 0:1], at_y == 0)
-    before = lax.ppermute(up, ("gy", "gz"), around_y(1))
-    after = lax.ppermute(down, ("gy", "gz"), around_y(-1))
-    both = jnp.concatenate([before, both, after], axis=2)
-    nx = lax.axis_size("gx")
-    before = lax.ppermute(both[..., 64:], "gx", along("gx", nx, 1))
-    after = lax.ppermute(both[..., :64], "gx", along("gx", nx, -1))
-    both = jnp.concatenate([before, both, after], axis=3).reshape(2, 30, 256)
-    both = jnp.pad(both, ((0, 0), (0, 2), (0, 0)))
-    chunks = []
-    for there in range(half):
-        ahead = at_z - there
-        first = (jnp.abs(ahead) < half // 2) | (ahead == -(half // 2))
-        chunks.append(turned(both, ~first))
-    groups = [list(range(half)), list(range(half, nz))]
-    recv = lax.all_to_all(jnp.stack(chunks), "gz", 0, 0, axis_index_groups=groups)
-    return at_z.astype(jnp.int32).reshape(1), recv
+    before = lax.ppermute(own[:, 7:8], "gy", along("gy", 1))
+    after = lax.ppermute(own[:, 0:1], "gy", along("gy", -1))
+    own = jnp.concatenate([before, own, after], axis=1)
+    before = lax.ppermute(own[..., 64:], "gx", along("gx", 1))
+    after = lax.ppermute(own[..., :64], "gx", along("gx", -1))
+    own = jnp.concatenate([before, own, after], axis=2).reshape(30, 256)
+    own = jnp.pad(own, ((0, 2), (0, 0)))
+    recv = lax.all_to_all(jnp.broadcast_to(own, (nz, 32, 256)), "gz", 0, 0)
+    return lax.axis_index("gz").astype(jnp.int32).reshape(1), recv
 
 
 def body(positions, counts):
     force, energy = local_step(*gathered(positions, counts))
-    force = jnp.swapaxes(force.reshape(3, 8, 2, 64), 1, 2)[:, None]
-    energy = jnp.swapaxes(energy.reshape(8, 2, 64), 0, 1)[None]
-    return force, energy
+    return force[:, None], energy[None]
 
 
 def solution(mesh):

time: 94.9 us -> 89 us (0.938)
  the two profiles are of different devices: /device:TPU:122 before, /device:TPU:20 now
where the time goes in v3:
time: 89 us; the launch traced here: 88.6 us
  Pallas kernels  34.3 us (39%)
  starting transfers between devices  25.4 us (29%)
  waiting for transfers between devices  24.7 us (28%)
  local copies, waits for them, and re-layouts  2.46 us (3%)
  between operations  0.92 us (1%)
    pallas_call x1, Pallas kernels, local_step(): pl.pallas_call(kernel, out_shape=(jax.ShapeDtypeStruct((3, 2, 8, SLOTS),...  34.3 us
    all_to_all x1, waiting for transfers between devices, gathered(): recv = lax.all_to_all(jnp.broadcast_to(own, (nz, 32, 256)), 'gz', 0, 0)  20.5 us
    all_to_all x1, starting transfers between devices, gathered(): recv = lax.all_to_all(jnp.broadcast_to(own, (nz, 32, 256)), 'gz', 0, 0)  14 us
    ppermute x1, starting transfers between devices, gathered(): after = lax.ppermute(own[:, 0:1], 'gy', along('gy', -1))  3.64 us
    ppermute x1, starting transfers between devices, gathered(): before = lax.ppermute(own[..., 64:], 'gx', along('gx', 1))  3.1 us
    ppermute x1, waiting for transfers between devices, gathered(): after = lax.ppermute(own[..., :64], 'gx', along('gx', -1))  2.97 us
    ppermute x1, starting transfers between devices, gathered(): after = lax.ppermute(own[..., :64], 'gx', along('gx', -1))  2.74 us
    ppermute x1, starting transfers between devices, gathered(): before = lax.ppermute(own[:, 7:8], 'gy', along('gy', 1))  1.91 us
  transfers between devices with their start and end apart: 5, of which 3 were waited for; matrix products, arithmetic and copies ran while one was open for 0% of the time, Pallas kernels for 0%

profile of v3, /device:TPU:20, one launch (start us, length us, event | category | flops | bytes accessed | tf_op | source)
XLA Modules:
  0.0 88.6 jit_solution(13586418300477464284)
XLA Ops:
  0.6 0.7 slice_bitcast_fusion.1
  1.3 0.0 copy-start.5
  1.4 0.7 copy-done.5
  2.0 0.8 bitcast_select_fusion
  2.8 0.1 reshape.31
  2.9 1.9 %collective-permute-start = (f32[3,1,128]{2,1,0:T(1,128)S(1)}, f32[3,1,128]{2,1,0:T(1,128)S(1)}, u32[]{:S(2)}, u32[]{:S(2)}) collective-permute-start(f32[3,1,128]{2,1,0:T(1,128)S(1)} %get-tuple-element.14), channel_id=1, source_target_pairs={{0,16},{16,32},{32,48},{48,64},{64,80},{80,96},{96,112},{112,0},{1... | collective-permute-start | bytes 4616 | tf_op jit(solution)/shard_map/ppermute | solution.py:420
  4.8 3.6 %collective-permute-start.1 = (f32[3,1,128]{2,1,0:T(1,128)S(1)}, f32[3,1,128]{2,1,0:T(1,128)S(1)}, u32[]{:S(2)}, u32[]{:S(2)}) collective-permute-start(f32[3,1,128]{2,1,0:T(1,128)S(1)} %get-tuple-element.15), channel_id=1, source_target_pairs={{0,112},{16,0},{32,16},{48,32},{64,48},{80,64},{96,80},{112,96},{1... | collective-permute-start | bytes 4616 | tf_op jit(solution)/shard_map/ppermute | solution.py:421
  8.5 0.0 collective-permute-done
  8.5 1.3 %collective-permute-done.1 = f32[3,1,128]{2,1,0:T(1,128)S(1)} collective-permute-done((f32[3,1,128]{2,1,0:T(1,128)S(1)}, f32[3,1,128]{2,1,0:T(1,128)S(1)}, u32[]{:S(2)}, u32[]{:S(2)}) %collective-permute-start.1) | collective-permute-done | bytes 1568 | tf_op jit(solution)/shard_map/ppermute | solution.py:421
  9.8 0.1 fusion
  9.9 3.1 %collective-permute-start.2 = (f32[3,10,64]{2,1,0:T(8,128)S(1)}, f32[3,10,64]{2,1,0:T(8,128)S(1)}, u32[]{:S(2)}, u32[]{:S(2)}) collective-permute-start(f32[3,10,64]{2,1,0:T(8,128)S(1)} %get-tuple-element.10), channel_id=1, source_target_pairs={{0,128},{128,256},{256,384},{384,0},{1,129},{129,257},{257,385},{3... | collective-permute-start | bytes 23048 | tf_op jit(solution)/shard_map/ppermute | solution.py:423
  13.0 2.7 %collective-permute-start.3 = (f32[3,10,64]{2,1,0:T(8,128)S(1)}, f32[3,10,64]{2,1,0:T(8,128)S(1)}, u32[]{:S(2)}, u32[]{:S(2)}) collective-permute-start(f32[3,10,64]{2,1,0:T(8,128)S(1)} %get-tuple-element.11), channel_id=1, source_target_pairs={{0,384},{128,0},{256,128},{384,256},{1,385},{129,1},{257,129},{385... | collective-permute-start | bytes 23048 | tf_op jit(solution)/shard_map/ppermute | solution.py:424
  15.7 0.0 collective-permute-done.2
  15.7 3.0 %collective-permute-done.3 = f32[3,10,64]{2,1,0:T(8,128)S(1)} collective-permute-done((f32[3,10,64]{2,1,0:T(8,128)S(1)}, f32[3,10,64]{2,1,0:T(8,128)S(1)}, u32[]{:S(2)}, u32[]{:S(2)}) %collective-permute-start.3) | collective-permute-done | bytes 7712 | tf_op jit(solution)/shard_map/ppermute | solution.py:424
  18.7 0.1 pad_maximum_fusion
  18.8 0.0 copy-start.3
  18.8 0.0 copy-start.4
  18.8 0.8 broadcast_in_dim.15
  19.7 0.0 copy-start
  19.7 0.0 copy-start.1
  19.7 0.0 copy-start.2
  19.7 14.0 %all-to-all-start = ((f32[16,32,256]{2,1,0:T(8,128)}), f32[16,32,256]{2,1,0:T(8,128)S(1)}, u32[]{:S(2)}, u32[]{:S(2)}) async-start(f32[16,32,256]{2,1,0:T(8,128)} %broadcast_in_dim.15), calls=%async_computation | async-start | bytes 1048576 | tf_op jit(solution)/shard_map/all_to_all | solution.py:427
  33.7 20.5 %all-to-all-done.recv = f32[16,32,256]{2,1,0:T(8,128)S(1)} async-done(((f32[16,32,256]{2,1,0:T(8,128)}), f32[16,32,256]{2,1,0:T(8,128)S(1)}, u32[]{:S(2)}, u32[]{:S(2)}) %all-to-all-start) | async-done | bytes 524320 | tf_op jit(solution)/shard_map/all_to_all | solution.py:427
  54.2 0.0 copy-done.3
  54.2 0.0 copy-done.4
  54.2 0.0 copy-done
  54.2 0.0 copy-done.1
  54.2 0.0 copy-done.2
  54.2 34.3 %shard_map.86 = (f32[3,2,8,64]{3,2,1,0:T(8,128)}, f32[2,8,64]{2,1,0:T(8,128)}) custom-call(s32[1]{0:T(128)} %bitcast.at_z, f32[16,32,256]{2,1,0:T(8,128)S(1)} %all-to-all-done.recv, bf16[208,1280]{1,0:T(8,128)(2,1)S(1)} %copy-done, bf16[320,208]{1,0:T(8,128)(2,1)S(1)} %copy-done.2, bf16[256,256]{1,0:T(8,128)(2,1)S(1)} %copy-done.3, ...), custom_call_target="tpu_custom_call" | custom-call | tf_op jit(solution)/shard_map/pallas_call | solution.py:376
  (6 shorter events, 0.1 us)
Async XLA Ops:
  1.3 0.7 copy-start.5
  2.9 5.6 %collective-permute-start = (f32[3,1,128]{2,1,0:T(1,128)S(1)}, f32[3,1,128]{2,1,0:T(1,128)S(1)}, u32[]{:S(2)}, u32[]{:S(2)}) collective-permute-start(f32[3,1,128]{2,1,0:T(1,128)S(1)} %get-tuple-element.14), channel_id=1, source_target_pairs={{0,16},{16,32},{32,48},{48,64},{64,80},{80,96},{96,112},{112,0},{1... | collective-permute-start | bytes 4616 | tf_op jit(solution)/shard_map/ppermute | solution.py:420
  4.8 4.9 %collective-permute-start.1 = (f32[3,1,128]{2,1,0:T(1,128)S(1)}, f32[3,1,128]{2,1,0:T(1,128)S(1)}, u32[]{:S(2)}, u32[]{:S(2)}) collective-permute-start(f32[3,1,128]{2,1,0:T(1,128)S(1)} %get-tuple-element.15), channel_id=1, source_target_pairs={{0,112},{16,0},{32,16},{48,32},{64,48},{80,64},{96,80},{112,96},{1... | collective-permute-start | bytes 4616 | tf_op jit(solution)/shard_map/ppermute | solution.py:421
  9.9 5.9 %collective-permute-start.2 = (f32[3,10,64]{2,1,0:T(8,128)S(1)}, f32[3,10,64]{2,1,0:T(8,128)S(1)}, u32[]{:S(2)}, u32[]{:S(2)}) collective-permute-start(f32[3,10,64]{2,1,0:T(8,128)S(1)} %get-tuple-element.10), channel_id=1, source_target_pairs={{0,128},{128,256},{256,384},{384,0},{1,129},{129,257},{257,385},{3... | collective-permute-start | bytes 23048 | tf_op jit(solution)/shard_map/ppermute | solution.py:423
  13.0 5.7 %collective-permute-start.3 = (f32[3,10,64]{2,1,0:T(8,128)S(1)}, f32[3,10,64]{2,1,0:T(8,128)S(1)}, u32[]{:S(2)}, u32[]{:S(2)}) collective-permute-start(f32[3,10,64]{2,1,0:T(8,128)S(1)} %get-tuple-element.11), channel_id=1, source_target_pairs={{0,384},{128,0},{256,128},{384,256},{1,385},{129,1},{257,129},{385... | collective-permute-start | bytes 23048 | tf_op jit(solution)/shard_map/ppermute | solution.py:424
  18.8 35.4 %copy-start.3 = (bf16[256,256]{1,0:T(8,128)(2,1)S(1)}, bf16[256,256]{1,0:T(8,128)(2,1)}, u32[]{:S(2)}) copy-start(bf16[256,256]{1,0:T(8,128)(2,1)} %constant.21.clone.eye) | copy-start | bytes 393220
  18.8 35.3 %copy-start.4 = (bf16[256,256]{1,0:T(8,128)(2,1)S(1)}, bf16[256,256]{1,0:T(8,128)(2,1)}, u32[]{:S(2)}) copy-start(bf16[256,256]{1,0:T(8,128)(2,1)} %constant.22.clone.upto) | copy-start | bytes 393220
  19.7 34.5 %copy-start = (bf16[208,1280]{1,0:T(8,128)(2,1)S(1)}, bf16[208,1280]{1,0:T(8,128)(2,1)}, u32[]{:S(2)}) copy-start(bf16[208,1280]{1,0:T(8,128)(2,1)} %constant.19.clone.place_b) | copy-start | bytes 1597444
  19.7 34.5 %copy-start.1 = (bf16[896,32]{1,0:T(8,128)(2,1)S(1)}, bf16[896,32]{1,0:T(8,128)(2,1)}, u32[]{:S(2)}) copy-start(bf16[896,32]{1,0:T(8,128)(2,1)} %constant.23.clone.outside) | copy-start | bytes 172036
  19.7 34.5 %copy-start.2 = (bf16[320,208]{1,0:T(8,128)(2,1)S(1)}, bf16[320,208]{1,0:T(8,128)(2,1)}, u32[]{:S(2)}) copy-start(bf16[320,208]{1,0:T(8,128)(2,1)} %constant.20.clone.sel_a) | copy-start | bytes 399364
  19.7 34.5 %all-to-all-start = ((f32[16,32,256]{2,1,0:T(8,128)}), f32[16,32,256]{2,1,0:T(8,128)S(1)}, u32[]{:S(2)}, u32[]{:S(2)}) async-start(f32[16,32,256]{2,1,0:T(8,128)} %broadcast_in_dim.15), calls=%async_computation | async-start | bytes 1048576 | tf_op jit(solution)/shard_map/all_to_all | solution.py:427

commit v4 on v3

--- a/solution.py
+++ b/solution.py
@@ -21,9 +21,9 @@
 RATIO = 8.0 / 3.0
 DENSITY = 2.0 ** (-TOP) / TOP**2
 PAIR = 2.0 ** (-TOP * RATIO)
-SLOPE = 2.0 * 2.0 ** (-TOP) / TOP
-G1, G2 = 2.0 / cutoff_sq, 1.0 / (8.0 * TOP)
-H1, H2 = 4.0 * PAIR / TOP * 2.0 / cutoff_sq, 4.0 * PAIR / (3.0 * TOP * TOP)
+G, H = 8.0 * 2.0 * TOP / cutoff_sq, 3.0 * 2.0 * TOP / cutoff_sq
+FORCE = 4.0 * PAIR / (3.0 * TOP * TOP) / UNIT
+SLOPE = 2.0 * 2.0 ** (-TOP) / (8.0 * TOP * TOP) / (FORCE * UNIT)
 PHI = 2.0 * PAIR / TOP**2
 
 NY = 10
@@ -31,7 +31,7 @@
 LAYERS, MIDDLE = 9, 5
 TERMS = 32
 DEPTH = 13 * TILE
-WINDOW, EDGE, EXTRA = 768, 512, 128
+WINDOW, EDGE, EXTRA = 704, 512, 128
 STEP = 16
 CAPACITY = LAYERS * 256 + WINDOW + EXTRA
 EMPTY = FAR * side_xy * UNIT
@@ -79,6 +79,7 @@
         cast(np.eye(256, dtype=np.float32)),
         cast((lane[:, None] <= lane[None, :]).astype(np.float32)),
         cast(outside),
+        cast((np.arange(512)[:, None] // 128 == lane[None, :128]).astype(np.float32)),
     )
 
 
@@ -93,16 +94,6 @@
 def pieces(x, y, z):
     parts = split3(x) + split3(y) + split3(z) + split3(x * x + y * y + z * z)
     return jnp.concatenate(parts + (jnp.ones((TILE, x.shape[1]), bf16),), axis=0)
-
-
-def lanes_summed(rows):
-    ones = jnp.ones((8, rows.shape[1]), bf16)
-    total = jnp.zeros((8, rows.shape[0]), f32)
-    for part in split3(rows):
-        total = total + lax.dot_general(
-            ones, part, (((1,), (1,)), ((), ())), preferred_element_type=f32
-        )
-    return total
 
 
 def across(x, index):
@@ -141,14 +132,13 @@
     (xp, yp, zp, sp), (xq, yq, zq, sq), (fx, fy, fz, ph) = centre, partner, sums
     dx, dy, dz = xp - xq, yp - yq, zp - zq
     tau = jnp.maximum(TOP - (dx * dx + dy * dy + dz * dz), 0.0)
-    u = jnp.exp2(tau) * tau
     w = jnp.exp2(tau * RATIO) * tau
-    push = (sp + sq) * (u * (G1 + G2 * tau)) + w * (H1 + H2 * tau)
+    push = (sp + sq) * (jnp.exp2(tau) * tau * (tau + G)) + w * (tau + H)
     return fx + push * dx, fy + push * dy, fz + push * dz, ph + w * tau
 
 
 def kernel(
-    at_z, recv, place_b, sel_a, eye, upto, outside, force, energy,
+    at_z, recv, place_b, sel_a, eye, upto, outside, add_up, force, energy,
     COUNT, MASK, CUM, NUMS, OFF, XYZ, TURNED, P, C, D, SLOPE_D, ROOT_D, OWN, LATE, COL, SUM, RES, sem,
 ):
     SLOPE_D[...] = jnp.ones(SLOPE_D.shape, f32)
@@ -184,13 +174,15 @@
     for l in range(MIDDLE):
         count = CUM[TILE * (l + 9) : TILE * (l + 10)]
         fields = [XYZ[l + 2, c] for c in range(3)]
-        groups = [packed(count, fields, w) for w in range(2)]
+        lists = [packed(count, fields, w) for w in range(2)]
         for w in range(2):
             for c in range(3):
-                D[l, c, w] = groups[w][c]
-            terms = jnp.dot(sel_a[...], pieces(*groups[w]), preferred_element_type=f32).astype(bf16)
-            for j in range(NY):
-                C[l, j, w] = terms[TERMS * j : TERMS * (j + 1)]
+                D[l, c, w] = lists[w][c]
+        both = jnp.concatenate([pieces(*lists[w]) for w in range(2)], axis=1)
+        terms = jnp.dot(sel_a[...], both, preferred_element_type=f32).astype(bf16)
+        for j in range(NY):
+            for w in range(2):
+                C[l, j, w] = terms[TERMS * j : TERMS * (j + 1), 128 * w : 128 * (w + 1)]
     copy.wait()
 
     for j in range(NY + 2):
@@ -332,7 +324,7 @@
             late = tuple(LATE[c, pl.ds(j + 1, 1), :] for c in range(4))
             sums = push_parts(mine, late, sums)
             for i in range(4):
-                SUM[j, i, rows, :] = sums[i]
+                SUM[j, rows, 128 * i : 128 * (i + 1)] = sums[i]
 
     @pl.when(crowded)
     def _():
@@ -340,19 +332,25 @@
         def _(l):
             @pl.loop(0, NY)
             def _(k):
+                some = jnp.where(NUMS[0, TILE * (l + 9) + k] > 128, 1, 0)
+
                 @pl.loop(jnp.maximum(k - 2, 0), jnp.minimum(k + 1, 8))
                 def _(j):
-                    @pl.loop(0, steps(j))
+                    @pl.loop(0, steps(j) * some)
                     def _(g):
                         rows = pl.ds(pl.multiple_of(g * STEP, STEP), STEP)
-                        sums = tuple(SUM[j, i, rows, :] for i in range(4))
+                        sums = tuple(SUM[j, rows, 128 * i : 128 * (i + 1)] for i in range(4))
                         sums = push_parts(centre(j, rows), partner(l, k, 1), sums)
                         for i in range(4):
-                            SUM[j, i, rows, :] = sums[i]
-
+                            SUM[j, rows, 128 * i : 128 * (i + 1)] = sums[i]
+
+    total = jnp.zeros((8 * 128, 128), f32)
+    for part in split3(SUM[...].reshape(8 * 128, 4 * 128))[:2]:
+        total = total + jnp.dot(part, add_up[...], preferred_element_type=f32)
     for j in range(8):
+        across_lanes = total[128 * j : 128 * (j + 1), 0:8].T
         for i in range(4):
-            RES[i, j : j + 1, :] = lanes_summed(SUM[j, i])[0:1]
+            RES[i, j : j + 1, :] = across_lanes[i : i + 1]
 
     back = pltpu.roll(count, 256 - SLOTS, 1)[:, :128].astype(jnp.int32) - 1 - before
     back = jnp.concatenate([pltpu.roll(back, TILE - 1, 0)[0:8]], axis=0)
@@ -360,7 +358,7 @@
     occupied = pltpu.roll(occupied, TILE - 1, 0)[0:8] < 0.5 * EMPTY
     back = jnp.where(occupied, back, 0)
     root = pltpu.roll(OWN[4], TILE - 1, 0)[0:8]
-    values = [RES[i] * (1.0 / UNIT) for i in range(3)] + [RES[3] * (0.5 * PHI) - 1.0 - root]
+    values = [RES[i] * FORCE for i in range(3)] + [RES[3] * (0.5 * PHI) - 1.0 - root]
     for i, value in enumerate(values):
         value = jnp.where(occupied, across(value, back), 0.0)
         for half, part in enumerate((value, pltpu.roll(value, SLOTS, 1))):
@@ -379,7 +377,7 @@
             jax.ShapeDtypeStruct((3, 2, 8, SLOTS), f32),
             jax.ShapeDtypeStruct((2, 8, SLOTS), f32),
         ),
-        in_specs=[pl.BlockSpec(memory_space=pltpu.SMEM)] + [vmem] * 6,
+        in_specs=[pl.BlockSpec(memory_space=pltpu.SMEM)] + [vmem] * 7,
         out_specs=(vmem, vmem),
         scratch_shapes=[
             pltpu.VMEM((8, 256), jnp.int32),
@@ -397,7 +395,7 @@
             pltpu.VMEM((5, TILE, 128), f32),
             pltpu.VMEM((4, TILE, 128), f32),
             pltpu.VMEM((8, 128, 128), f32),
-            pltpu.VMEM((8, 4, 128, 128), f32),
+            pltpu.VMEM((8, 128, 512), f32),
             pltpu.VMEM((4, 8, 128), f32),
             pltpu.SemaphoreType.DMA,
         ],
@@ -411,14 +409,35 @@
     return [(i, (i + distance) % n) for i in range(n)]
 
 
+def marking_kernel(counts, positions, own, up, down):
+    lane = lax.broadcasted_iota(jnp.int32, (1, SLOTS), 1)
+    for i in range(2):
+        lanes = slice(SLOTS * i, SLOTS * (i + 1))
+        for j in range(8):
+            row = jnp.where(lane < counts[0, i, j], positions[0, 0, i, j : j + 1, :], FAR)
+            own[0, j : j + 1, lanes] = row
+        for c in (1, 2):
+            own[c, :, lanes] = positions[c, 0, i]
+    for c in range(3):
+        up[c] = own[c, 7:8]
+        down[c] = own[c, 0:1]
+
+
+def marked(positions, counts):
+    vmem = pl.BlockSpec(memory_space=pltpu.VMEM)
+    return pl.pallas_call(
+        marking_kernel,
+        out_shape=tuple(jax.ShapeDtypeStruct((3, n, 128), f32) for n in (8, 1, 1)),
+        in_specs=[pl.BlockSpec(memory_space=pltpu.SMEM), vmem],
+        out_specs=(vmem,) * 3,
+    )(counts, positions)
+
+
 def gathered(positions, counts):
     nz = lax.axis_size("gz")
-    empty = jnp.arange(SLOTS) >= counts[0][..., None]
-    x = jnp.where(empty, FAR, positions[0, 0])
-    own = jnp.stack([x, positions[1, 0], positions[2, 0]])
-    own = jnp.swapaxes(own, 1, 2).reshape(3, 8, 128)
-    before = lax.ppermute(own[:, 7:8], "gy", along("gy", 1))
-    after = lax.ppermute(own[:, 0:1], "gy", along("gy", -1))
+    own, up, down = marked(positions, counts)
+    before = lax.ppermute(up, "gy", along("gy", 1))
+    after = lax.ppermute(down, "gy", along("gy", -1))
     own = jnp.concatenate([before, own, after], axis=1)
     before = lax.ppermute(own[..., 64:], "gx", along("gx", 1))
     after = lax.ppermute(own[..., :64], "gx", along("gx", -1))

time: 89 us -> 89 us (level)
  the two profiles are of different devices: /device:TPU:20 before, /device:TPU:64 now
where the time goes in v4:
time: 89 us; the launch traced here: 88.6 us
  Pallas kernels  38.1 us (43%)
  starting transfers between devices  29.9 us (34%)
  waiting for transfers between devices  18 us (20%)
  local copies, waits for them, and re-layouts  0.97 us (1%)
    pallas_call x1, Pallas kernels, local_step(): pl.pallas_call(kernel, out_shape=(jax.ShapeDtypeStruct((3, 2, 8, SLOTS),...  36.7 us
    all_to_all x1, starting transfers between devices, gathered(): recv = lax.all_to_all(jnp.broadcast_to(own, (nz, 32, 256)), 'gz', 0, 0)  15.4 us
    all_to_all x1, waiting for transfers between devices, gathered(): recv = lax.all_to_all(jnp.broadcast_to(own, (nz, 32, 256)), 'gz', 0, 0)  14.7 us
    ppermute x1, starting transfers between devices, gathered(): after = lax.ppermute(down, 'gy', along('gy', -1))  5.44 us
    ppermute x1, starting transfers between devices, gathered(): after = lax.ppermute(own[..., :64], 'gx', along('gx', -1))  3.65 us
    ppermute x1, starting transfers between devices, gathered(): before = lax.ppermute(own[..., 64:], 'gx', along('gx', 1))  3.39 us
    ppermute x1, waiting for transfers between devices, gathered(): after = lax.ppermute(own[..., :64], 'gx', along('gx', -1))  2.05 us
    ppermute x1, starting transfers between devices, gathered(): before = lax.ppermute(up, 'gy', along('gy', 1))  2.04 us
  transfers between devices with their start and end apart: 5, of which 3 were waited for; matrix products, arithmetic and copies ran while one was open for 0% of the time, Pallas kernels for 0%

profile of v4, /device:TPU:64, one launch (start us, length us, event | category | flops | bytes accessed | tf_op | source)
XLA Modules:
  0.0 88.6 jit_solution(11826578145882540856)
XLA Ops:
  0.6 1.4 %shard_map.95 = (f32[3,8,128]{2,1,0:T(8,128)}, f32[3,1,128]{2,1,0:T(1,128)}, f32[3,1,128]{2,1,0:T(1,128)}) custom-call(s32[1,2,8]{2,1,0:T(2,128)} %counts.1, f32[3,1,2,8,64]{4,3,2,1,0:T(8,128)} %positions.1), custom_call_target="tpu_custom_call" | custom-call | tf_op jit(solution)/shard_map/pallas_call | solution.py:428
  2.1 0.0 copy-start.7
  2.1 2.0 %collective-permute-start = (f32[3,1,128]{2,1,0:T(1,128)}, f32[3,1,128]{2,1,0:T(1,128)S(1)}, u32[]{:S(2)}, u32[]{:S(2)}) collective-permute-start(f32[3,1,128]{2,1,0:T(1,128)} %get-tuple-element.7), channel_id=1, source_target_pairs={{0,16},{16,32},{32,48},{48,64},{64,80},{80,96},{96,112},{112,0},{1... | collective-permute-start | bytes 4616 | tf_op jit(solution)/shard_map/ppermute | solution.py:439
  4.1 0.0 copy-done.7
  4.1 5.4 %collective-permute-start.1 = (f32[3,1,128]{2,1,0:T(1,128)S(1)}, f32[3,1,128]{2,1,0:T(1,128)S(1)}, u32[]{:S(2)}, u32[]{:S(2)}) collective-permute-start(f32[3,1,128]{2,1,0:T(1,128)S(1)} %copy-done.7), channel_id=1, source_target_pairs={{0,112},{16,0},{32,16},{48,32},{64,48},{80,64},{96,80},{112,96},{1... | collective-permute-start | bytes 4616 | tf_op jit(solution)/shard_map/ppermute | solution.py:440
  9.6 0.0 collective-permute-done
  9.6 1.3 %collective-permute-done.1 = f32[3,1,128]{2,1,0:T(1,128)S(1)} collective-permute-done((f32[3,1,128]{2,1,0:T(1,128)S(1)}, f32[3,1,128]{2,1,0:T(1,128)S(1)}, u32[]{:S(2)}, u32[]{:S(2)}) %collective-permute-start.1) | collective-permute-done | bytes 1568 | tf_op jit(solution)/shard_map/ppermute | solution.py:440
  10.9 0.7 pad_maximum_fusion.1
  11.6 0.0 copy-start.6
  11.6 0.1 fusion
  11.7 3.4 %collective-permute-start.2 = (f32[3,10,64]{2,1,0:T(8,128)S(1)}, f32[3,10,64]{2,1,0:T(8,128)S(1)}, u32[]{:S(2)}, u32[]{:S(2)}) collective-permute-start(f32[3,10,64]{2,1,0:T(8,128)S(1)} %get-tuple-element.16), channel_id=1, source_target_pairs={{0,128},{128,256},{256,384},{384,0},{1,129},{129,257},{257,385},{3... | collective-permute-start | bytes 23048 | tf_op jit(solution)/shard_map/ppermute | solution.py:442
  15.1 3.7 %collective-permute-start.3 = (f32[3,10,64]{2,1,0:T(8,128)S(1)}, f32[3,10,64]{2,1,0:T(8,128)S(1)}, u32[]{:S(2)}, u32[]{:S(2)}) collective-permute-start(f32[3,10,64]{2,1,0:T(8,128)S(1)} %get-tuple-element.17), channel_id=1, source_target_pairs={{0,384},{128,0},{256,128},{384,256},{1,385},{129,1},{257,129},{385... | collective-permute-start | bytes 23048 | tf_op jit(solution)/shard_map/ppermute | solution.py:443
  18.7 0.0 collective-permute-done.2
  18.7 2.0 %collective-permute-done.3 = f32[3,10,64]{2,1,0:T(8,128)S(1)} collective-permute-done((f32[3,10,64]{2,1,0:T(8,128)S(1)}, f32[3,10,64]{2,1,0:T(8,128)S(1)}, u32[]{:S(2)}, u32[]{:S(2)}) %collective-permute-start.3) | collective-permute-done | bytes 7712 | tf_op jit(solution)/shard_map/ppermute | solution.py:443
  20.8 0.0 copy-done.6
  20.8 0.1 pad_maximum_fusion
  20.9 0.0 copy-start.4
  20.9 0.0 copy-start.5
  20.9 0.8 broadcast_in_dim.9
  21.8 0.0 copy-start
  21.8 0.0 copy-start.1
  21.8 0.0 copy-start.2
  21.8 0.0 copy-start.3
  21.8 15.4 %all-to-all-start = ((f32[16,32,256]{2,1,0:T(8,128)}), f32[16,32,256]{2,1,0:T(8,128)S(1)}, u32[]{:S(2)}, u32[]{:S(2)}) async-start(f32[16,32,256]{2,1,0:T(8,128)} %broadcast_in_dim.9), calls=%async_computation | async-start | bytes 1048576 | tf_op jit(solution)/shard_map/all_to_all | solution.py:446
  37.2 14.7 %all-to-all-done.recv = f32[16,32,256]{2,1,0:T(8,128)S(1)} async-done(((f32[16,32,256]{2,1,0:T(8,128)}), f32[16,32,256]{2,1,0:T(8,128)S(1)}, u32[]{:S(2)}, u32[]{:S(2)}) %all-to-all-start) | async-done | bytes 524320 | tf_op jit(solution)/shard_map/all_to_all | solution.py:446
  51.8 0.0 copy-done.4
  51.9 0.0 copy-done.5
  51.9 0.0 copy-done
  51.9 0.0 copy-done.1
  51.9 0.0 copy-done.2
  51.9 0.0 copy-done.3
  51.9 36.7 %shard_map.96 = (f32[3,2,8,64]{3,2,1,0:T(8,128)}, f32[2,8,64]{2,1,0:T(8,128)}) custom-call(s32[1]{0:T(128)} %bitcast.at_z, f32[16,32,256]{2,1,0:T(8,128)S(1)} %all-to-all-done.recv, bf16[208,1280]{1,0:T(8,128)(2,1)S(1)} %copy-done, bf16[320,208]{1,0:T(8,128)(2,1)S(1)} %copy-done.2, bf16[256,256]{1,0:T(8,128)(2,1)S(1)} %copy-done.3, ...), custom_call_target="tpu_custom_call" | custom-call | tf_op jit(solution)/shard_map/pallas_call | solution.py:374
  (2 shorter events, 0.0 us)
Async XLA Ops:
  2.1 2.1 %copy-start.7 = (f32[3,1,128]{2,1,0:T(1,128)S(1)}, f32[3,1,128]{2,1,0:T(1,128)}, u32[]{:S(2)}) copy-start(f32[3,1,128]{2,1,0:T(1,128)} %get-tuple-element.9) | copy-start | bytes 4612
  2.1 7.5 %collective-permute-start = (f32[3,1,128]{2,1,0:T(1,128)}, f32[3,1,128]{2,1,0:T(1,128)S(1)}, u32[]{:S(2)}, u32[]{:S(2)}) collective-permute-start(f32[3,1,128]{2,1,0:T(1,128)} %get-tuple-element.7), channel_id=1, source_target_pairs={{0,16},{16,32},{32,48},{48,64},{64,80},{80,96},{96,112},{112,0},{1... | collective-permute-start | bytes 4616 | tf_op jit(solution)/shard_map/ppermute | solution.py:439
  4.1 6.7 %collective-permute-start.1 = (f32[3,1,128]{2,1,0:T(1,128)S(1)}, f32[3,1,128]{2,1,0:T(1,128)S(1)}, u32[]{:S(2)}, u32[]{:S(2)}) collective-permute-start(f32[3,1,128]{2,1,0:T(1,128)S(1)} %copy-done.7), channel_id=1, source_target_pairs={{0,112},{16,0},{32,16},{48,32},{64,48},{80,64},{96,80},{112,96},{1... | collective-permute-start | bytes 4616 | tf_op jit(solution)/shard_map/ppermute | solution.py:440
  11.6 9.2 %copy-start.6 = (f32[3,8,128]{2,1,0:T(8,128)S(1)}, f32[3,8,128]{2,1,0:T(8,128)}, u32[]{:S(2)}) copy-start(f32[3,8,128]{2,1,0:T(8,128)} %get-tuple-element.8) | copy-start | bytes 36868
  11.7 7.1 %collective-permute-start.2 = (f32[3,10,64]{2,1,0:T(8,128)S(1)}, f32[3,10,64]{2,1,0:T(8,128)S(1)}, u32[]{:S(2)}, u32[]{:S(2)}) collective-permute-start(f32[3,10,64]{2,1,0:T(8,128)S(1)} %get-tuple-element.16), channel_id=1, source_target_pairs={{0,128},{128,256},{256,384},{384,0},{1,129},{129,257},{257,385},{3... | collective-permute-start | bytes 23048 | tf_op jit(solution)/shard_map/ppermute | solution.py:442
  15.1 5.7 %collective-permute-start.3 = (f32[3,10,64]{2,1,0:T(8,128)S(1)}, f32[3,10,64]{2,1,0:T(8,128)S(1)}, u32[]{:S(2)}, u32[]{:S(2)}) collective-permute-start(f32[3,10,64]{2,1,0:T(8,128)S(1)} %get-tuple-element.17), channel_id=1, source_target_pairs={{0,384},{128,0},{256,128},{384,256},{1,385},{129,1},{257,129},{385... | collective-permute-start | bytes 23048 | tf_op jit(solution)/shard_map/ppermute | solution.py:443
  20.9 30.9 %copy-start.4 = (bf16[256,256]{1,0:T(8,128)(2,1)S(1)}, bf16[256,256]{1,0:T(8,128)(2,1)}, u32[]{:S(2)}) copy-start(bf16[256,256]{1,0:T(8,128)(2,1)} %constant.22.clone.upto) | copy-start | bytes 393220
  20.9 30.9 %copy-start.5 = (bf16[512,128]{1,0:T(8,128)(2,1)S(1)}, bf16[512,128]{1,0:T(8,128)(2,1)}, u32[]{:S(2)}) copy-start(bf16[512,128]{1,0:T(8,128)(2,1)} %constant.24.clone.add_up) | copy-start | bytes 393220
  21.8 30.1 %copy-start = (bf16[208,1280]{1,0:T(8,128)(2,1)S(1)}, bf16[208,1280]{1,0:T(8,128)(2,1)}, u32[]{:S(2)}) copy-start(bf16[208,1280]{1,0:T(8,128)(2,1)} %constant.19.clone.place_b) | copy-start | bytes 1597444
  21.8 30.1 %copy-start.1 = (bf16[832,32]{1,0:T(8,128)(2,1)S(1)}, bf16[832,32]{1,0:T(8,128)(2,1)}, u32[]{:S(2)}) copy-start(bf16[832,32]{1,0:T(8,128)(2,1)} %constant.23.clone.outside) | copy-start | bytes 159748
  21.8 30.1 %copy-start.2 = (bf16[320,208]{1,0:T(8,128)(2,1)S(1)}, bf16[320,208]{1,0:T(8,128)(2,1)}, u32[]{:S(2)}) copy-start(bf16[320,208]{1,0:T(8,128)(2,1)} %constant.20.clone.sel_a) | copy-start | bytes 399364
  21.8 30.1 %copy-start.3 = (bf16[256,256]{1,0:T(8,128)(2,1)S(1)}, bf16[256,256]{1,0:T(8,128)(2,1)}, u32[]{:S(2)}) copy-start(bf16[256,256]{1,0:T(8,128)(2,1)} %constant.21.clone.eye) | copy-start | bytes 393220
  21.8 30.1 %all-to-all-start = ((f32[16,32,256]{2,1,0:T(8,128)}), f32[16,32,256]{2,1,0:T(8,128)S(1)}, u32[]{:S(2)}, u32[]{:S(2)}) async-start(f32[16,32,256]{2,1,0:T(8,128)} %broadcast_in_dim.9), calls=%async_computation | async-start | bytes 1048576 | tf_op jit(solution)/shard_map/all_to_all | solution.py:446

commit v5 on v4

--- a/solution.py
+++ b/solution.py
@@ -31,7 +31,7 @@
 LAYERS, MIDDLE = 9, 5
 TERMS = 32
 DEPTH = 13 * TILE
-WINDOW, EDGE, EXTRA = 704, 512, 128
+WINDOW, EDGE, EXTRA = 768, 576, 128
 STEP = 16
 CAPACITY = LAYERS * 256 + WINDOW + EXTRA
 EMPTY = FAR * side_xy * UNIT

time: 89 us -> 86.6 us (0.973)
  the two profiles are of different devices: /device:TPU:64 before, /device:TPU:18 now
where the time goes in v5:
time: 86.6 us; the launch traced here: 86.1 us
  Pallas kernels  32.9 us (38%)
  starting transfers between devices  25.5 us (29%)
  waiting for transfers between devices  25 us (29%)
  local copies, waits for them, and re-layouts  0.97 us (1%)
  between operations  0.94 us (1%)
    pallas_call x1, Pallas kernels, local_step(): pl.pallas_call(kernel, out_shape=(jax.ShapeDtypeStruct((3, 2, 8, SLOTS),...  31.5 us
    all_to_all x1, waiting for transfers between devices, gathered(): recv = lax.all_to_all(jnp.broadcast_to(own, (nz, 32, 256)), 'gz', 0, 0)  20.5 us
    all_to_all x1, starting transfers between devices, gathered(): recv = lax.all_to_all(jnp.broadcast_to(own, (nz, 32, 256)), 'gz', 0, 0)  14 us
    ppermute x1, starting transfers between devices, gathered(): after = lax.ppermute(down, 'gy', along('gy', -1))  3.64 us
    ppermute x1, starting transfers between devices, gathered(): before = lax.ppermute(own[..., 64:], 'gx', along('gx', 1))  3.39 us
    ppermute x1, waiting for transfers between devices, gathered(): after = lax.ppermute(own[..., :64], 'gx', along('gx', -1))  3.26 us
    ppermute x1, starting transfers between devices, gathered(): after = lax.ppermute(own[..., :64], 'gx', along('gx', -1))  2.44 us
    ppermute x1, starting transfers between devices, gathered(): before = lax.ppermute(up, 'gy', along('gy', 1))  2.04 us
  transfers between devices with their start and end apart: 5, of which 3 were waited for; matrix products, arithmetic and copies ran while one was open for 0% of the time, Pallas kernels for 0%

profile of v5, /device:TPU:18, one launch (start us, length us, event | category | flops | bytes accessed | tf_op | source)
XLA Modules:
  0.0 86.1 jit_solution(14782628130086388600)
XLA Ops:
  0.6 1.4 %shard_map.95 = (f32[3,8,128]{2,1,0:T(8,128)}, f32[3,1,128]{2,1,0:T(1,128)}, f32[3,1,128]{2,1,0:T(1,128)}) custom-call(s32[1,2,8]{2,1,0:T(2,128)} %counts.1, f32[3,1,2,8,64]{4,3,2,1,0:T(8,128)} %positions.1), custom_call_target="tpu_custom_call" | custom-call | tf_op jit(solution)/shard_map/pallas_call | solution.py:428
  2.1 0.0 copy-start.7
  2.1 2.0 %collective-permute-start = (f32[3,1,128]{2,1,0:T(1,128)}, f32[3,1,128]{2,1,0:T(1,128)S(1)}, u32[]{:S(2)}, u32[]{:S(2)}) collective-permute-start(f32[3,1,128]{2,1,0:T(1,128)} %get-tuple-element.7), channel_id=1, source_target_pairs={{0,16},{16,32},{32,48},{48,64},{64,80},{80,96},{96,112},{112,0},{1... | collective-permute-start | bytes 4616 | tf_op jit(solution)/shard_map/ppermute | solution.py:439
  4.1 0.0 copy-done.7
  4.1 3.6 %collective-permute-start.1 = (f32[3,1,128]{2,1,0:T(1,128)S(1)}, f32[3,1,128]{2,1,0:T(1,128)S(1)}, u32[]{:S(2)}, u32[]{:S(2)}) collective-permute-start(f32[3,1,128]{2,1,0:T(1,128)S(1)} %copy-done.7), channel_id=1, source_target_pairs={{0,112},{16,0},{32,16},{48,32},{64,48},{80,64},{96,80},{112,96},{1... | collective-permute-start | bytes 4616 | tf_op jit(solution)/shard_map/ppermute | solution.py:440
  7.8 0.0 collective-permute-done
  7.8 1.3 %collective-permute-done.1 = f32[3,1,128]{2,1,0:T(1,128)S(1)} collective-permute-done((f32[3,1,128]{2,1,0:T(1,128)S(1)}, f32[3,1,128]{2,1,0:T(1,128)S(1)}, u32[]{:S(2)}, u32[]{:S(2)}) %collective-permute-start.1) | collective-permute-done | bytes 1568 | tf_op jit(solution)/shard_map/ppermute | solution.py:440
  9.1 0.7 pad_maximum_fusion.1
  9.8 0.0 copy-start.6
  9.8 0.1 fusion
  9.9 3.4 %collective-permute-start.2 = (f32[3,10,64]{2,1,0:T(8,128)S(1)}, f32[3,10,64]{2,1,0:T(8,128)S(1)}, u32[]{:S(2)}, u32[]{:S(2)}) collective-permute-start(f32[3,10,64]{2,1,0:T(8,128)S(1)} %get-tuple-element.16), channel_id=1, source_target_pairs={{0,128},{128,256},{256,384},{384,0},{1,129},{129,257},{257,385},{3... | collective-permute-start | bytes 23048 | tf_op jit(solution)/shard_map/ppermute | solution.py:442
  13.3 2.4 %collective-permute-start.3 = (f32[3,10,64]{2,1,0:T(8,128)S(1)}, f32[3,10,64]{2,1,0:T(8,128)S(1)}, u32[]{:S(2)}, u32[]{:S(2)}) collective-permute-start(f32[3,10,64]{2,1,0:T(8,128)S(1)} %get-tuple-element.17), channel_id=1, source_target_pairs={{0,384},{128,0},{256,128},{384,256},{1,385},{129,1},{257,129},{385... | collective-permute-start | bytes 23048 | tf_op jit(solution)/shard_map/ppermute | solution.py:443
  15.7 0.0 collective-permute-done.2
  15.7 3.3 %collective-permute-done.3 = f32[3,10,64]{2,1,0:T(8,128)S(1)} collective-permute-done((f32[3,10,64]{2,1,0:T(8,128)S(1)}, f32[3,10,64]{2,1,0:T(8,128)S(1)}, u32[]{:S(2)}, u32[]{:S(2)}) %collective-permute-start.3) | collective-permute-done | bytes 7712 | tf_op jit(solution)/shard_map/ppermute | solution.py:443
  19.0 0.0 copy-done.6
  19.0 0.1 pad_maximum_fusion
  19.1 0.0 copy-start.3
  19.1 0.0 copy-start.4
  19.1 0.0 copy-start.5
  19.1 0.8 broadcast_in_dim.9
  20.0 0.0 copy-start
  20.0 0.0 copy-start.1
  20.0 0.0 copy-start.2
  20.0 14.0 %all-to-all-start = ((f32[16,32,256]{2,1,0:T(8,128)}), f32[16,32,256]{2,1,0:T(8,128)S(1)}, u32[]{:S(2)}, u32[]{:S(2)}) async-start(f32[16,32,256]{2,1,0:T(8,128)} %broadcast_in_dim.9), calls=%async_computation | async-start | bytes 1048576 | tf_op jit(solution)/shard_map/all_to_all | solution.py:446
  34.0 20.5 %all-to-all-done.recv = f32[16,32,256]{2,1,0:T(8,128)S(1)} async-done(((f32[16,32,256]{2,1,0:T(8,128)}), f32[16,32,256]{2,1,0:T(8,128)S(1)}, u32[]{:S(2)}, u32[]{:S(2)}) %all-to-all-start) | async-done | bytes 524320 | tf_op jit(solution)/shard_map/all_to_all | solution.py:446
  54.5 0.0 copy-done.3
  54.5 0.0 copy-done.4
  54.5 0.0 copy-done.5
  54.5 0.0 copy-done
  54.5 0.0 copy-done.1
  54.5 0.0 copy-done.2
  54.5 31.5 %shard_map.96 = (f32[3,2,8,64]{3,2,1,0:T(8,128)}, f32[2,8,64]{2,1,0:T(8,128)}) custom-call(s32[1]{0:T(128)} %bitcast.at_z, f32[16,32,256]{2,1,0:T(8,128)S(1)} %all-to-all-done.recv, bf16[208,1280]{1,0:T(8,128)(2,1)S(1)} %copy-done, bf16[320,208]{1,0:T(8,128)(2,1)S(1)} %copy-done.2, bf16[256,256]{1,0:T(8,128)(2,1)S(1)} %copy-done.3, ...), custom_call_target="tpu_custom_call" | custom-call | tf_op jit(solution)/shard_map/pallas_call | solution.py:374
  (2 shorter events, 0.0 us)
Async XLA Ops:
  2.1 2.1 %copy-start.7 = (f32[3,1,128]{2,1,0:T(1,128)S(1)}, f32[3,1,128]{2,1,0:T(1,128)}, u32[]{:S(2)}) copy-start(f32[3,1,128]{2,1,0:T(1,128)} %get-tuple-element.9) | copy-start | bytes 4612
  2.1 5.7 %collective-permute-start = (f32[3,1,128]{2,1,0:T(1,128)}, f32[3,1,128]{2,1,0:T(1,128)S(1)}, u32[]{:S(2)}, u32[]{:S(2)}) collective-permute-start(f32[3,1,128]{2,1,0:T(1,128)} %get-tuple-element.7), channel_id=1, source_target_pairs={{0,16},{16,32},{32,48},{48,64},{64,80},{80,96},{96,112},{112,0},{1... | collective-permute-start | bytes 4616 | tf_op jit(solution)/shard_map/ppermute | solution.py:439
  4.1 4.9 %collective-permute-start.1 = (f32[3,1,128]{2,1,0:T(1,128)S(1)}, f32[3,1,128]{2,1,0:T(1,128)S(1)}, u32[]{:S(2)}, u32[]{:S(2)}) collective-permute-start(f32[3,1,128]{2,1,0:T(1,128)S(1)} %copy-done.7), channel_id=1, source_target_pairs={{0,112},{16,0},{32,16},{48,32},{64,48},{80,64},{96,80},{112,96},{1... | collective-permute-start | bytes 4616 | tf_op jit(solution)/shard_map/ppermute | solution.py:440
  9.8 9.2 %copy-start.6 = (f32[3,8,128]{2,1,0:T(8,128)S(1)}, f32[3,8,128]{2,1,0:T(8,128)}, u32[]{:S(2)}) copy-start(f32[3,8,128]{2,1,0:T(8,128)} %get-tuple-element.8) | copy-start | bytes 36868
  9.9 5.9 %collective-permute-start.2 = (f32[3,10,64]{2,1,0:T(8,128)S(1)}, f32[3,10,64]{2,1,0:T(8,128)S(1)}, u32[]{:S(2)}, u32[]{:S(2)}) collective-permute-start(f32[3,10,64]{2,1,0:T(8,128)S(1)} %get-tuple-element.16), channel_id=1, source_target_pairs={{0,128},{128,256},{256,384},{384,0},{1,129},{129,257},{257,385},{3... | collective-permute-start | bytes 23048 | tf_op jit(solution)/shard_map/ppermute | solution.py:442
  13.3 5.7 %collective-permute-start.3 = (f32[3,10,64]{2,1,0:T(8,128)S(1)}, f32[3,10,64]{2,1,0:T(8,128)S(1)}, u32[]{:S(2)}, u32[]{:S(2)}) collective-permute-start(f32[3,10,64]{2,1,0:T(8,128)S(1)} %get-tuple-element.17), channel_id=1, source_target_pairs={{0,384},{128,0},{256,128},{384,256},{1,385},{129,1},{257,129},{385... | collective-permute-start | bytes 23048 | tf_op jit(solution)/shard_map/ppermute | solution.py:443
  19.1 35.4 %copy-start.3 = (bf16[256,256]{1,0:T(8,128)(2,1)S(1)}, bf16[256,256]{1,0:T(8,128)(2,1)}, u32[]{:S(2)}) copy-start(bf16[256,256]{1,0:T(8,128)(2,1)} %constant.21.clone.eye) | copy-start | bytes 393220
  19.1 35.4 %copy-start.4 = (bf16[256,256]{1,0:T(8,128)(2,1)S(1)}, bf16[256,256]{1,0:T(8,128)(2,1)}, u32[]{:S(2)}) copy-start(bf16[256,256]{1,0:T(8,128)(2,1)} %constant.22.clone.upto) | copy-start | bytes 393220
  19.1 35.4 %copy-start.5 = (bf16[512,128]{1,0:T(8,128)(2,1)S(1)}, bf16[512,128]{1,0:T(8,128)(2,1)}, u32[]{:S(2)}) copy-start(bf16[512,128]{1,0:T(8,128)(2,1)} %constant.24.clone.add_up) | copy-start | bytes 393220
  20.0 34.5 %copy-start = (bf16[208,1280]{1,0:T(8,128)(2,1)S(1)}, bf16[208,1280]{1,0:T(8,128)(2,1)}, u32[]{:S(2)}) copy-start(bf16[208,1280]{1,0:T(8,128)(2,1)} %constant.19.clone.place_b) | copy-start | bytes 1597444
  20.0 34.5 %copy-start.1 = (bf16[896,32]{1,0:T(8,128)(2,1)S(1)}, bf16[896,32]{1,0:T(8,128)(2,1)}, u32[]{:S(2)}) copy-start(bf16[896,32]{1,0:T(8,128)(2,1)} %constant.23.clone.outside) | copy-start | bytes 172036
  20.0 34.5 %copy-start.2 = (bf16[320,208]{1,0:T(8,128)(2,1)S(1)}, bf16[320,208]{1,0:T(8,128)(2,1)}, u32[]{:S(2)}) copy-start(bf16[320,208]{1,0:T(8,128)(2,1)} %constant.20.clone.sel_a) | copy-start | bytes 399364
  20.0 34.5 %all-to-all-start = ((f32[16,32,256]{2,1,0:T(8,128)}), f32[16,32,256]{2,1,0:T(8,128)S(1)}, u32[]{:S(2)}, u32[]{:S(2)}) async-start(f32[16,32,256]{2,1,0:T(8,128)} %broadcast_in_dim.9), calls=%async_computation | async-start | bytes 1048576 | tf_op jit(solution)/shard_map/all_to_all | solution.py:446

commit v6 on v5

--- a/solution.py
+++ b/solution.py
@@ -433,6 +433,23 @@
     )(counts, positions)
 
 
+def spreading_kernel(before, own, after, out):
+    rows = [jnp.concatenate([before[c], own[c], after[c]], axis=1) for c in range(3)]
+    layer = jnp.concatenate(rows + [jnp.zeros((2, 256), f32)], axis=0)
+    for k in range(out.shape[0]):
+        out[k] = layer
+
+
+def spread(before, own, after, copies):
+    vmem = pl.BlockSpec(memory_space=pltpu.VMEM)
+    return pl.pallas_call(
+        spreading_kernel,
+        out_shape=jax.ShapeDtypeStruct((copies, 32, 256), f32),
+        in_specs=[vmem] * 3,
+        out_specs=vmem,
+    )(before, own, after)
+
+
 def gathered(positions, counts):
     nz = lax.axis_size("gz")
     own, up, down = marked(positions, counts)
@@ -441,9 +458,7 @@
     own = jnp.concatenate([before, own, after], axis=1)
     before = lax.ppermute(own[..., 64:], "gx", along("gx", 1))
     after = lax.ppermute(own[..., :64], "gx", along("gx", -1))
-    own = jnp.concatenate([before, own, after], axis=2).reshape(30, 256)
-    own = jnp.pad(own, ((0, 2), (0, 0)))
-    recv = lax.all_to_all(jnp.broadcast_to(own, (nz, 32, 256)), "gz", 0, 0)
+    recv = lax.all_to_all(spread(before, own, after, nz), "gz", 0, 0)
     return lax.axis_index("gz").astype(jnp.int32).reshape(1), recv
 
 

time: 86.6 us -> 88.6 us (1.023)
  the two profiles are of different devices: /device:TPU:18 before, /device:TPU:22 now
where the time goes in v6:
time: 88.6 us; the launch traced here: 88.2 us
  Pallas kernels  34.6 us (39%)
  starting transfers between devices  25.5 us (29%)
  waiting for transfers between devices  25.2 us (28%)
  local copies, waits for them, and re-layouts  1.25 us (1%)
  between operations  0.91 us (1%)
    pallas_call x1, Pallas kernels, local_step(): pl.pallas_call(kernel, out_shape=(jax.ShapeDtypeStruct((3, 2, 8, SLOTS),...  31.4 us
    all_to_all x1, waiting for transfers between devices, gathered(): recv = lax.all_to_all(spread(before, own, after, nz), 'gz', 0, 0)  20.5 us
    all_to_all x1, starting transfers between devices, gathered(): recv = lax.all_to_all(spread(before, own, after, nz), 'gz', 0, 0)  14 us
    ppermute x1, starting transfers between devices, gathered(): after = lax.ppermute(down, 'gy', along('gy', -1))  3.64 us
    ppermute x1, starting transfers between devices, gathered(): after = lax.ppermute(own[..., :64], 'gx', along('gx', -1))  3.46 us
    ppermute x1, waiting for transfers between devices, gathered(): after = lax.ppermute(own[..., :64], 'gx', along('gx', -1))  3.44 us
    ppermute x1, starting transfers between devices, gathered(): before = lax.ppermute(own[..., 64:], 'gx', along('gx', 1))  2.37 us
    ppermute x1, starting transfers between devices, gathered(): before = lax.ppermute(up, 'gy', along('gy', 1))  2.04 us
  transfers between devices with their start and end apart: 5, of which 3 were waited for; matrix products, arithmetic and copies ran while one was open for 0% of the time, Pallas kernels for 0%

profile of v6, /device:TPU:22, one launch (start us, length us, event | category | flops | bytes accessed | tf_op | source)
XLA Modules:
  0.0 88.2 jit_solution(924197423954257543)
XLA Ops:
  0.6 1.4 %shard_map.95 = (f32[3,8,128]{2,1,0:T(8,128)}, f32[3,1,128]{2,1,0:T(1,128)}, f32[3,1,128]{2,1,0:T(1,128)}) custom-call(s32[1,2,8]{2,1,0:T(2,128)} %counts.1, f32[3,1,2,8,64]{4,3,2,1,0:T(8,128)} %positions.1), custom_call_target="tpu_custom_call" | custom-call | tf_op jit(solution)/shard_map/pallas_call | solution.py:428
  2.1 0.0 copy-start.9
  2.1 2.0 %collective-permute-start = (f32[3,1,128]{2,1,0:T(1,128)}, f32[3,1,128]{2,1,0:T(1,128)S(1)}, u32[]{:S(2)}, u32[]{:S(2)}) collective-permute-start(f32[3,1,128]{2,1,0:T(1,128)} %get-tuple-element.7), channel_id=1, source_target_pairs={{0,16},{16,32},{32,48},{48,64},{64,80},{80,96},{96,112},{112,0},{1... | collective-permute-start | bytes 4616 | tf_op jit(solution)/shard_map/ppermute | solution.py:456
  4.1 0.0 copy-done.9
  4.1 3.6 %collective-permute-start.1 = (f32[3,1,128]{2,1,0:T(1,128)S(1)}, f32[3,1,128]{2,1,0:T(1,128)S(1)}, u32[]{:S(2)}, u32[]{:S(2)}) collective-permute-start(f32[3,1,128]{2,1,0:T(1,128)S(1)} %copy-done.9), channel_id=1, source_target_pairs={{0,112},{16,0},{32,16},{48,32},{64,48},{80,64},{96,80},{112,96},{1... | collective-permute-start | bytes 4616 | tf_op jit(solution)/shard_map/ppermute | solution.py:457
  7.8 0.0 collective-permute-done
  7.8 1.3 %collective-permute-done.1 = f32[3,1,128]{2,1,0:T(1,128)S(1)} collective-permute-done((f32[3,1,128]{2,1,0:T(1,128)S(1)}, f32[3,1,128]{2,1,0:T(1,128)S(1)}, u32[]{:S(2)}, u32[]{:S(2)}) %collective-permute-start.1) | collective-permute-done | bytes 1568 | tf_op jit(solution)/shard_map/ppermute | solution.py:457
  9.1 0.7 pad_maximum_fusion.own
  9.8 0.0 copy-start.6
  9.8 0.1 fusion
  9.9 0.5 copy-done.6
  10.4 2.4 %collective-permute-start.2 = (f32[3,10,64]{2,1,0:T(8,128)S(1)}, f32[3,10,64]{2,1,0:T(8,128)S(1)}, u32[]{:S(2)}, u32[]{:S(2)}) collective-permute-start(f32[3,10,64]{2,1,0:T(8,128)S(1)} %get-tuple-element.15), channel_id=1, source_target_pairs={{0,128},{128,256},{256,384},{384,0},{1,129},{129,257},{257,385},{3... | collective-permute-start | bytes 23048 | tf_op jit(solution)/shard_map/ppermute | solution.py:459
  12.8 3.5 %collective-permute-start.3 = (f32[3,10,64]{2,1,0:T(8,128)S(1)}, f32[3,10,64]{2,1,0:T(8,128)S(1)}, u32[]{:S(2)}, u32[]{:S(2)}) collective-permute-start(f32[3,10,64]{2,1,0:T(8,128)S(1)} %get-tuple-element.14), channel_id=1, source_target_pairs={{0,384},{128,0},{256,128},{384,256},{1,385},{129,1},{257,129},{385... | collective-permute-start | bytes 23048 | tf_op jit(solution)/shard_map/ppermute | solution.py:460
  16.2 0.0 collective-permute-done.2.before
  16.2 0.0 copy-start.7
  16.3 3.4 %collective-permute-done.3.after = f32[3,10,64]{2,1,0:T(8,128)S(1)} collective-permute-done((f32[3,10,64]{2,1,0:T(8,128)S(1)}, f32[3,10,64]{2,1,0:T(8,128)S(1)}, u32[]{:S(2)}, u32[]{:S(2)}) %collective-permute-start.3) | collective-permute-done | bytes 7712 | tf_op jit(solution)/shard_map/ppermute | solution.py:460
  19.7 0.0 copy-done.7
  19.7 0.0 copy-start.8
  19.7 0.6 copy-done.8
  20.3 0.0 copy-start.3
  20.3 0.0 copy-start.4
  20.3 0.0 copy-start.5
  20.3 1.7 %shard_map.96 = f32[16,32,256]{2,1,0:T(8,128)} custom-call(f32[3,10,64]{2,1,0:T(8,128)} %copy-done.7, f32[3,10,128]{2,1,0:T(8,128)} %copy-done.6, f32[3,10,64]{2,1,0:T(8,128)} %copy-done.8), custom_call_target="tpu_custom_call" | custom-call | tf_op jit(solution)/shard_map/pallas_call | solution.py:445
  22.1 0.0 copy-start
  22.1 0.0 copy-start.1
  22.1 0.0 copy-start.2
  22.1 14.0 %all-to-all-start = ((f32[16,32,256]{2,1,0:T(8,128)}), f32[16,32,256]{2,1,0:T(8,128)S(1)}, u32[]{:S(2)}, u32[]{:S(2)}) async-start(f32[16,32,256]{2,1,0:T(8,128)} %shard_map.96), calls=%async_computation | async-start | bytes 1048576 | tf_op jit(solution)/shard_map/all_to_all | solution.py:461
  36.1 20.5 %all-to-all-done.recv = f32[16,32,256]{2,1,0:T(8,128)S(1)} async-done(((f32[16,32,256]{2,1,0:T(8,128)}), f32[16,32,256]{2,1,0:T(8,128)S(1)}, u32[]{:S(2)}, u32[]{:S(2)}) %all-to-all-start) | async-done | bytes 524320 | tf_op jit(solution)/shard_map/all_to_all | solution.py:461
  56.6 0.0 copy-done.3
  56.6 0.0 copy-done.4
  56.6 0.0 copy-done.5
  56.6 0.0 copy-done
  56.6 0.0 copy-done.1
  56.6 0.0 copy-done.2
  56.6 31.4 %shard_map.97 = (f32[3,2,8,64]{3,2,1,0:T(8,128)}, f32[2,8,64]{2,1,0:T(8,128)}) custom-call(s32[1]{0:T(128)} %bitcast.at_z, f32[16,32,256]{2,1,0:T(8,128)S(1)} %all-to-all-done.recv, bf16[208,1280]{1,0:T(8,128)(2,1)S(1)} %copy-done, bf16[320,208]{1,0:T(8,128)(2,1)S(1)} %copy-done.2, bf16[256,256]{1,0:T(8,128)(2,1)S(1)} %copy-done.3, ...), custom_call_target="tpu_custom_call" | custom-call | tf_op jit(solution)/shard_map/pallas_call | solution.py:374
Async XLA Ops:
  2.1 2.1 %copy-start.9 = (f32[3,1,128]{2,1,0:T(1,128)S(1)}, f32[3,1,128]{2,1,0:T(1,128)}, u32[]{:S(2)}) copy-start(f32[3,1,128]{2,1,0:T(1,128)} %get-tuple-element.9) | copy-start | bytes 4612
  2.1 5.7 %collective-permute-start = (f32[3,1,128]{2,1,0:T(1,128)}, f32[3,1,128]{2,1,0:T(1,128)S(1)}, u32[]{:S(2)}, u32[]{:S(2)}) collective-permute-start(f32[3,1,128]{2,1,0:T(1,128)} %get-tuple-element.7), channel_id=1, source_target_pairs={{0,16},{16,32},{32,48},{48,64},{64,80},{80,96},{96,112},{112,0},{1... | collective-permute-start | bytes 4616 | tf_op jit(solution)/shard_map/ppermute | solution.py:456
  4.1 4.9 %collective-permute-start.1 = (f32[3,1,128]{2,1,0:T(1,128)S(1)}, f32[3,1,128]{2,1,0:T(1,128)S(1)}, u32[]{:S(2)}, u32[]{:S(2)}) collective-permute-start(f32[3,1,128]{2,1,0:T(1,128)S(1)} %copy-done.9), channel_id=1, source_target_pairs={{0,112},{16,0},{32,16},{48,32},{64,48},{80,64},{96,80},{112,96},{1... | collective-permute-start | bytes 4616 | tf_op jit(solution)/shard_map/ppermute | solution.py:457
  9.8 0.6 copy-start.6
  10.4 5.8 %collective-permute-start.2 = (f32[3,10,64]{2,1,0:T(8,128)S(1)}, f32[3,10,64]{2,1,0:T(8,128)S(1)}, u32[]{:S(2)}, u32[]{:S(2)}) collective-permute-start(f32[3,10,64]{2,1,0:T(8,128)S(1)} %get-tuple-element.15), channel_id=1, source_target_pairs={{0,128},{128,256},{256,384},{384,0},{1,129},{129,257},{257,385},{3... | collective-permute-start | bytes 23048 | tf_op jit(solution)/shard_map/ppermute | solution.py:459
  12.8 6.9 %collective-permute-start.3 = (f32[3,10,64]{2,1,0:T(8,128)S(1)}, f32[3,10,64]{2,1,0:T(8,128)S(1)}, u32[]{:S(2)}, u32[]{:S(2)}) collective-permute-start(f32[3,10,64]{2,1,0:T(8,128)S(1)} %get-tuple-element.14), channel_id=1, source_target_pairs={{0,384},{128,0},{256,128},{384,256},{1,385},{129,1},{257,129},{385... | collective-permute-start | bytes 23048 | tf_op jit(solution)/shard_map/ppermute | solution.py:460
  16.2 3.5 %copy-start.7 = (f32[3,10,64]{2,1,0:T(8,128)}, f32[3,10,64]{2,1,0:T(8,128)S(1)}, u32[]{:S(2)}) copy-start(f32[3,10,64]{2,1,0:T(8,128)S(1)} %collective-permute-done.2.before) | copy-start | bytes 23044
  19.7 0.6 copy-start.8
  20.3 36.2 %copy-start.3 = (bf16[256,256]{1,0:T(8,128)(2,1)S(1)}, bf16[256,256]{1,0:T(8,128)(2,1)}, u32[]{:S(2)}) copy-start(bf16[256,256]{1,0:T(8,128)(2,1)} %constant.18.clone.eye) | copy-start | bytes 393220
  20.3 36.2 %copy-start.4 = (bf16[256,256]{1,0:T(8,128)(2,1)S(1)}, bf16[256,256]{1,0:T(8,128)(2,1)}, u32[]{:S(2)}) copy-start(bf16[256,256]{1,0:T(8,128)(2,1)} %constant.19.clone.upto) | copy-start | bytes 393220
  20.3 36.2 %copy-start.5 = (bf16[512,128]{1,0:T(8,128)(2,1)S(1)}, bf16[512,128]{1,0:T(8,128)(2,1)}, u32[]{:S(2)}) copy-start(bf16[512,128]{1,0:T(8,128)(2,1)} %constant.21.clone.add_up) | copy-start | bytes 393220
  22.1 34.5 %copy-start = (bf16[208,1280]{1,0:T(8,128)(2,1)S(1)}, bf16[208,1280]{1,0:T(8,128)(2,1)}, u32[]{:S(2)}) copy-start(bf16[208,1280]{1,0:T(8,128)(2,1)} %constant.16.clone.place_b) | copy-start | bytes 1597444
  22.1 34.5 %copy-start.1 = (bf16[896,32]{1,0:T(8,128)(2,1)S(1)}, bf16[896,32]{1,0:T(8,128)(2,1)}, u32[]{:S(2)}) copy-start(bf16[896,32]{1,0:T(8,128)(2,1)} %constant.20.clone.outside) | copy-start | bytes 172036
  22.1 34.5 %copy-start.2 = (bf16[320,208]{1,0:T(8,128)(2,1)S(1)}, bf16[320,208]{1,0:T(8,128)(2,1)}, u32[]{:S(2)}) copy-start(bf16[320,208]{1,0:T(8,128)(2,1)} %constant.17.clone.sel_a) | copy-start | bytes 399364
  22.1 34.5 %all-to-all-start = ((f32[16,32,256]{2,1,0:T(8,128)}), f32[16,32,256]{2,1,0:T(8,128)S(1)}, u32[]{:S(2)}, u32[]{:S(2)}) async-start(f32[16,32,256]{2,1,0:T(8,128)} %shard_map.96), calls=%async_computation | async-start | bytes 1048576 | tf_op jit(solution)/shard_map/all_to_all | solution.py:461

commit v7 on v5

--- a/solution.py
+++ b/solution.py
@@ -32,7 +32,7 @@
 TERMS = 32
 DEPTH = 13 * TILE
 WINDOW, EDGE, EXTRA = 768, 576, 128
-STEP = 16
+STEP = 32
 CAPACITY = LAYERS * 256 + WINDOW + EXTRA
 EMPTY = FAR * side_xy * UNIT
 BOX = (side_xy * UNIT, 4 * side_xy * UNIT, 0.5 * side_z * UNIT)

time: 86.6 us -> 85.9 us (level)
  the two profiles are of different devices: /device:TPU:18 before, /device:TPU:16 now
where the time goes in v7:
time: 85.9 us; the launch traced here: 84.5 us
  Pallas kernels  31.4 us (37%)
  starting transfers between devices  26.7 us (31%)
  waiting for transfers between devices  23.7 us (28%)
  local copies, waits for them, and re-layouts  0.97 us (1%)
  between operations  0.94 us (1%)
    pallas_call x1, Pallas kernels, local_step(): pl.pallas_call(kernel, out_shape=(jax.ShapeDtypeStruct((3, 2, 8, SLOTS),...  29.9 us
    all_to_all x1, waiting for transfers between devices, gathered(): recv = lax.all_to_all(jnp.broadcast_to(own, (nz, 32, 256)), 'gz', 0, 0)  20.4 us
    all_to_all x1, starting transfers between devices, gathered(): recv = lax.all_to_all(jnp.broadcast_to(own, (nz, 32, 256)), 'gz', 0, 0)  14 us
    ppermute x1, starting transfers between devices, gathered(): after = lax.ppermute(own[..., :64], 'gx', along('gx', -1))  3.65 us
    ppermute x1, starting transfers between devices, gathered(): after = lax.ppermute(down, 'gy', along('gy', -1))  3.64 us
    ppermute x1, starting transfers between devices, gathered(): before = lax.ppermute(own[..., 64:], 'gx', along('gx', 1))  3.39 us
    ppermute x1, waiting for transfers between devices, gathered(): after = lax.ppermute(own[..., :64], 'gx', along('gx', -1))  2.05 us
    ppermute x1, starting transfers between devices, gathered(): before = lax.ppermute(up, 'gy', along('gy', 1))  2.04 us
  transfers between devices with their start and end apart: 5, of which 3 were waited for; matrix products, arithmetic and copies ran while one was open for 0% of the time, Pallas kernels for 0%

profile of v7, /device:TPU:16, one launch (start us, length us, event | category | flops | bytes accessed | tf_op | source)
XLA Modules:
  0.0 84.5 jit_solution(16307620069432360430)
XLA Ops:
  0.6 1.4 %shard_map.95 = (f32[3,8,128]{2,1,0:T(8,128)}, f32[3,1,128]{2,1,0:T(1,128)}, f32[3,1,128]{2,1,0:T(1,128)}) custom-call(s32[1,2,8]{2,1,0:T(2,128)} %counts.1, f32[3,1,2,8,64]{4,3,2,1,0:T(8,128)} %positions.1), custom_call_target="tpu_custom_call" | custom-call | tf_op jit(solution)/shard_map/pallas_call | solution.py:428
  2.1 0.0 copy-start.7
  2.1 2.0 %collective-permute-start = (f32[3,1,128]{2,1,0:T(1,128)}, f32[3,1,128]{2,1,0:T(1,128)S(1)}, u32[]{:S(2)}, u32[]{:S(2)}) collective-permute-start(f32[3,1,128]{2,1,0:T(1,128)} %get-tuple-element.7), channel_id=1, source_target_pairs={{0,16},{16,32},{32,48},{48,64},{64,80},{80,96},{96,112},{112,0},{1... | collective-permute-start | bytes 4616 | tf_op jit(solution)/shard_map/ppermute | solution.py:439
  4.1 0.0 copy-done.7
  4.1 3.6 %collective-permute-start.1 = (f32[3,1,128]{2,1,0:T(1,128)S(1)}, f32[3,1,128]{2,1,0:T(1,128)S(1)}, u32[]{:S(2)}, u32[]{:S(2)}) collective-permute-start(f32[3,1,128]{2,1,0:T(1,128)S(1)} %copy-done.7), channel_id=1, source_target_pairs={{0,112},{16,0},{32,16},{48,32},{64,48},{80,64},{96,80},{112,96},{1... | collective-permute-start | bytes 4616 | tf_op jit(solution)/shard_map/ppermute | solution.py:440
  7.8 0.0 collective-permute-done
  7.8 1.3 %collective-permute-done.1 = f32[3,1,128]{2,1,0:T(1,128)S(1)} collective-permute-done((f32[3,1,128]{2,1,0:T(1,128)S(1)}, f32[3,1,128]{2,1,0:T(1,128)S(1)}, u32[]{:S(2)}, u32[]{:S(2)}) %collective-permute-start.1) | collective-permute-done | bytes 1568 | tf_op jit(solution)/shard_map/ppermute | solution.py:440
  9.1 0.7 pad_maximum_fusion.1
  9.8 0.0 copy-start.6
  9.8 0.1 fusion
  9.9 3.4 %collective-permute-start.2 = (f32[3,10,64]{2,1,0:T(8,128)S(1)}, f32[3,10,64]{2,1,0:T(8,128)S(1)}, u32[]{:S(2)}, u32[]{:S(2)}) collective-permute-start(f32[3,10,64]{2,1,0:T(8,128)S(1)} %get-tuple-element.16), channel_id=1, source_target_pairs={{0,128},{128,256},{256,384},{384,0},{1,129},{129,257},{257,385},{3... | collective-permute-start | bytes 23048 | tf_op jit(solution)/shard_map/ppermute | solution.py:442
  13.3 3.7 %collective-permute-start.3 = (f32[3,10,64]{2,1,0:T(8,128)S(1)}, f32[3,10,64]{2,1,0:T(8,128)S(1)}, u32[]{:S(2)}, u32[]{:S(2)}) collective-permute-start(f32[3,10,64]{2,1,0:T(8,128)S(1)} %get-tuple-element.17), channel_id=1, source_target_pairs={{0,384},{128,0},{256,128},{384,256},{1,385},{129,1},{257,129},{385... | collective-permute-start | bytes 23048 | tf_op jit(solution)/shard_map/ppermute | solution.py:443
  16.9 0.0 collective-permute-done.2
  16.9 2.0 %collective-permute-done.3 = f32[3,10,64]{2,1,0:T(8,128)S(1)} collective-permute-done((f32[3,10,64]{2,1,0:T(8,128)S(1)}, f32[3,10,64]{2,1,0:T(8,128)S(1)}, u32[]{:S(2)}, u32[]{:S(2)}) %collective-permute-start.3) | collective-permute-done | bytes 7712 | tf_op jit(solution)/shard_map/ppermute | solution.py:443
  19.0 0.0 copy-done.6
  19.0 0.1 pad_maximum_fusion
  19.1 0.0 copy-start.3
  19.1 0.0 copy-start.4
  19.1 0.0 copy-start.5
  19.1 0.8 %broadcast_in_dim.9 = f32[16,32,256]{2,1,0:T(8,128)} broadcast(f32[32,256]{1,0:T(8,128)S(1)} %pad.4), dimensions={1,2} | broadcast | bytes 557056 | tf_op jit(solution)/shard_map/broadcast_in_dim | solution.py:446
  20.0 0.0 copy-start
  20.0 0.0 copy-start.1
  20.0 0.0 copy-start.2
  20.0 14.0 %all-to-all-start = ((f32[16,32,256]{2,1,0:T(8,128)}), f32[16,32,256]{2,1,0:T(8,128)S(1)}, u32[]{:S(2)}, u32[]{:S(2)}) async-start(f32[16,32,256]{2,1,0:T(8,128)} %broadcast_in_dim.9), calls=%async_computation | async-start | bytes 1048576 | tf_op jit(solution)/shard_map/all_to_all | solution.py:446
  34.0 20.4 %all-to-all-done.recv = f32[16,32,256]{2,1,0:T(8,128)S(1)} async-done(((f32[16,32,256]{2,1,0:T(8,128)}), f32[16,32,256]{2,1,0:T(8,128)S(1)}, u32[]{:S(2)}, u32[]{:S(2)}) %all-to-all-start) | async-done | bytes 524320 | tf_op jit(solution)/shard_map/all_to_all | solution.py:446
  54.4 0.0 copy-done.3
  54.4 0.0 copy-done.4
  54.4 0.0 copy-done.5
  54.4 0.0 copy-done
  54.4 0.0 copy-done.1
  54.4 0.0 copy-done.2
  54.4 29.9 %shard_map.96 = (f32[3,2,8,64]{3,2,1,0:T(8,128)}, f32[2,8,64]{2,1,0:T(8,128)}) custom-call(s32[1]{0:T(128)} %bitcast.at_z, f32[16,32,256]{2,1,0:T(8,128)S(1)} %all-to-all-done.recv, bf16[208,1280]{1,0:T(8,128)(2,1)S(1)} %copy-done, bf16[320,208]{1,0:T(8,128)(2,1)S(1)} %copy-done.2, bf16[256,256]{1,0:T(8,128)(2,1)S(1)} %copy-done.3, ...), custom_call_target="tpu_custom_call" | custom-call | tf_op jit(solution)/shard_map/pallas_call | solution.py:374
  (2 shorter events, 0.0 us)
Async XLA Ops:
  2.1 2.1 %copy-start.7 = (f32[3,1,128]{2,1,0:T(1,128)S(1)}, f32[3,1,128]{2,1,0:T(1,128)}, u32[]{:S(2)}) copy-start(f32[3,1,128]{2,1,0:T(1,128)} %get-tuple-element.9) | copy-start | bytes 4612
  2.1 5.7 %collective-permute-start = (f32[3,1,128]{2,1,0:T(1,128)}, f32[3,1,128]{2,1,0:T(1,128)S(1)}, u32[]{:S(2)}, u32[]{:S(2)}) collective-permute-start(f32[3,1,128]{2,1,0:T(1,128)} %get-tuple-element.7), channel_id=1, source_target_pairs={{0,16},{16,32},{32,48},{48,64},{64,80},{80,96},{96,112},{112,0},{1... | collective-permute-start | bytes 4616 | tf_op jit(solution)/shard_map/ppermute | solution.py:439
  4.1 4.9 %collective-permute-start.1 = (f32[3,1,128]{2,1,0:T(1,128)S(1)}, f32[3,1,128]{2,1,0:T(1,128)S(1)}, u32[]{:S(2)}, u32[]{:S(2)}) collective-permute-start(f32[3,1,128]{2,1,0:T(1,128)S(1)} %copy-done.7), channel_id=1, source_target_pairs={{0,112},{16,0},{32,16},{48,32},{64,48},{80,64},{96,80},{112,96},{1... | collective-permute-start | bytes 4616 | tf_op jit(solution)/shard_map/ppermute | solution.py:440
  9.8 9.2 %copy-start.6 = (f32[3,8,128]{2,1,0:T(8,128)S(1)}, f32[3,8,128]{2,1,0:T(8,128)}, u32[]{:S(2)}) copy-start(f32[3,8,128]{2,1,0:T(8,128)} %get-tuple-element.8) | copy-start | bytes 36868
  9.9 7.1 %collective-permute-start.2 = (f32[3,10,64]{2,1,0:T(8,128)S(1)}, f32[3,10,64]{2,1,0:T(8,128)S(1)}, u32[]{:S(2)}, u32[]{:S(2)}) collective-permute-start(f32[3,10,64]{2,1,0:T(8,128)S(1)} %get-tuple-element.16), channel_id=1, source_target_pairs={{0,128},{128,256},{256,384},{384,0},{1,129},{129,257},{257,385},{3... | collective-permute-start | bytes 23048 | tf_op jit(solution)/shard_map/ppermute | solution.py:442
  13.3 5.7 %collective-permute-start.3 = (f32[3,10,64]{2,1,0:T(8,128)S(1)}, f32[3,10,64]{2,1,0:T(8,128)S(1)}, u32[]{:S(2)}, u32[]{:S(2)}) collective-permute-start(f32[3,10,64]{2,1,0:T(8,128)S(1)} %get-tuple-element.17), channel_id=1, source_target_pairs={{0,384},{128,0},{256,128},{384,256},{1,385},{129,1},{257,129},{385... | collective-permute-start | bytes 23048 | tf_op jit(solution)/shard_map/ppermute | solution.py:443
  19.1 35.3 %copy-start.3 = (bf16[256,256]{1,0:T(8,128)(2,1)S(1)}, bf16[256,256]{1,0:T(8,128)(2,1)}, u32[]{:S(2)}) copy-start(bf16[256,256]{1,0:T(8,128)(2,1)} %constant.21.clone.eye) | copy-start | bytes 393220
  19.1 35.3 %copy-start.4 = (bf16[256,256]{1,0:T(8,128)(2,1)S(1)}, bf16[256,256]{1,0:T(8,128)(2,1)}, u32[]{:S(2)}) copy-start(bf16[256,256]{1,0:T(8,128)(2,1)} %constant.22.clone.upto) | copy-start | bytes 393220
  19.1 35.3 %copy-start.5 = (bf16[512,128]{1,0:T(8,128)(2,1)S(1)}, bf16[512,128]{1,0:T(8,128)(2,1)}, u32[]{:S(2)}) copy-start(bf16[512,128]{1,0:T(8,128)(2,1)} %constant.24.clone.add_up) | copy-start | bytes 393220
  20.0 34.4 %copy-start = (bf16[208,1280]{1,0:T(8,128)(2,1)S(1)}, bf16[208,1280]{1,0:T(8,128)(2,1)}, u32[]{:S(2)}) copy-start(bf16[208,1280]{1,0:T(8,128)(2,1)} %constant.19.clone.place_b) | copy-start | bytes 1597444
  20.0 34.4 %copy-start.1 = (bf16[896,32]{1,0:T(8,128)(2,1)S(1)}, bf16[896,32]{1,0:T(8,128)(2,1)}, u32[]{:S(2)}) copy-start(bf16[896,32]{1,0:T(8,128)(2,1)} %constant.23.clone.outside) | copy-start | bytes 172036
  20.0 34.4 %copy-start.2 = (bf16[320,208]{1,0:T(8,128)(2,1)S(1)}, bf16[320,208]{1,0:T(8,128)(2,1)}, u32[]{:S(2)}) copy-start(bf16[320,208]{1,0:T(8,128)(2,1)} %constant.20.clone.sel_a) | copy-start | bytes 399364
  20.0 34.4 %all-to-all-start = ((f32[16,32,256]{2,1,0:T(8,128)}), f32[16,32,256]{2,1,0:T(8,128)S(1)}, u32[]{:S(2)}, u32[]{:S(2)}) async-start(f32[16,32,256]{2,1,0:T(8,128)} %broadcast_in_dim.9), calls=%async_computation | async-start | bytes 1048576 | tf_op jit(solution)/shard_map/all_to_all | solution.py:446
